TPU v7x, 32 devices: a whole 2x2x4 slice. The times are simulated.
32 devices in a mesh: ctx: 8 (over z, x), tp: 4 (over y, core).
Axes of the slice: x: 2, y: 2, z: 4, core: 2. Of those that a mesh axis runs over, the one named last changes fastest.
Arguments:
- streams: bfloat16 [3, 1024, 8192], P(None, 'ctx', 'tp'), may hold values from -6 to 6
- short_filter: bfloat16 [3, 512, 7], P(None, 'tp'), may hold values from -3 to 3
- decay_rate: float32 [16, 8192], P(None, 'tp'), may hold values from 0.00029296876 to 0.05
- residue: float32 [16, 8192], P(None, 'tp'), may hold values from -5 to 5
- norm_gain: float32 [8192], P('tp'), may hold values from 0.5 to 1.5
- out_grad: bfloat16 [1024, 8192], P('ctx', 'tp'), may hold values from -6 to 6
Outputs:
- output: bfloat16 [1024, 8192], P('ctx', 'tp')
- stream_grads: bfloat16 [3, 1024, 8192], P(None, 'ctx', 'tp')
All inputs are finite; a program needn't handle non-finite values.
Results may differ from a plain program's by a relative error of at most 0.002.
Values may be sent and summed in bfloat16 or wider, within the bound.
No kernel may reach another device: no remote copies, remote signals or barrier semaphores. Data moves between devices by JAX's collectives and lax.ppermute only.
A program may use at most 64 MiB of HBM per device.

v0:
```python
import jax
import jax.numpy as jnp
from jax import lax
from jax.sharding import PartitionSpec as P

GROUP = 16
BLOCK = 16


EPSILON = 1e-05


def shifted(block, axis, distance):
    devices = range(lax.axis_size(axis))
    route = [(i - distance, i) for i in devices if i - distance in devices]
    return lax.ppermute(block, axis, route)


def carried_in(part, axis, combine, identity, reverse):
    count = lax.axis_size(axis)
    place = lax.axis_index(axis)
    ahead = count - 1 - place if reverse else place
    gathered = jax.tree.map(lambda a: lax.all_gather(a, axis), part)
    state = jax.tree.map(lambda a, e: jnp.zeros_like(a) + jnp.asarray(e, a.dtype), part, identity)

    def one(turn, state):
        source = count - 1 - turn if reverse else turn
        return combine(
            state, jax.tree.map(lambda a: lax.dynamic_index_in_dim(a, source, 0, False), gathered)
        )

    return lax.fori_loop(0, ahead, one, state)


def for_sending(value):
    return jax.tree.map(lambda a: a.astype(jnp.bfloat16) if a.dtype == jnp.float32 else a, value)


def channel_weights(short_filter):
    stream_count, group_count, tap_count = short_filter.shape
    spread = jnp.broadcast_to(
        short_filter.astype(jnp.float32)[:, :, None, :],
        (stream_count, group_count, GROUP, tap_count),
    )
    return jnp.transpose(spread.reshape(stream_count, group_count * GROUP, tap_count), (0, 2, 1))


def filter_tables(decay_rate, residue):
    lag_steps = jnp.arange(BLOCK, dtype=jnp.float32)
    scaled = residue * jnp.sqrt(2.0 * decay_rate)
    places = jnp.arange(BLOCK, dtype=jnp.int32)
    lagged = places[:, None] - places[None, :]
    lag_float = jnp.maximum(lagged, 0).astype(jnp.float32)
    terms = scaled[:, None, None, :] * jnp.exp(
        -decay_rate[:, None, None, :] * lag_float[None, :, :, None]
    )
    toeplitz = jnp.where(
        (lagged >= 0)[:, :, None], jnp.sum(terms, axis=0), jnp.zeros((), jnp.float32)
    )
    end_weight = jnp.exp(-decay_rate[:, None, :] * (BLOCK - 1.0 - lag_steps)[None, :, None])
    out_weight = scaled[:, None, :] * jnp.exp(
        -decay_rate[:, None, :] * (lag_steps + 1.0)[None, :, None]
    )
    return (toeplitz, end_weight, out_weight)


def block_terms(signal, tables):
    toeplitz, end_weight, out_weight = tables
    pieces = signal.reshape(-1, BLOCK, signal.shape[-1])
    within = jnp.sum(toeplitz[None, :, :, :] * pieces[:, None, :, :], axis=2)
    block_ends = jnp.sum(end_weight[None, :, :, :] * pieces[:, None, :, :], axis=2)
    return (within, block_ends)


def chain_blocks(block_ends, block_decay):

    def advance(carried_state, block_term):
        return (block_decay * carried_state + block_term, carried_state)

    zero_state = jnp.zeros(block_decay.shape, jnp.float32)
    return lax.scan(advance, zero_state, block_ends)


def apply_states(within, entering, incoming, decay_rate, out_weight):
    block_count = entering.shape[0]
    offsets = jnp.arange(block_count, dtype=jnp.float32) * BLOCK
    entering = (
        entering + jnp.exp(-decay_rate[None, :, :] * offsets[:, None, None]) * incoming[None, :, :]
    )
    carried = jnp.sum(out_weight[None, :, :, :] * entering[:, :, None, :], axis=1)
    return (within + carried).reshape(-1, within.shape[-1])


def scan_pieces(local_end, decay_rate, row_count):

    def combine(earlier_part, later_part):
        reach_decay = jnp.exp(-decay_rate * (row_count * later_part[0]))
        return (earlier_part[0] + later_part[0], reach_decay * earlier_part[1] + later_part[1])

    elements = (jnp.ones((), jnp.float32), local_end)
    identity = (jnp.zeros((), jnp.float32), jnp.zeros_like(local_end))
    return (elements, combine, identity)


def on_device(streams, short_filter, decay_rate, residue, norm_gain, out_grad):
    stream_count, row_count, channels = streams.shape
    reach_rows = short_filter.shape[2] - 1
    weights = channel_weights(short_filter)
    earlier_rows = shifted(streams[:, row_count - reach_rows :, :], "ctx", 1)
    extended = jnp.concatenate([earlier_rows, streams], axis=1)
    convolved = weights[:, 0, None, :] * extended[:, reach_rows:, :].astype(jnp.float32)
    for offset in range(1, reach_rows + 1):
        convolved = convolved + weights[:, offset, None, :] * extended[
            :, reach_rows - offset : reach_rows - offset + row_count, :
        ].astype(jnp.float32)
    query_conv = convolved[0]
    key_conv = convolved[1]
    value_conv = convolved[2]
    tables = filter_tables(decay_rate, residue)
    block_decay = jnp.exp(-decay_rate * BLOCK)
    within, block_ends = block_terms(key_conv * value_conv, tables)
    local_end, entering = chain_blocks(block_ends, block_decay)
    elements, combine, identity = scan_pieces(local_end, decay_rate, row_count)
    incoming = carried_in(elements, "ctx", combine, identity, False)[1]
    long_conv = apply_states(within, entering, incoming, decay_rate, tables[2])
    modulated = query_conv * long_conv
    scaled_grad = norm_gain * out_grad.astype(jnp.float32)
    square_sum, cross_sum = lax.psum(
        (jnp.sum(modulated * modulated, axis=1), jnp.sum(scaled_grad * modulated, axis=1)), "tp"
    )
    total_width = channels * lax.axis_size("tp")
    inverse = lax.rsqrt(square_sum / total_width + EPSILON)
    output = (norm_gain * modulated * inverse[:, None]).astype(jnp.bfloat16)
    mixed_grad = (
        inverse[:, None] * scaled_grad
        - modulated * (inverse * inverse * inverse * cross_sum / total_width)[:, None]
    )
    query_grad = mixed_grad * long_conv
    long_grad = mixed_grad * query_conv
    within_back, ends_back = block_terms(jnp.flip(long_grad, axis=0), tables)
    end_back, entering_back = chain_blocks(ends_back, block_decay)
    elements_back, combine_back, identity_back = scan_pieces(end_back, decay_rate, row_count)
    later_state = carried_in(elements_back, "ctx", combine_back, identity_back, True)[1]
    gated_grad = jnp.flip(
        apply_states(within_back, entering_back, later_state, decay_rate, tables[2]), axis=0
    )
    conv_grad = jnp.stack([query_grad, gated_grad * value_conv, gated_grad * key_conv])
    later_rows = shifted(for_sending(conv_grad[:, :reach_rows, :]), "ctx", -1)
    extended_grad = jnp.concatenate([conv_grad, later_rows], axis=1)
    summed = weights[:, 0, None, :] * conv_grad
    for offset in range(1, reach_rows + 1):
        summed = (
            summed + weights[:, offset, None, :] * extended_grad[:, offset : offset + row_count, :]
        )
    return (output, summed.astype(jnp.bfloat16))


def solution(mesh):
    return jax.shard_map(
        on_device,
        mesh=mesh,
        in_specs=(
            P(None, "ctx", "tp"),
            P(None, "tp", None),
            P(None, "tp"),
            P(None, "tp"),
            P("tp"),
            P("ctx", "tp"),
        ),
        out_specs=(P("ctx", "tp"), P(None, "ctx", "tp")),
        check_vma=False,
    )
```

profile of v0, /device:TPU:0, one launch (start us, length us, event | category | flops | bytes accessed | tf_op | source)
XLA Modules:
  0.0 257.8 jit_solution(14517318136616207579)
XLA Ops:
  8.2 4.8 %collective-permute-start = (bf16[3,6,2048]{2,1,0:T(8,128)(2,1)S(1)}, bf16[3,6,2048]{2,1,0:T(8,128)(2,1)S(1)}, u32[]{:S(2)}, u32[]{:S(2)}) collective-permute-start(bf16[3,6,2048]{2,1,0:T(8,128)(2,1)S(1)} %slice.82), channel_id=1, source_target_pairs={{0,4},{4,8},{8,12},{12,16},{16,20},{20,24},{24,28},{1,5},{5,9},{9,... | collective-permute-start | bytes 221192 | tf_op jit(solution)/shard_map/ppermute | solution.py:16
  13.1 1.1 broadcast_in_dim.20
  16.5 5.5 %multiply_reduce_fusion = f32[16,16,2048]{2,1,0:T(8,128)S(1)} fusion(f32[16,16]{1,0:T(8,128)S(1)} %maximum_convert_fusion, f32[16,2048]{1,0:T(8,128)S(1)} %get-tuple-element.587, f32[16,2048]{1,0:T(8,128)S(1)} %get-tuple-element.362), kind=kLoop, calls=%fused_computation.6 | loop fusion | flops 24641536 | bytes 2360320 | tf_op jit(solution)/shard_map/reduce_sum | solution.py:58
  22.0 2.6 exponential_multiply_fusion
  24.6 1.6 broadcast_select_fusion
  28.1 7.7 %multiply_add_fusion = f32[3,128,2048]{2,1,0:T(8,128)S(1)} fusion(bf16[3,128,2048]{2,1,0:T(8,128)(2,1)} %param.14, bf16[3,6,2048]{2,1,0:T(8,128)(2,1)} %copy-done.20, f32[3,2048]{1,0:T(4,128)} %get-tuple-element.367, f32[3,2048]{1,0:T(4,128)} %get-tuple-element.368, f32[3,2048]{1,0:T(4,128)} %get-tuple-element.369, f32[3,2048]{1,0:T(4,128)} %get-tuple-element.370, ...), kind=kLoop, calls=%fused_computation.33 | loop fusion | flops 29884416 | bytes 4964352 | tf_op jit(solution)/shard_map/add | solution.py:113
  35.9 11.5 %multiply_reduce_fusion.5 = (f32[8,16,2048]{2,1,0:T(8,128)}, f32[8,16,2048]{2,1,0:T(8,128)}) fusion(f32[16,16,2048]{2,1,0:T(8,128)} %get-tuple-element.359, f32[8,16,2048]{2,1,0:T(8,128)S(1)} %bitcast.83, f32[16,16,2048]{2,1,0:T(8,128)} %broadcast_select_fusion), kind=kLoop, calls=%fused_computation.11 | loop fusion | flops 16252928 | bytes 7340032 | tf_op jit(solution)/shard_map/reduce_sum | solution.py:71
  47.4 1.2 broadcast.98.clone
  48.6 13.3 %while.56 = (s32[]{:T(128)}, f32[16,2048]{1,0:T(8,128)S(1)}, f32[8,16,2048]{2,1,0:T(8,128)}, f32[16,2048]{1,0:T(8,128)S(1)}, f32[8,16,2048]{2,1,0:T(8,128)}, /*index=5*/s32[]{:T(128)}, s32[]{:T(128)}) while((s32[]{:T(128)}, f32[16,2048]{1,0:T(8,128)S(1)}, f32[8,16,2048]{2,1,0:T(8,128)}, f32[16,2048]{1,0:T(8,128)S(1)}, ...), condition=%wide.region_4.5_spmd.clone, body=%wide.region_3.4_spmd.clone.sunk | while | flops 131075 | bytes 787036 | solution.py:81
  64.0 19.6 %all-reduce = f32[8]{0:T(128)S(1)} all-reduce(f32[8]{0:T(128)S(1)} %dynamic-update-slice), channel_id=1, replica_groups=mesh['ctx'=8,'tp'=4] {'ctx'}, use_global_device_ids=true, to_apply=%add | all-reduce | flops 8 | bytes 64
  83.6 19.6 %all-gather.5.cloned.1.call-done = f32[128,2048]{1,0:T(8,128)} async-done(((f32[16,2048]{1,0:T(8,128)}), f32[128,2048]{1,0:T(8,128)}) %all-gather.5.cloned.1.call-update) | async-done | bytes 1048592 | tf_op jit(solution)/shard_map/all_gather | solution.py:23
  103.5 1.6 multiply_add_fusion.2
  105.4 1.3 multiply_reduce_fusion.4
  107.7 1.3 multiply_reduce_fusion.7
  109.0 5.6 %all-reduce.1 = (f32[128]{0:T(128)S(1)}, f32[128]{0:T(128)S(1)}) all-reduce(f32[128]{0:T(128)S(1)} %get-tuple-element.296, f32[128]{0:T(128)S(1)} %get-tuple-element.295), channel_id=1, replica_groups=mesh['ctx'=8,'tp'=4] {'tp'}, use_global_device_ids=true, to_apply=%region_9.10 | all-reduce | flops 256 | bytes 2048 | tf_op jit(solution)/shard_map/psum | solution.py:128
  114.7 3.6 %bitcast_multiply_fusion.2 = (f32[128,2048]{1,0:T(8,128)}, f32[128,2048]{1,0:T(8,128)}, bf16[128,2048]{1,0:T(8,128)(2,1)}) fusion(f32[8,16,2048]{2,1,0:T(8,128)} %copy-done.7, f32[128,2048]{1,0:T(8,128)} %get-tuple-element.345, bf16[128,2048]{1,0:T(8,128)(2,1)} %param.19, f32[128]{0:T(128)S(1)} %get-tuple-element.363, f32[128]{0:T(128)S(1)} %get-tuple-element.364, ...), kind=kLoop, calls=%fused_computation.50 | loop fusion | flops 2621440 | bytes 6300672 | tf_op jit(solution)/shard_map/mul | solution.py:138
  118.3 8.9 %rev.7 = f32[128,2048]{1,0:T(8,128)} reverse(f32[128,2048]{1,0:T(8,128)} %get-tuple-element.349), dimensions={0} | reverse | bytes 2097152 | tf_op jit(solution)/shard_map/jit(_flip)/rev | solution.py:140
  127.1 11.8 %multiply_reduce_fusion.2 = (f32[8,16,2048]{2,1,0:T(8,128)}, f32[8,16,2048]{2,1,0:T(8,128)}) fusion(f32[8,16,2048]{2,1,0:T(8,128)} %bitcast.84, f32[16,16,2048]{2,1,0:T(8,128)} %get-tuple-element.359, f32[16,16,2048]{2,1,0:T(8,128)} %broadcast_select_fusion), kind=kLoop, calls=%fused_computation.8 | loop fusion | flops 16252928 | bytes 7340032 | tf_op jit(solution)/shard_map/reduce_sum | solution.py:71
  138.9 1.1 broadcast.98
  140.0 13.3 %while.57 = (s32[]{:T(128)}, f32[16,2048]{1,0:T(8,128)S(1)}, f32[8,16,2048]{2,1,0:T(8,128)}, f32[16,2048]{1,0:T(8,128)S(1)}, f32[8,16,2048]{2,1,0:T(8,128)}, /*index=5*/s32[]{:T(128)}, s32[]{:T(128)}) while((s32[]{:T(128)}, f32[16,2048]{1,0:T(8,128)S(1)}, f32[8,16,2048]{2,1,0:T(8,128)}, f32[16,2048]{1,0:T(8,128)S(1)}, ...), condition=%wide.region_15.16_spmd.clone, body=%wide.region_14.15_spmd.clone.sunk | while | flops 131075 | bytes 787036 | solution.py:81
  154.1 55.0 %all-gather.7.cloned.1.call-done = f32[128,2048]{1,0:T(8,128)} async-done(((f32[16,2048]{1,0:T(8,128)}), f32[128,2048]{1,0:T(8,128)}) %all-gather.7.cloned.1.call-update) | async-done | bytes 1048592 | tf_op jit(solution)/shard_map/all_gather | solution.py:23
  209.1 15.9 %while.55 = (s32[]{:T(128)}, f32[16,2048]{1,0:T(8,128)S(1)}, s32[]{:T(128)}, f32[8]{0:T(128)S(1)}, f32[16,2048]{1,0:T(8,128)S(1)}, /*index=5*/f32[8,16,2048]{2,1...) while((s32[]{:T(128)}, f32[16,2048]{1,0:T(8,128)S(1)}, s32[]{:T(128)}, ...), condition=%wide.region_17.18_spmd, body=%wide.region_16.17_spmd.sunk | while | flops 98311 | bytes 524475 | solution.py:32
  210.3 1.0 bitcast_add_fusion.9
  212.6 1.0 bitcast_add_fusion.9
  225.0 1.6 multiply_add_fusion.1
  226.9 1.3 multiply_reduce_fusion.1
  228.1 1.1 add.145
  229.2 8.9 %rev.8 = f32[128,2048]{1,0:T(8,128)} reverse(f32[128,2048]{1,0:T(8,128)} %bitcast.85), dimensions={0} | reverse | bytes 2097152 | tf_op jit(solution)/shard_map/jit(_flip)/rev | solution.py:144
  238.1 1.5 fusion.13
  240.0 1.3 collective-permute-start.1
  241.3 5.2 %collective-permute-done.1 = bf16[3,6,2048]{2,1,0:T(8,128)(2,1)S(1)} collective-permute-done((bf16[3,6,2048]{2,1,0:T(8,128)(2,1)S(1)}, bf16[3,6,2048]{2,1,0:T(8,128)(2,1)S(1)}, u32[]{:S(2)}, u32[]{:S(2)}) %collective-permute-start.1) | collective-permute-done | bytes 73760 | tf_op jit(solution)/shard_map/ppermute | solution.py:16
  247.4 3.5 %fusion.1 = bf16[3,128,2048]{2,1,0:T(8,128)(2,1)} fusion(f32[3,134,2048]{2,1,0:T(8,128)S(1)} %pad_maximum_fusion, f32[3,2048]{1,0:T(4,128)S(1)} %copy-done.11, f32[3,2048]{1,0:T(4,128)S(1)} %copy-done.12, f32[3,2048]{1,0:T(4,128)S(1)} %copy-done.13, f32[3,2048]{1,0:T(4,128)S(1)} %copy-done.14, f32[3,2048]{1,0:T(4,128)S(1)} %copy-done.15, ...), kind=kLoop, calls=%fused_computation.21 | loop fusion | flops 12582912 | bytes 23764992 | tf_op jit(solution)/shard_map/convert_element_type | solution.py:155
  (122 shorter events, 46.7 us)
Async XLA Ops:
  7.2 9.3 %copy-start.18 = (f32[16,2048]{1,0:T(8,128)S(1)}, f32[16,2048]{1,0:T(8,128)}, u32[]{:S(2)}) copy-start(f32[16,2048]{1,0:T(8,128)} %param.16) | copy-start | bytes 393220
  7.2 9.3 %copy-start.19 = (f32[16,2048]{1,0:T(8,128)S(1)}, f32[16,2048]{1,0:T(8,128)}, u32[]{:S(2)}) copy-start(f32[16,2048]{1,0:T(8,128)} %param.17) | copy-start | bytes 393220
  7.2 96.0 %all-gather.5.cloned.1.call-start = ((), (), s32[]{:S(2)}) async-start(), calls=%async_computation | async-start | bytes 1179648 | tf_op jit(solution)/shard_map/all_gather | solution.py:23
  8.2 19.2 %collective-permute-start = (bf16[3,6,2048]{2,1,0:T(8,128)(2,1)S(1)}, bf16[3,6,2048]{2,1,0:T(8,128)(2,1)S(1)}, u32[]{:S(2)}, u32[]{:S(2)}) collective-permute-start(bf16[3,6,2048]{2,1,0:T(8,128)(2,1)S(1)} %slice.82), channel_id=1, source_target_pairs={{0,4},{4,8},{8,12},{12,16},{16,20},{20,24},{24,28},{1,5},{5,9},{9,... | collective-permute-start | bytes 221192 | tf_op jit(solution)/shard_map/ppermute | solution.py:16
  27.5 0.6 copy-start.20
  47.4 15.3 %copy-start.22 = (u32[32]{0:T(128)S(1)}, u32[32]{0:T(128)}, u32[]{:S(2)}) copy-start(u32[32]{0:T(128)} %constant.117) | copy-start | bytes 388
  61.9 0.7 copy-start.4
  61.9 21.7 %copy-start.5 = (f32[16,2048]{1,0:T(8,128)}, f32[16,2048]{1,0:T(8,128)S(1)}, u32[]{:S(2)}) copy-start(f32[16,2048]{1,0:T(8,128)S(1)} %get-tuple-element.624) | copy-start | bytes 393220
  62.6 146.5 %all-gather.7.cloned.1.call-start = ((), (), s32[]{:S(2)}) async-start(), calls=%async_computation.1 | async-start | bytes 1179648 | tf_op jit(solution)/shard_map/all_gather | solution.py:23
  103.4 1.9 copy-start
  103.5 3.2 %copy-start.8 = (f32[8,16,2048]{2,1,0:T(8,128)S(1)}, f32[8,16,2048]{2,1,0:T(8,128)}, u32[]{:S(2)}) copy-start(f32[8,16,2048]{2,1,0:T(8,128)} %get-tuple-element.298) | copy-start | bytes 3145732
  105.3 2.4 copy-start.10
  105.4 2.4 copy-start.21
  106.8 1.0 copy-start.7
  127.1 12.9 %copy-start.6 = (f32[16,2048]{1,0:T(8,128)S(1)}, f32[16,2048]{1,0:T(8,128)}, u32[]{:S(2)}) copy-start(f32[16,2048]{1,0:T(8,128)} %copy-done.5) | copy-start | bytes 393220
  153.4 0.7 copy-start.3
  225.0 1.9 copy-start.1
  225.0 3.2 %copy-start.9 = (f32[8,16,2048]{2,1,0:T(8,128)S(1)}, f32[8,16,2048]{2,1,0:T(8,128)}, u32[]{:S(2)}) copy-start(f32[8,16,2048]{2,1,0:T(8,128)} %get-tuple-element.294) | copy-start | bytes 3145732
  238.1 1.5 copy-start.2
  240.0 6.5 %collective-permute-start.1 = (bf16[3,6,2048]{2,1,0:T(8,128)(2,1)S(1)}, bf16[3,6,2048]{2,1,0:T(8,128)(2,1)S(1)}, u32[]{:S(2)}, u32[]{:S(2)}) collective-permute-start(bf16[3,6,2048]{2,1,0:T(8,128)(2,1)S(1)} %slice.207), channel_id=1, source_target_pairs={{4,0},{8,4},{12,8},{16,12},{20,16},{24,20},{28,24},{5,1},{9,5},{13... | collective-permute-start | bytes 221192 | tf_op jit(solution)/shard_map/ppermute | solution.py:16
  246.5 0.8 copy-start.11
  246.6 0.8 copy-start.12
  246.6 0.8 copy-start.13
  246.6 0.8 copy-start.14
  246.6 0.8 copy-start.15
  246.6 0.8 copy-start.16
  246.6 0.8 copy-start.17
Sparse Core Ops, SparseCore 0:
  62.7 40.4 all-gather.4
  154.2 54.8 all-gather.6
where the time goes:
time: 260 us; the launch traced here: 258 us
  other arithmetic  91.8 us (35%)
  waiting for transfers between devices  79.8 us (31%)
  local copies, waits for them, and re-layouts  35 us (13%)
  blocking collectives  25.2 us (10%)
  between operations  14.4 us (6%)
  starting transfers between devices  6.22 us (2%)
  loops' own time  5.31 us (2%)
    all_gather x2, waiting for transfers between devices, carried_in(): gathered = jax.tree.map(lambda a: lax.all_gather(a, axis), part)  74.6 us
    reduce_sum x2, other arithmetic, block_terms(): jnp.sum(end_weight[None, :, :, :] * pieces[:, None, :, :], axis=2)  23.3 us
    unnamed x1, blocking collectives  19.6 us
    add x16, other arithmetic, advance(): return (block_decay * carried_state + block_term, carried_state)  15.7 us
    dynamic_update_slice x16, other arithmetic, chain_blocks(): return lax.scan(advance, zero_state, block_ends)  10.7 us
    rev x1, local copies, waits for them, and re-layouts, on_device(): jnp.flip(apply_states(within_back, entering_back, later_state, decay_rate...  8.87 us
    rev x1, local copies, waits for them, and re-layouts, on_device(): within_back, ends_back = block_terms(jnp.flip(long_grad, axis=0), tables)  8.86 us
    unnamed x53, local copies, waits for them, and re-layouts  7.81 us
  transfers between devices with their start and end apart: 4, of which 3 were waited for; matrix products, arithmetic and copies ran while one was open for 6% of the time, Pallas kernels for 0%

commit v1 on v0

v1 whole, which is shorter than its diff:
```python
import functools

import jax
import jax.numpy as jnp
from jax import lax
from jax.experimental import pallas as pl
from jax.experimental.pallas import tpu as pltpu
from jax.sharding import PartitionSpec as P

GROUP = 16
LANES = 128
SUB = 8
EPSILON = 1e-05
VMEM_LIMIT = 48 * 1024 * 1024


def halves(lane_blocks):
    return [pl.ds(SUB * h, SUB) for h in range(lane_blocks // SUB)]


def total(terms):
    terms = list(terms)
    while len(terms) > 1:
        paired = [terms[i] + terms[i + 1] for i in range(0, len(terms) - 1, 2)]
        terms = paired + ([terms[-1]] if len(terms) % 2 else [])
    return terms[0]


def spread_rows(source, target, first, pitch, lane_blocks):
    rows = source.shape[0]
    for lb in range(lane_blocks):
        tile = source[:, lb * LANES : (lb + 1) * LANES]
        target[pl.ds(first + lb * pitch, rows), :] = tile.astype(jnp.float32)


def row_at(ref, first, pitch, half, place):
    return ref[pl.ds(first + half * SUB * pitch + place, SUB, stride=pitch), :]


def prepare_kernel(x, filt, rate, res, conv, table, taps, ends, xs, ps):
    rows, channels = x.shape[1:]
    modes = rate.shape[0]
    lane_blocks = channels // LANES
    tap_count = taps.shape[1]
    pitch = rows + SUB
    spread = (
        lax.broadcasted_iota(jnp.int32, (SUB, LANES), 1) // GROUP
        == lax.broadcasted_iota(jnp.int32, (SUB, LANES), 0)
    ).astype(jnp.bfloat16)
    weights = jnp.dot(filt[...], spread, preferred_element_type=jnp.float32)
    taps[...] = weights.reshape(taps.shape)
    spread_rows(rate, ps, 0, modes, lane_blocks)
    spread_rows(res, ps, lane_blocks * modes, modes, lane_blocks)
    for h, half in enumerate(halves(lane_blocks)):
        for m in range(modes):
            r = row_at(ps, 0, modes, h, m)
            c = row_at(ps, lane_blocks * modes, modes, h, m)
            table[0, m, half, :] = jnp.exp(-r)
            table[1, m, half, :] = c * jnp.sqrt(2.0 * r)
            table[2, m, half, :] = r
    zero = jnp.zeros((SUB, LANES), jnp.float32)
    for s in range(3):
        first = s * lane_blocks * pitch
        for lb in range(lane_blocks):
            xs[pl.ds(first + lb * pitch, SUB), :] = zero
        spread_rows(x.at[s], xs, first + SUB, pitch, lane_blocks)
    for h, half in enumerate(halves(lane_blocks)):
        for s in range(3):
            first = s * lane_blocks * pitch + SUB
            w = [taps[s, i, half, :] for i in range(tap_count)]

            def body(block, window):
                window = list(window)
                for k in range(SUB):
                    t = block * SUB + k
                    window.append(row_at(xs, first, pitch, h, t))
                    conv[s, t, half, :] = total(
                        w[i] * window[-1 - i] for i in range(tap_count)
                    )
                return tuple(window[-(tap_count - 1) :])

            lax.fori_loop(0, rows // SUB, body, (zero,) * (tap_count - 1))
        decay = [table[0, m, half, :] for m in range(modes)]

        def step(t, state):
            u = conv[1, t, half, :] * conv[2, t, half, :]
            return tuple(decay[m] * state[m] + u for m in range(modes))

        state = (zero,) * modes
        for t in range(tap_count - 1, SUB):
            state = step(t, state)

        def block_step(block, state):
            for k in range(SUB):
                state = step(block * SUB + k, state)
            return state

        state = lax.fori_loop(1, rows // SUB, block_step, state)
        for m in range(modes):
            ends[m, half, :] = state[m]


def head_kernel(conv_in, halo, table, taps, ends, conv, state_out, hs):
    del conv_in
    rows = conv.shape[1]
    modes, lane_blocks = ends.shape[:2]
    reach = taps.shape[1] - 1
    for s in range(3):
        spread_rows(halo.at[s], hs, s * lane_blocks * SUB, SUB, lane_blocks)
    for h, half in enumerate(halves(lane_blocks)):
        heads = []
        for s in range(3):
            w = [taps[s, i, half, :] for i in range(reach + 1)]
            before = [row_at(hs, s * lane_blocks * SUB, SUB, h, j) for j in range(SUB)]
            head = []
            for t in range(reach):
                row = conv[s, t, half, :] + total(
                    w[i] * before[SUB + t - i] for i in range(t + 1, reach + 1)
                )
                conv[s, t, half, :] = row
                head.append(row)
            heads.append(head)
        product = [heads[1][t] * heads[2][t] for t in range(reach)]
        for m in range(modes):
            decay = table[0, m, half, :]
            state = product[0]
            for t in range(1, reach):
                state = decay * state + product[t]
            fade = jnp.exp(table[2, m, half, :] * -float(rows - reach))
            state_out[m, half, :] = ends[m, half, :] + fade * state


def local_kernel(conv, table, local):
    rows = conv.shape[1]
    modes, lane_blocks = table.shape[1:3]
    zero = jnp.zeros((SUB, LANES), jnp.float32)
    for half in halves(lane_blocks):
        decay = [table[0, m, half, :] for m in range(modes)]
        scale = [table[1, m, half, :] for m in range(modes)]

        def block_step(block, state):
            for k in range(SUB):
                t = block * SUB + k
                u = conv[1, t, half, :] * conv[2, t, half, :]
                state = tuple(decay[m] * state[m] + u for m in range(modes))
                local[t, half, :] = total(scale[m] * state[m] for m in range(modes))
            return state

        lax.fori_loop(0, rows // SUB, block_step, (zero,) * modes)


def carry_kernel(entering, received, table, conv, local, gain, grad, long_conv, scaled, sums, gs, sq, cr):
    rows = local.shape[0]
    modes, lane_blocks = table.shape[1:3]
    pitch = rows + SUB
    spread_rows(grad, gs, 0, pitch, lane_blocks)
    for h, half in enumerate(halves(lane_blocks)):
        decay = [table[0, m, half, :] for m in range(modes)]
        start = []
        for m in range(modes):
            fade = jnp.exp(table[2, m, half, :] * -float(rows))
            incoming = fade * entering[m, half, :] + received[m, half, :]
            start.append(table[1, m, half, :] * decay[m] * incoming)
        g = gain[half, :]

        def block_step(block, state):
            for k in range(SUB):
                t = block * SUB + k
                row = local[t, half, :] + total(state)
                state = tuple(decay[m] * state[m] for m in range(modes))
                long_conv[t, half, :] = row
                modulated = conv[0, t, half, :] * row
                sg = g * row_at(gs, 0, pitch, h, t)
                scaled[t, half, :] = sg
                place = pl.ds(pl.multiple_of(t * SUB, SUB), SUB)
                if h == 0:
                    sq[place, :] = modulated * modulated
                    cr[place, :] = sg * modulated
                else:
                    sq[place, :] += modulated * modulated
                    cr[place, :] += sg * modulated
            return state

        lax.fori_loop(0, rows // SUB, block_step, tuple(start))
    for which, ref in enumerate((sq, cr)):
        blocks = []
        for b in range(rows // SUB):
            blocks.append(
                total(
                    ref[pl.ds(b * SUB * SUB + s, SUB, stride=SUB), :] for s in range(SUB)
                )
            )
        by_row = jnp.concatenate(blocks, axis=0)
        sums[which : which + 1, :] = jnp.sum(jnp.transpose(by_row), axis=0, keepdims=True)


def mixed_kernel(width, sums, table, conv, long_conv, scaled, mixed, long_grad, state_out, inv, inv_s, off_s):
    rows = long_conv.shape[0]
    modes, lane_blocks = table.shape[1:3]
    zero = jnp.zeros((SUB, LANES), jnp.float32)
    inverse = lax.rsqrt(sums[0:1, :] / width + EPSILON)
    offset = inverse * inverse * inverse * sums[1:2, :] / width
    inv_s[...] = jnp.transpose(jnp.broadcast_to(inverse, (LANES, rows)))
    off_s[...] = jnp.transpose(jnp.broadcast_to(offset, (LANES, rows)))
    inv[...] = inv_s[...]
    blocks = rows // SUB
    for half in halves(lane_blocks):
        decay = [table[0, m, half, :] for m in range(modes)]

        def block_step(block, state):
            for k in range(SUB):
                t = (blocks - 1 - block) * SUB + SUB - 1 - k
                q = conv[0, t, half, :]
                modulated = q * long_conv[t, half, :]
                mix = (
                    inv_s[pl.ds(t, 1), :] * scaled[t, half, :] - off_s[pl.ds(t, 1), :] * modulated
                )
                mixed[t, half, :] = mix
                lg = mix * q
                long_grad[t, half, :] = lg
                state = tuple(decay[m] * state[m] + lg for m in range(modes))
            return state

        state = lax.fori_loop(0, blocks, block_step, (zero,) * modes)
        for m in range(modes):
            state_out[m, half, :] = state[m]


def output_kernel(inv, table, gain, conv, long_conv, mixed, long_grad, output, query_grad, local, head, os):
    rows = long_conv.shape[0]
    modes, lane_blocks = table.shape[1:3]
    pitch = rows + SUB
    blocks = rows // SUB
    zero = jnp.zeros((SUB, LANES), jnp.float32)
    for h, half in enumerate(halves(lane_blocks)):
        decay = [table[0, m, half, :] for m in range(modes)]
        scale = [table[1, m, half, :] for m in range(modes)]
        g = gain[half, :]

        def block_step(block, state):
            for k in range(SUB):
                t = (blocks - 1 - block) * SUB + SUB - 1 - k
                lg = long_grad[t, half, :]
                state = tuple(decay[m] * state[m] + lg for m in range(modes))
                local[t, half, :] = total(scale[m] * state[m] for m in range(modes))
            return state

        lax.fori_loop(0, blocks, block_step, (zero,) * modes)

        def out_step(block, _):
            for k in range(SUB):
                t = block * SUB + k
                long_row = long_conv[t, half, :]
                query_grad[t, half, :] = mixed[t, half, :] * long_row
                row = g * (conv[0, t, half, :] * long_row) * inv[pl.ds(t, 1), :]
                os[pl.ds(h * SUB * pitch + t, SUB, stride=pitch), :] = row
            return 0

        lax.fori_loop(0, blocks, out_step, 0)
        for t in range(SUB):
            head[0, t, half, :] = query_grad[t, half, :]
            head[1, t, half, :] = local[t, half, :]
            head[2, t, half, :] = conv[2, t, half, :]
            head[3, t, half, :] = conv[1, t, half, :]
    for lb in range(lane_blocks):
        output[:, lb * LANES : (lb + 1) * LANES] = os[pl.ds(lb * pitch, rows), :].astype(output.dtype)


def far_rows(table, half, state, rows, reach, fade_first):
    modes = table.shape[1]
    at = [
        table[1, m, half, :]
        * state[m]
        * jnp.exp(table[2, m, half, :] * -float(rows - reach + 1 + fade_first))
        for m in range(modes)
    ]
    found = [None] * reach
    for i in reversed(range(reach)):
        found[i] = total(at)
        if i:
            at = [at[m] * table[0, m, half, :] for m in range(modes)]
    return found


def turn_kernel(rows, reach, lower, near, beyond, table, own, entering, message):
    modes, lane_blocks = own.shape[:2]
    is_lower = jnp.full((SUB, LANES), lower[0]) > 0
    for half in halves(lane_blocks):
        state = []
        for m in range(modes):
            step = jnp.exp(table[2, m, half, :] * -float(2 * rows))
            e = near[m, half, :] + step * beyond[m, half, :]
            entering[m, half, :] = e
            message[m, half, :] = jnp.where(is_lower, e, own[m, half, :] + step * e)
            state.append(jnp.where(is_lower, beyond[m, half, :], e))
        added = far_rows(table, half, state, rows, reach, rows)
        for i in range(reach):
            message[modes + i, half, :] = added[i]
        for i in range(reach, SUB):
            message[modes + i, half, :] = jnp.zeros((SUB, LANES), jnp.float32)


def final_kernel(entering, received, table, taps, conv, local, query_grad, head, grads, cg, os):
    rows = local.shape[0]
    modes, lane_blocks = table.shape[1:3]
    tap_count = taps.shape[1]
    reach = tap_count - 1
    pitch = rows + SUB
    blocks = rows // SUB
    for h, half in enumerate(halves(lane_blocks)):
        decay = [table[0, m, half, :] for m in range(modes)]
        start = []
        for m in range(modes):
            fade = jnp.exp(table[2, m, half, :] * -float(rows))
            incoming = fade * entering[m, half, :] + received[m, half, :]
            start.append(table[1, m, half, :] * decay[m] * incoming)

        def block_step(block, state):
            for k in range(SUB):
                t = (blocks - 1 - block) * SUB + SUB - 1 - k
                gated = local[t, half, :] + total(state)
                state = tuple(decay[m] * state[m] for m in range(modes))
                cg[0, t, half, :] = gated * conv[2, t, half, :]
                cg[1, t, half, :] = gated * conv[1, t, half, :]
            return state

        lax.fori_loop(0, blocks, block_step, tuple(start))
        own = far_rows(table, half, [entering[m, half, :] for m in range(modes)], rows, reach, 0)
        beyond = [[], [], []]
        for i in range(reach):
            gated = head[1, i, half, :] + received[modes + i, half, :] + own[i]
            beyond[0].append(head[0, i, half, :])
            beyond[1].append(gated * head[2, i, half, :])
            beyond[2].append(gated * head[3, i, half, :])
        for s in range(3):
            w = [taps[s, i, half, :] for i in range(tap_count)]

            def conv_step(block, window):
                window = list(window)
                for k in range(SUB):
                    t = (blocks - 1 - block) * SUB + SUB - 1 - k
                    row = query_grad[t, half, :] if s == 0 else cg[s - 1, t, half, :]
                    window.insert(0, row)
                    os[pl.ds((s * lane_blocks + h * SUB) * pitch + t, SUB, stride=pitch), :] = total(
                        w[i] * window[i] for i in range(tap_count)
                    )
                return tuple(window[:reach])

            lax.fori_loop(0, blocks, conv_step, tuple(beyond[s]))
    for s in range(3):
        for lb in range(lane_blocks):
            grads[s, :, lb * LANES : (lb + 1) * LANES] = os[
                pl.ds((s * lane_blocks + lb) * pitch, rows), :
            ].astype(grads.dtype)


def run(kernel, ins, outs, scratch=(), flops=0, aliases=None, kept=True):
    out_shapes, out_specs = [], []
    for shape, dtype in outs:
        out_shapes.append(jax.ShapeDtypeStruct(shape, dtype))
        out_specs.append(pl.BlockSpec(memory_space=pltpu.VMEM))
    in_specs = [
        pl.BlockSpec(memory_space=pltpu.SMEM if i.dtype == jnp.int32 else pltpu.VMEM) for i in ins
    ]
    return pl.pallas_call(
        kernel,
        out_shape=out_shapes,
        in_specs=in_specs,
        out_specs=out_specs,
        scratch_shapes=[pltpu.VMEM(s, jnp.float32) for s in scratch],
        input_output_aliases=aliases or {},
        compiler_params=pltpu.CompilerParams(vmem_limit_bytes=VMEM_LIMIT),
        cost_estimate=pl.CostEstimate(flops=flops, bytes_accessed=4 * 1024 * 1024, transcendentals=0),
    )(*ins)


def shifted(block, distance):
    devices = range(lax.axis_size("ctx"))
    route = [(i, i + distance) for i in devices if i + distance in devices]
    return lax.ppermute(block, "ctx", route)


def swapped(block):
    return lax.ppermute(block, "ctx", [(i, i ^ 1) for i in range(lax.axis_size("ctx"))])


def on_device(streams, short_filter, decay_rate, residue, norm_gain, out_grad):
    f32 = jnp.float32
    stream_count, rows, channels = streams.shape
    modes = decay_rate.shape[0]
    lane_blocks = channels // LANES
    tap_count = short_filter.shape[2]
    reach = tap_count - 1
    pitch = rows + SUB
    count = lax.axis_size("ctx")
    row_shape = (rows, lane_blocks, LANES)
    state_shape = (modes, lane_blocks, LANES)

    halo = shifted(streams[:, rows - SUB :, :], 1)
    filt = jnp.transpose(
        short_filter.reshape(stream_count, lane_blocks, SUB, tap_count), (0, 3, 1, 2)
    ).reshape(stream_count * tap_count * lane_blocks, SUB)
    gain = norm_gain.reshape(lane_blocks, LANES)
    conv, table, taps, ends = run(
        prepare_kernel,
        (streams, filt, decay_rate, residue),
        (
            ((3,) + row_shape, f32),
            ((3,) + state_shape, f32),
            ((3, tap_count, lane_blocks, LANES), f32),
            (state_shape, f32),
        ),
        ((3 * lane_blocks * pitch, LANES), (2 * lane_blocks * modes, LANES)),
    )
    conv, state = run(
        head_kernel,
        (conv, halo, table, taps, ends),
        (((3,) + row_shape, f32), (state_shape, f32)),
        ((3 * lane_blocks * SUB, LANES),),
        aliases={0: 0},
    )
    rate = table[2]
    lower = (1 - lax.axis_index("ctx") % 2).astype(jnp.int32)

    inclusive = state
    entering = None
    width = 1
    while 2 * width < count:
        got = shifted(inclusive, 2 * width)
        if entering is None:
            entering = got
        else:
            entering = entering + jnp.exp(rate * -float(2 * rows * (width - 1))) * got
        inclusive = state + jnp.exp(rate * -float(2 * rows)) * entering
        width *= 2
    received = swapped(jnp.where(lower > 0, inclusive, entering))
    (local,) = run(local_kernel, (conv, table), ((row_shape, f32),), flops=10**9)
    long_conv, scaled, sums = run(
        carry_kernel,
        (entering, received, table, conv, local, gain, out_grad),
        ((row_shape, f32), (row_shape, f32), ((2, rows), f32)),
        ((lane_blocks * pitch, LANES), (rows * SUB, LANES), (rows * SUB, LANES)),
    )
    sums = lax.psum(sums, "tp")
    mixed, long_grad, back, inv = run(
        functools.partial(mixed_kernel, float(channels * lax.axis_size("tp"))),
        (sums, table, conv, long_conv, scaled),
        ((row_shape, f32), (row_shape, f32), (state_shape, f32), ((rows, LANES), f32)),
        ((rows, LANES), (rows, LANES)),
    )

    inclusive = back
    near = beyond = None
    width = 1
    while 2 * width < count:
        got = shifted(inclusive, -2 * width)
        if near is None:
            near, beyond = got, jnp.zeros_like(got)
            inclusive = back + jnp.exp(rate * -float(2 * rows)) * near
        else:
            beyond = beyond + jnp.exp(rate * -float(2 * rows * (width - 2))) * got
            if 4 * width < count:
                step = jnp.exp(rate * -float(2 * rows))
                inclusive = back + step * (near + step * beyond)
        width *= 2
    output, query_grad, local_back, head = run(
        output_kernel,
        (inv, table, gain, conv, long_conv, mixed, long_grad),
        (
            ((rows, channels), jnp.bfloat16),
            (row_shape, f32),
            (row_shape, f32),
            ((4, SUB, lane_blocks, LANES), f32),
        ),
        ((lane_blocks * pitch, LANES),),
        flops=10**9,
    )
    head = shifted(head, -1)
    entering_back, message = run(
        functools.partial(turn_kernel, rows, reach),
        (lower[None], near, beyond, table, back),
        ((state_shape, f32), ((modes + SUB, lane_blocks, LANES), f32)),
    )
    received_back = swapped(message)
    (grads,) = run(
        final_kernel,
        (entering_back, received_back, table, taps, conv, local_back, query_grad, head),
        (((3, rows, channels), jnp.bfloat16),),
        ((2, rows, lane_blocks, LANES), (3 * lane_blocks * pitch, LANES)),
    )
    return output, grads


def solution(mesh):
    return jax.shard_map(
        on_device,
        mesh=mesh,
        in_specs=(
            P(None, "ctx", "tp"),
            P(None, "tp", None),
            P(None, "tp"),
            P(None, "tp"),
            P("tp"),
            P("ctx", "tp"),
        ),
        out_specs=(P("ctx", "tp"), P(None, "ctx", "tp")),
        check_vma=False,
    )
```

time: 260 us -> 91.7 us (0.35)
  other arithmetic: 91.8 us -> 1.83 us
  waiting for transfers between devices: 79.8 us -> 24 us
  Pallas kernels: 0 us -> 26.3 us
  local copies, waits for them, and re-layouts: 35 us -> 11.5 us
  blocking collectives: 25.2 us -> 5.63 us
  starting transfers between devices: 6.22 us -> 20.9 us
  between operations: 14.4 us -> 0.78 us
  loops' own time: 5.31 us -> 0 us
    all_gather x2 -> x0, waiting for transfers between devices: 74.6 us -> none  [carried_in(): gathered = jax.tree.map(lambda a: lax.all_gather(a, axis), part)]
    add x28 -> x2, other arithmetic: 34.7 us -> 0.73 us  [the longest x1 0.69 us: on_device(): inclusive = state + jnp.exp(rate * -float(2 * rows)) * entering]
    reduce_sum x6 -> x0, other arithmetic: 32.6 us -> none  [the longest x2 23.3 us: block_terms(): jnp.sum(end_weight[None, :, :, :] * pieces[:, None, :, :], axis=2)]
    pallas_call x0 -> x8, Pallas kernels: none -> 26.3 us  [run(): pl.pallas_call(kernel, out_shape=out_shapes, in_specs=in_specs, out_specs...]
    unnamed x1 -> x0, blocking collectives: 19.6 us -> none
    ppermute x2 -> x8, waiting for transfers between devices: 5.21 us -> 24 us  [the longest x6 20.5 us: shifted(): return lax.ppermute(block, 'ctx', route)]
    rev x2 -> x0, local copies, waits for them, and re-layouts: 17.7 us -> none  [the longest x1 8.87 us: on_device(): jnp.flip(apply_states(within_back, entering_back, later_state, decay_rate...]
    ppermute x2 -> x8, starting transfers between devices: 6.14 us -> 20.9 us  [the longest x6 18.3 us: shifted(): return lax.ppermute(block, 'ctx', route)]
  transfers between devices with their start and end apart: 4 -> 8, of which waited for: 3 -> 7; matrix products, arithmetic and copies ran while one was open for 6% -> 2% of each run, Pallas kernels for 0% -> 13%
where the time goes in v1:
time: 91.7 us; the launch traced here: 91 us
  Pallas kernels  26.3 us (29%)
  waiting for transfers between devices  24 us (26%)
  starting transfers between devices  20.9 us (23%)
  local copies, waits for them, and re-layouts  11.5 us (13%)
  blocking collectives  5.63 us (6%)
  other arithmetic  1.83 us (2%)
    pallas_call x8, Pallas kernels, run(): pl.pallas_call(kernel, out_shape=out_shapes, in_specs=in_specs, out_specs...  26.3 us
    ppermute x6, waiting for transfers between devices, shifted(): return lax.ppermute(block, 'ctx', route)  20.5 us
    ppermute x6, starting transfers between devices, shifted(): return lax.ppermute(block, 'ctx', route)  18.3 us
    unnamed x32, local copies, waits for them, and re-layouts  8.51 us
    psum x1, blocking collectives, on_device(): sums = lax.psum(sums, 'tp')  5.63 us
    ppermute x2, waiting for transfers between devices, swapped(): lax.ppermute(block, 'ctx', [(i, i ^ 1) for i in range(lax.axis_size('ctx'...  3.48 us
    ppermute x2, starting transfers between devices, swapped(): lax.ppermute(block, 'ctx', [(i, i ^ 1) for i in range(lax.axis_size('ctx'...  2.6 us
  transfers between devices with their start and end apart: 8, of which 7 were waited for; matrix products, arithmetic and copies ran while one was open for 2% of the time, Pallas kernels for 13%

profile of v1, /device:TPU:0, one launch (start us, length us, event | category | flops | bytes accessed | tf_op | source)
XLA Modules:
  0.0 91.0 jit_solution(7907928899263576531)
XLA Ops:
  0.6 1.5 %slice.6 = bf16[3,8,2048]{2,1,0:T(8,128)(2,1)} slice(bf16[3,128,2048]{2,1,0:T(8,128)(2,1)} %x.1), slice={[0:3], [120:128], [0:2048]} | slice | bytes 196608 | tf_op jit(solution)/shard_map/slice | solution.py:399
  2.2 5.5 %collective-permute-start = (bf16[3,8,2048]{2,1,0:T(8,128)(2,1)}, bf16[3,8,2048]{2,1,0:T(8,128)(2,1)}, u32[]{:S(2)}, u32[]{:S(2)}) collective-permute-start(bf16[3,8,2048]{2,1,0:T(8,128)(2,1)} %slice.6), channel_id=1, source_target_pairs={{0,4},{4,8},{8,12},{12,16},{16,20},{20,24},{24,28},{1,5},{5,9},{9,... | collective-permute-start | bytes 294920 | tf_op jit(solution)/shard_map/ppermute | solution.py:380
  7.7 1.5 %reshape.19 = bf16[3,16,8,7]{2,1,3,0:T(8,128)(2,1)} reshape(bf16[3,128,7]{1,2,0:T(8,128)(2,1)} %param.7) | data formatting | bytes 10752 | tf_op jit(solution)/shard_map/reshape | solution.py:401
  9.1 1.4 %copy-done.4 = bf16[3,128,2048]{2,1,0:T(8,128)(2,1)S(1)} copy-done((bf16[3,128,2048]{2,1,0:T(8,128)(2,1)S(1)}, bf16[3,128,2048]{2,1,0:T(8,128)(2,1)}, u32[]{:S(2)}) %copy-start.4) | copy-done | bytes 1572888
  11.4 0.9 copy-done.12
  13.2 3.4 %shard_map.77 = (f32[3,128,16,128]{3,2,1,0:T(8,128)S(1)}, f32[3,16,16,128]{3,2,1,0:T(8,128)S(1)}, f32[3,7,16,128]{3,2,1,0:T(8,128)S(1)}, f32[16,16,128]{2,1,0:T(8,128)S(1)}) custom-call(bf16[3,128,2048]{2,1,0:T(8,128)(2,1)S(1)} %copy-done.4, bf16[336,8]{1,0:T(8,128)(2,1)S(1)} %bitcast.25, f32[16,2048]{1,0:T(8,128)S(1)} %copy-done.12, f32[16,2048]{1,0:T(8,128)S(1)} %copy-done.13), custom_call_target="tpu_custom_call" | custom-call | bytes 4194304 | tf_op jit(solution)/shard_map/pallas_call | solution.py:365
  16.6 1.1 %shard_map.78 = (f32[3,128,16,128]{3,2,1,0:T(8,128)S(1)}, f32[16,16,128]{2,1,0:T(8,128)S(1)}) custom-call(f32[3,128,16,128]{3,2,1,0:T(8,128)S(1)} %get-tuple-element.21.conv_in, bf16[3,8,2048]{2,1,0:T(8,128)(2,1)} %collective-permute-done.halo, f32[3,16,16,128]{3,2,1,0:T(8,128)S(1)} %get-tuple-element.22.table, ...), custom_call_target="tpu_custom_call", output_to_operand_aliasing={{0}: (0, {})} | custom-call | bytes 4194304 | tf_op jit(solution)/shard_map/pallas_call | solution.py:365
  17.7 3.0 %collective-permute-start.1 = (f32[16,16,128]{2,1,0:T(8,128)S(1)}, f32[16,16,128]{2,1,0:T(8,128)S(1)}, u32[]{:S(2)}, u32[]{:S(2)}) collective-permute-start(f32[16,16,128]{2,1,0:T(8,128)S(1)} %get-tuple-element.25), channel_id=1, source_target_pairs={{0,8},{4,12},{8,16},{12,20},{16,24},{20,28},{1,9},{5,13},{9,17},{1... | collective-permute-start | bytes 393224 | tf_op jit(solution)/shard_map/ppermute | solution.py:380
  20.7 2.5 %collective-permute-done.1 = f32[16,16,128]{2,1,0:T(8,128)S(1)} collective-permute-done((f32[16,16,128]{2,1,0:T(8,128)S(1)}, f32[16,16,128]{2,1,0:T(8,128)S(1)}, u32[]{:S(2)}, u32[]{:S(2)}) %collective-permute-start.1) | collective-permute-done | bytes 131104 | tf_op jit(solution)/shard_map/ppermute | solution.py:380
  23.9 6.0 %collective-permute-start.2 = (f32[16,16,128]{2,1,0:T(8,128)}, f32[16,16,128]{2,1,0:T(8,128)}, u32[]{:S(2)}, u32[]{:S(2)}) collective-permute-start(f32[16,16,128]{2,1,0:T(8,128)} %fusion), channel_id=1, source_target_pairs={{0,16},{4,20},{8,24},{12,28},{1,17},{5,21},{9,25},{13,29},{2,18},{... | collective-permute-start | bytes 393224 | tf_op jit(solution)/shard_map/ppermute | solution.py:380
  29.9 2.2 %collective-permute-done.2 = f32[16,16,128]{2,1,0:T(8,128)} collective-permute-done((f32[16,16,128]{2,1,0:T(8,128)}, f32[16,16,128]{2,1,0:T(8,128)}, u32[]{:S(2)}, u32[]{:S(2)}) %collective-permute-start.2) | collective-permute-done | bytes 131104 | tf_op jit(solution)/shard_map/ppermute | solution.py:380
  32.1 1.1 %fusion.3 = (f32[16,16,128]{2,1,0:T(8,128)S(1)}, f32[16,16,128]{2,1,0:T(8,128)S(1)}) fusion(f32[16,16,128]{2,1,0:T(8,128)} %copy-done.9, pred[]{:T(512)S(6)} %gt.3, f32[3,16,16,128]{3,2,1,0:T(8,128)S(1)} %get-tuple-element.22.table, f32[16,16,128]{2,1,0:T(8,128)} %copy-done.15, f32[16,16,128]{2,1,0:T(8,128)} %collective-permute-done.2), kind=kLoop, calls=%fused_computation.8 | loop fusion | flops 196608 | bytes 786433 | tf_op jit(solution)/shard_map/jit(_where)/select_n | solution.py:436
  33.2 1.6 %collective-permute-start.3 = (f32[16,16,128]{2,1,0:T(8,128)S(1)}, f32[16,16,128]{2,1,0:T(8,128)S(1)}, u32[]{:S(2)}, u32[]{:S(2)}) collective-permute-start(f32[16,16,128]{2,1,0:T(8,128)S(1)} %get-tuple-element.40), channel_id=1, source_target_pairs={{0,4},{4,0},{8,12},{12,8},{16,20},{20,16},{24,28},{28,24},{1,5},{5... | collective-permute-start | bytes 393224 | tf_op jit(solution)/shard_map/ppermute | solution.py:384
  34.8 2.4 %shard_map.79.local = f32[128,16,128]{2,1,0:T(8,128)S(1)} custom-call(f32[3,128,16,128]{3,2,1,0:T(8,128)S(1)} %get-tuple-element.26.conv, f32[3,16,16,128]{3,2,1,0:T(8,128)S(1)} %get-tuple-element.22.table), custom_call_target="tpu_custom_call" | custom-call | flops 1000000000 | bytes 4194304 | tf_op jit(solution)/shard_map/pallas_call | solution.py:365
  37.2 1.0 %collective-permute-done.3.received = f32[16,16,128]{2,1,0:T(8,128)S(1)} collective-permute-done((f32[16,16,128]{2,1,0:T(8,128)S(1)}, f32[16,16,128]{2,1,0:T(8,128)S(1)}, u32[]{:S(2)}, u32[]{:S(2)}) %collective-permute-start.3) | collective-permute-done | bytes 131104 | tf_op jit(solution)/shard_map/ppermute | solution.py:384
  38.2 3.6 %shard_map.80 = (f32[128,16,128]{2,1,0:T(8,128)S(1)}, f32[128,16,128]{2,1,0:T(8,128)S(1)}, f32[2,128]{1,0:T(2,128)S(1)}) custom-call(f32[16,16,128]{2,1,0:T(8,128)S(1)} %get-tuple-element.41.entering, f32[16,16,128]{2,1,0:T(8,128)S(1)} %collective-permute-done.3.received, f32[3,16,16,128]{3,2,1,0:T(8,128)S(1)} %get-tuple-element.22.table, ...), custom_call_target="tpu_custom_call" | custom-call | bytes 4194304 | tf_op jit(solution)/shard_map/pallas_call | solution.py:365
  41.9 1.0 %copy-done.1 = f32[128,16,128]{2,1,0:T(8,128)} copy-done((f32[128,16,128]{2,1,0:T(8,128)}, f32[128,16,128]{2,1,0:T(8,128)S(1)}, u32[]{:S(2)}) %copy-start.1) | copy-done | bytes 1048600
  42.9 1.0 %copy-done.5 = f32[128,16,128]{2,1,0:T(8,128)} copy-done((f32[128,16,128]{2,1,0:T(8,128)}, f32[128,16,128]{2,1,0:T(8,128)S(1)}, u32[]{:S(2)}) %copy-start.5) | copy-done | bytes 1048600
  43.8 5.6 %psum.7.sums = f32[2,128]{1,0:T(2,128)S(1)} all-reduce(f32[2,128]{1,0:T(2,128)S(1)} %get-tuple-element.27), channel_id=1, replica_groups=mesh['ctx'=8,'tp'=4] {'tp'}, use_global_device_ids=true, to_apply=%region_0.1 | all-reduce | flops 256 | bytes 2048 | tf_op jit(solution)/shard_map/psum | solution.py:444
  49.4 1.2 %copy-done.2 = f32[128,16,128]{2,1,0:T(8,128)S(1)} copy-done((f32[128,16,128]{2,1,0:T(8,128)S(1)}, f32[128,16,128]{2,1,0:T(8,128)}, u32[]{:S(2)}) %copy-start.2) | copy-done | bytes 1048600
  50.7 1.2 %copy-done.6 = f32[128,16,128]{2,1,0:T(8,128)S(1)} copy-done((f32[128,16,128]{2,1,0:T(8,128)S(1)}, f32[128,16,128]{2,1,0:T(8,128)}, u32[]{:S(2)}) %copy-start.6) | copy-done | bytes 1048600
  51.9 3.6 %shard_map.81 = (f32[128,16,128]{2,1,0:T(8,128)S(1)}, f32[128,16,128]{2,1,0:T(8,128)S(1)}, f32[16,16,128]{2,1,0:T(8,128)S(1)}, f32[128,128]{1,0:T(8,128)S(1)}) custom-call(f32[2,128]{1,0:T(2,128)S(1)} %psum.7.sums, f32[3,16,16,128]{3,2,1,0:T(8,128)S(1)} %get-tuple-element.22.table, f32[3,128,16,128]{3,2,1,0:T(8,128)} %copy-done, ...), custom_call_target="tpu_custom_call" | custom-call | bytes 4194304 | tf_op jit(solution)/shard_map/pallas_call | solution.py:365
  55.5 1.3 %collective-permute-start.4 = (f32[16,16,128]{2,1,0:T(8,128)S(1)}, f32[16,16,128]{2,1,0:T(8,128)S(1)}, u32[]{:S(2)}, u32[]{:S(2)}) collective-permute-start(f32[16,16,128]{2,1,0:T(8,128)S(1)} %get-tuple-element.34.own), channel_id=1, source_target_pairs={{8,0},{12,4},{16,8},{20,12},{24,16},{28,20},{9,1},{13,5},{17,9},{2... | collective-permute-start | bytes 393224 | tf_op jit(solution)/shard_map/ppermute | solution.py:380
  56.8 7.2 %collective-permute-done.4.near = f32[16,16,128]{2,1,0:T(8,128)S(1)} collective-permute-done((f32[16,16,128]{2,1,0:T(8,128)S(1)}, f32[16,16,128]{2,1,0:T(8,128)S(1)}, u32[]{:S(2)}, u32[]{:S(2)}) %collective-permute-start.4) | collective-permute-done | bytes 131104 | tf_op jit(solution)/shard_map/ppermute | solution.py:380
  64.0 1.3 %collective-permute-start.5 = (f32[16,16,128]{2,1,0:T(8,128)S(1)}, f32[16,16,128]{2,1,0:T(8,128)S(1)}, u32[]{:S(2)}, u32[]{:S(2)}) collective-permute-start(f32[16,16,128]{2,1,0:T(8,128)S(1)} %fusion.4), channel_id=1, source_target_pairs={{16,0},{20,4},{24,8},{28,12},{17,1},{21,5},{25,9},{29,13},{18,2},{... | collective-permute-start | bytes 393224 | tf_op jit(solution)/shard_map/ppermute | solution.py:380
  65.3 5.6 %shard_map.82 = (bf16[128,2048]{1,0:T(8,128)(2,1)}, f32[128,16,128]{2,1,0:T(8,128)S(1)}, f32[128,16,128]{2,1,0:T(8,128)S(1)}, f32[4,8,16,128]{3,2,1,0:T(8,128)S(1)}) custom-call(f32[128,128]{1,0:T(8,128)S(1)} %get-tuple-element.30.inv, f32[3,16,16,128]{3,2,1,0:T(8,128)S(1)} %get-tuple-element.22.table, f32[16,128]{1,0:T(8,128)S(1)} %bitcast.27, ...), custom_call_target="tpu_custom_call" | custom-call | flops 1000000000 | bytes 4194304 | tf_op jit(solution)/shard_map/pallas_call | solution.py:365
  71.0 1.3 %collective-permute-start.7 = (f32[4,8,16,128]{3,2,1,0:T(8,128)S(1)}, f32[4,8,16,128]{3,2,1,0:T(8,128)S(1)}, u32[]{:S(2)}, u32[]{:S(2)}) collective-permute-start(f32[4,8,16,128]{3,2,1,0:T(8,128)S(1)} %get-tuple-element.39), channel_id=1, source_target_pairs={{4,0},{8,4},{12,8},{16,12},{20,16},{24,20},{28,24},{5,1},{9,5},{13... | collective-permute-start | bytes 786440 | tf_op jit(solution)/shard_map/ppermute | solution.py:380
  72.2 2.1 %collective-permute-done.5 = f32[16,16,128]{2,1,0:T(8,128)S(1)} collective-permute-done((f32[16,16,128]{2,1,0:T(8,128)S(1)}, f32[16,16,128]{2,1,0:T(8,128)S(1)}, u32[]{:S(2)}, u32[]{:S(2)}) %collective-permute-start.5) | collective-permute-done | bytes 131104 | tf_op jit(solution)/shard_map/ppermute | solution.py:380
  74.5 1.0 %collective-permute-start.6 = (f32[24,16,128]{2,1,0:T(8,128)S(1)}, f32[24,16,128]{2,1,0:T(8,128)S(1)}, u32[]{:S(2)}, u32[]{:S(2)}) collective-permute-start(f32[24,16,128]{2,1,0:T(8,128)S(1)} %get-tuple-element.36), channel_id=1, source_target_pairs={{0,4},{4,0},{8,12},{12,8},{16,20},{20,16},{24,28},{28,24},{1,5},{5... | collective-permute-start | bytes 589832 | tf_op jit(solution)/shard_map/ppermute | solution.py:384
  75.5 6.6 %collective-permute-done.7.head = f32[4,8,16,128]{3,2,1,0:T(8,128)S(1)} collective-permute-done((f32[4,8,16,128]{3,2,1,0:T(8,128)S(1)}, f32[4,8,16,128]{3,2,1,0:T(8,128)S(1)}, u32[]{:S(2)}, u32[]{:S(2)}) %collective-permute-start.7) | collective-permute-done | bytes 262176 | tf_op jit(solution)/shard_map/ppermute | solution.py:380
  82.1 2.5 %collective-permute-done.6.received = f32[24,16,128]{2,1,0:T(8,128)S(1)} collective-permute-done((f32[24,16,128]{2,1,0:T(8,128)S(1)}, f32[24,16,128]{2,1,0:T(8,128)S(1)}, u32[]{:S(2)}, u32[]{:S(2)}) %collective-permute-start.6) | collective-permute-done | bytes 196640 | tf_op jit(solution)/shard_map/ppermute | solution.py:384
  84.6 6.4 %shard_map.84 = bf16[3,128,2048]{2,1,0:T(8,128)(2,1)} custom-call(f32[16,16,128]{2,1,0:T(8,128)S(1)} %get-tuple-element.35.entering, f32[24,16,128]{2,1,0:T(8,128)S(1)} %collective-permute-done.6.received, f32[3,16,16,128]{3,2,1,0:T(8,128)S(1)} %get-tuple-element.22.table, f32[3,7,16,128]{3,2,1,0:T(8,128)S(1)} %copy-done.8, f32[3,128,16,128]{3,2,1,0:T(8,128)} %copy-done, ...), custom_call_target="tpu_custom_call" | custom-call | bytes 4194304 | tf_op jit(solution)/shard_map/pallas_call | solution.py:365
  (31 shorter events, 2.7 us)
Async XLA Ops:
  2.2 14.4 %collective-permute-start = (bf16[3,8,2048]{2,1,0:T(8,128)(2,1)}, bf16[3,8,2048]{2,1,0:T(8,128)(2,1)}, u32[]{:S(2)}, u32[]{:S(2)}) collective-permute-start(bf16[3,8,2048]{2,1,0:T(8,128)(2,1)} %slice.6), channel_id=1, source_target_pairs={{0,4},{4,8},{8,12},{12,16},{16,20},{20,24},{24,28},{1,5},{5,9},{9,... | collective-permute-start | bytes 294920 | tf_op jit(solution)/shard_map/ppermute | solution.py:380
  9.1 1.4 %copy-start.4 = (bf16[3,128,2048]{2,1,0:T(8,128)(2,1)S(1)}, bf16[3,128,2048]{2,1,0:T(8,128)(2,1)}, u32[]{:S(2)}) copy-start(bf16[3,128,2048]{2,1,0:T(8,128)(2,1)} %x.1) | copy-start | bytes 4718596
  10.5 0.9 copy-start.11
  11.4 0.9 copy-start.12
  12.3 0.9 copy-start.13
  16.6 1.1 %copy-start.7 = (f32[3,7,16,128]{3,2,1,0:T(8,128)}, f32[3,7,16,128]{3,2,1,0:T(8,128)S(1)}, u32[]{:S(2)}) copy-start(f32[3,7,16,128]{3,2,1,0:T(8,128)S(1)} %get-tuple-element.23.taps) | copy-start | bytes 516100
  17.7 5.5 %copy-start.9 = (f32[16,16,128]{2,1,0:T(8,128)}, f32[16,16,128]{2,1,0:T(8,128)S(1)}, u32[]{:S(2)}) copy-start(f32[16,16,128]{2,1,0:T(8,128)S(1)} %get-tuple-element.25) | copy-start | bytes 393220
  17.7 20.5 %copy-start = (f32[3,128,16,128]{3,2,1,0:T(8,128)}, f32[3,128,16,128]{3,2,1,0:T(8,128)S(1)}, u32[]{:S(2)}) copy-start(f32[3,128,16,128]{3,2,1,0:T(8,128)S(1)} %get-tuple-element.26.conv) | copy-start | bytes 9437188
  17.7 20.5 %copy-start.14 = (f32[2048]{0:T(1024)S(1)}, f32[2048]{0:T(1024)}, u32[]{:S(2)}) copy-start(f32[2048]{0:T(1024)} %param.10) | copy-start | bytes 24580
  17.7 5.5 %collective-permute-start.1 = (f32[16,16,128]{2,1,0:T(8,128)S(1)}, f32[16,16,128]{2,1,0:T(8,128)S(1)}, u32[]{:S(2)}, u32[]{:S(2)}) collective-permute-start(f32[16,16,128]{2,1,0:T(8,128)S(1)} %get-tuple-element.25), channel_id=1, source_target_pairs={{0,8},{4,12},{8,16},{12,20},{16,24},{20,28},{1,9},{5,13},{9,17},{1... | collective-permute-start | bytes 393224 | tf_op jit(solution)/shard_map/ppermute | solution.py:380
  23.2 0.7 copy-start.15
  23.9 8.2 %collective-permute-start.2 = (f32[16,16,128]{2,1,0:T(8,128)}, f32[16,16,128]{2,1,0:T(8,128)}, u32[]{:S(2)}, u32[]{:S(2)}) collective-permute-start(f32[16,16,128]{2,1,0:T(8,128)} %fusion), channel_id=1, source_target_pairs={{0,16},{4,20},{8,24},{12,28},{1,17},{5,21},{9,25},{13,29},{2,18},{... | collective-permute-start | bytes 393224 | tf_op jit(solution)/shard_map/ppermute | solution.py:380
  29.9 8.3 %copy-start.10 = (bf16[128,2048]{1,0:T(8,128)(2,1)S(1)}, bf16[128,2048]{1,0:T(8,128)(2,1)}, u32[]{:S(2)}) copy-start(bf16[128,2048]{1,0:T(8,128)(2,1)} %grad.1) | copy-start | bytes 1572868
  33.2 5.0 %collective-permute-start.3 = (f32[16,16,128]{2,1,0:T(8,128)S(1)}, f32[16,16,128]{2,1,0:T(8,128)S(1)}, u32[]{:S(2)}, u32[]{:S(2)}) collective-permute-start(f32[16,16,128]{2,1,0:T(8,128)S(1)} %get-tuple-element.40), channel_id=1, source_target_pairs={{0,4},{4,0},{8,12},{12,8},{16,20},{20,16},{24,28},{28,24},{1,5},{5... | collective-permute-start | bytes 393224 | tf_op jit(solution)/shard_map/ppermute | solution.py:384
  41.9 1.0 %copy-start.1 = (f32[128,16,128]{2,1,0:T(8,128)}, f32[128,16,128]{2,1,0:T(8,128)S(1)}, u32[]{:S(2)}) copy-start(f32[128,16,128]{2,1,0:T(8,128)S(1)} %get-tuple-element.28.long_conv) | copy-start | bytes 3145732
  42.9 1.0 %copy-start.5 = (f32[128,16,128]{2,1,0:T(8,128)}, f32[128,16,128]{2,1,0:T(8,128)S(1)}, u32[]{:S(2)}) copy-start(f32[128,16,128]{2,1,0:T(8,128)S(1)} %get-tuple-element.29.scaled) | copy-start | bytes 3145732
  49.4 1.2 %copy-start.2 = (f32[128,16,128]{2,1,0:T(8,128)S(1)}, f32[128,16,128]{2,1,0:T(8,128)}, u32[]{:S(2)}) copy-start(f32[128,16,128]{2,1,0:T(8,128)} %copy-done.1) | copy-start | bytes 3145732
  50.7 1.2 %copy-start.6 = (f32[128,16,128]{2,1,0:T(8,128)S(1)}, f32[128,16,128]{2,1,0:T(8,128)}, u32[]{:S(2)}) copy-start(f32[128,16,128]{2,1,0:T(8,128)} %copy-done.5) | copy-start | bytes 3145732
  51.9 13.4 %copy-start.3 = (f32[128,16,128]{2,1,0:T(8,128)S(1)}, f32[128,16,128]{2,1,0:T(8,128)}, u32[]{:S(2)}) copy-start(f32[128,16,128]{2,1,0:T(8,128)} %copy-done.1) | copy-start | bytes 3145732
  55.5 8.5 %collective-permute-start.4 = (f32[16,16,128]{2,1,0:T(8,128)S(1)}, f32[16,16,128]{2,1,0:T(8,128)S(1)}, u32[]{:S(2)}, u32[]{:S(2)}) collective-permute-start(f32[16,16,128]{2,1,0:T(8,128)S(1)} %get-tuple-element.34.own), channel_id=1, source_target_pairs={{8,0},{12,4},{16,8},{20,12},{24,16},{28,20},{9,1},{13,5},{17,9},{2... | collective-permute-start | bytes 393224 | tf_op jit(solution)/shard_map/ppermute | solution.py:380
  64.0 10.3 %collective-permute-start.5 = (f32[16,16,128]{2,1,0:T(8,128)S(1)}, f32[16,16,128]{2,1,0:T(8,128)S(1)}, u32[]{:S(2)}, u32[]{:S(2)}) collective-permute-start(f32[16,16,128]{2,1,0:T(8,128)S(1)} %fusion.4), channel_id=1, source_target_pairs={{16,0},{20,4},{24,8},{28,12},{17,1},{21,5},{25,9},{29,13},{18,2},{... | collective-permute-start | bytes 393224 | tf_op jit(solution)/shard_map/ppermute | solution.py:380
  65.3 19.3 %copy-start.8 = (f32[3,7,16,128]{3,2,1,0:T(8,128)S(1)}, f32[3,7,16,128]{3,2,1,0:T(8,128)}, u32[]{:S(2)}) copy-start(f32[3,7,16,128]{3,2,1,0:T(8,128)} %copy-done.7) | copy-start | bytes 516100
  71.0 11.1 %collective-permute-start.7 = (f32[4,8,16,128]{3,2,1,0:T(8,128)S(1)}, f32[4,8,16,128]{3,2,1,0:T(8,128)S(1)}, u32[]{:S(2)}, u32[]{:S(2)}) collective-permute-start(f32[4,8,16,128]{3,2,1,0:T(8,128)S(1)} %get-tuple-element.39), channel_id=1, source_target_pairs={{4,0},{8,4},{12,8},{16,12},{20,16},{24,20},{28,24},{5,1},{9,5},{13... | collective-permute-start | bytes 786440 | tf_op jit(solution)/shard_map/ppermute | solution.py:380
  74.5 10.1 %collective-permute-start.6 = (f32[24,16,128]{2,1,0:T(8,128)S(1)}, f32[24,16,128]{2,1,0:T(8,128)S(1)}, u32[]{:S(2)}, u32[]{:S(2)}) collective-permute-start(f32[24,16,128]{2,1,0:T(8,128)S(1)} %get-tuple-element.36), channel_id=1, source_target_pairs={{0,4},{4,0},{8,12},{12,8},{16,20},{20,16},{24,28},{28,24},{1,5},{5... | collective-permute-start | bytes 589832 | tf_op jit(solution)/shard_map/ppermute | solution.py:384

commit v2 on v1

v2 whole, which is shorter than its diff:
```python
import functools

import jax
import jax.numpy as jnp
from jax import lax
from jax.experimental import pallas as pl
from jax.experimental.pallas import tpu as pltpu
from jax.sharding import PartitionSpec as P

GROUP = 16
LANES = 128
SUB = 8
EPSILON = 1e-05
VMEM_LIMIT = 16 * 1024 * 1024


def halves(lane_blocks):
    return [pl.ds(SUB * h, SUB) for h in range(lane_blocks // SUB)]


def total(terms):
    terms = list(terms)
    while len(terms) > 1:
        paired = [terms[i] + terms[i + 1] for i in range(0, len(terms) - 1, 2)]
        terms = paired + ([terms[-1]] if len(terms) % 2 else [])
    return terms[0]


def spread_rows(source, target, first, pitch, lane_blocks):
    rows = source.shape[0]
    for lb in range(lane_blocks):
        tile = source[:, lb * LANES : (lb + 1) * LANES]
        target[pl.ds(first + lb * pitch, rows), :] = tile.astype(jnp.float32)


def row_at(ref, first, pitch, half, place):
    return ref[pl.ds(first + half * SUB * pitch + place, SUB, stride=pitch), :]


def tail_kernel(x, tail, edge, sem):
    rows = x.shape[1]
    move = pltpu.make_async_copy(x.at[:, pl.ds(rows - 2 * SUB, 2 * SUB), :], edge, sem)
    move.start()
    move.wait()
    tail[...] = edge[:, SUB:, :]


def prepare_kernel(
    x_far, filt_far, rate_far, res_far, pair_far, taps_far, first_rows, table, taps, ends,
    x, filt, rate, res, pair, xs, ps, sems,
):
    rows, channels = x.shape[1:]
    modes = rate.shape[0]
    lane_blocks = channels // LANES
    tap_count = taps.shape[1]
    pitch = rows + SUB
    fetches = [
        pltpu.make_async_copy(source, target, sems.at[i])
        for i, (source, target) in enumerate(
            [(filt_far, filt), (rate_far, rate), (res_far, res)]
            + [(x_far.at[1 + s], x.at[s]) for s in range(2)]
        )
    ]
    for fetch in fetches:
        fetch.start()
    spread = (
        lax.broadcasted_iota(jnp.int32, (channels // GROUP, channels), 1) // GROUP
        == lax.broadcasted_iota(jnp.int32, (channels // GROUP, channels), 0)
    ).astype(jnp.bfloat16)
    fetches[0].wait()
    for s in range(3):
        weights = jnp.dot(filt[s], spread, preferred_element_type=jnp.float32)
        for lb in range(lane_blocks):
            ps[pl.ds(lb * SUB, tap_count), :] = weights[:, lb * LANES : (lb + 1) * LANES]
        for h, half in enumerate(halves(lane_blocks)):
            for i in range(tap_count):
                taps[s, i, half, :] = row_at(ps, 0, SUB, h, i)
    stores = [pltpu.make_async_copy(taps, taps_far, sems.at[5])]
    stores[0].start()
    fetches[1].wait()
    fetches[2].wait()
    spread_rows(rate, ps, 0, modes, lane_blocks)
    spread_rows(res, ps, lane_blocks * modes, modes, lane_blocks)
    for h, half in enumerate(halves(lane_blocks)):
        for m in range(modes):
            r = row_at(ps, 0, modes, h, m)
            c = row_at(ps, lane_blocks * modes, modes, h, m)
            table[0, m, half, :] = jnp.exp(-r)
            table[1, m, half, :] = c * jnp.sqrt(2.0 * r)
            table[2, m, half, :] = r
    zero = jnp.zeros((SUB, LANES), jnp.float32)
    for s in range(2):
        fetches[3 + s].wait()
        spread_rows(x.at[s], xs, s * lane_blocks * pitch, pitch, lane_blocks)
    for h, half in enumerate(halves(lane_blocks)):
        for s in range(2):
            w = [taps[1 + s, i, half, :] for i in range(tap_count)]

            def body(block, window):
                window = list(window)
                for k in range(SUB):
                    t = block * SUB + k
                    window.append(row_at(xs, s * lane_blocks * pitch, pitch, h, t))
                    pair[s, t, half, :] = total(w[i] * window[-1 - i] for i in range(tap_count))
                return tuple(window[-(tap_count - 1) :])

            lax.fori_loop(0, rows // SUB, body, (zero,) * (tap_count - 1))
            stores.append(
                pltpu.make_async_copy(
                    pair.at[s, :, half, :], pair_far.at[s, :, half, :], sems.at[6 + 2 * h + s]
                )
            )
            stores[-1].start()
            first_rows[s, :, half, :] = pair[s, :SUB, half, :]
        decay = [table[0, m, half, :] for m in range(modes)]

        def step(t, state):
            u = pair[0, t, half, :] * pair[1, t, half, :]
            return tuple(decay[m] * state[m] + u for m in range(modes))

        state = (zero,) * modes
        for t in range(tap_count - 1, SUB):
            state = step(t, state)

        def block_step(block, state):
            for k in range(SUB):
                state = step(block * SUB + k, state)
            return state

        state = lax.fori_loop(1, rows // SUB, block_step, state)
        for m in range(modes):
            ends[m, half, :] = state[m]
    for store in stores:
        store.wait()


def head_kernel(rows, first_in, halo, table, taps, ends, first_rows, state_out, hs):
    modes, lane_blocks = ends.shape[:2]
    reach = taps.shape[1] - 1
    for s in range(2):
        spread_rows(halo.at[1 + s], hs, s * lane_blocks * SUB, SUB, lane_blocks)
    for h, half in enumerate(halves(lane_blocks)):
        heads = []
        for s in range(2):
            w = [taps[1 + s, i, half, :] for i in range(reach + 1)]
            before = [row_at(hs, s * lane_blocks * SUB, SUB, h, j) for j in range(SUB)]
            head = []
            for t in range(SUB):
                row = first_in[s, t, half, :]
                if t < reach:
                    row = row + total(w[i] * before[SUB + t - i] for i in range(t + 1, reach + 1))
                    head.append(row)
                first_rows[s, t, half, :] = row
            heads.append(head)
        product = [heads[0][t] * heads[1][t] for t in range(reach)]
        for m in range(modes):
            decay = table[0, m, half, :]
            state = product[0]
            for t in range(1, reach):
                state = decay * state + product[t]
            fade = jnp.exp(table[2, m, half, :] * -float(rows - reach))
            state_out[m, half, :] = ends[m, half, :] + fade * state


def query_kernel(x_far, halo, taps, gain, grad_far, query, scaled, x, grad, xs, gs, sems):
    rows, channels = x.shape
    lane_blocks = channels // LANES
    tap_count = taps.shape[1]
    pitch = rows + SUB
    fetches = [
        pltpu.make_async_copy(x_far.at[0], x, sems.at[0]),
        pltpu.make_async_copy(grad_far, grad, sems.at[1]),
    ]
    for fetch in fetches:
        fetch.start()
    spread_rows(halo.at[0], xs, 0, pitch, lane_blocks)
    fetches[0].wait()
    spread_rows(x, xs, SUB, pitch, lane_blocks)
    fetches[1].wait()
    spread_rows(grad, gs, 0, pitch, lane_blocks)
    for h, half in enumerate(halves(lane_blocks)):
        w = [taps[0, i, half, :] for i in range(tap_count)]
        g = gain[half, :]

        def body(block, window):
            window = list(window)
            for k in range(SUB):
                t = block * SUB + k
                window.append(row_at(xs, SUB, pitch, h, t))
                query[t, half, :] = total(w[i] * window[-1 - i] for i in range(tap_count))
                scaled[t, half, :] = g * row_at(gs, 0, pitch, h, t)
            return tuple(window[-(tap_count - 1) :])

        lax.fori_loop(
            0, rows // SUB, body, tuple(row_at(xs, 0, pitch, h, SUB + 1 - tap_count + j) for j in range(tap_count - 1))
        )


def local_kernel(pair, first_rows, table, local):
    rows = local.shape[0]
    modes, lane_blocks = table.shape[1:3]
    zero = jnp.zeros((SUB, LANES), jnp.float32)
    for half in halves(lane_blocks):
        decay = [table[0, m, half, :] for m in range(modes)]
        scale = [table[1, m, half, :] for m in range(modes)]

        def block_step(source, block, state):
            for k in range(SUB):
                t = block * SUB + k
                u = source[0, t, half, :] * source[1, t, half, :]
                state = tuple(decay[m] * state[m] + u for m in range(modes))
                local[t, half, :] = total(scale[m] * state[m] for m in range(modes))
            return state

        state = block_step(first_rows, 0, (zero,) * modes)
        lax.fori_loop(1, rows // SUB, functools.partial(block_step, pair), state)


def carry_kernel(entering, received, table, query, local, scaled, long_conv, sums, sq, cr):
    rows = local.shape[0]
    modes, lane_blocks = table.shape[1:3]
    for h, half in enumerate(halves(lane_blocks)):
        decay = [table[0, m, half, :] for m in range(modes)]
        start = []
        for m in range(modes):
            fade = jnp.exp(table[2, m, half, :] * -float(rows))
            incoming = fade * entering[m, half, :] + received[m, half, :]
            start.append(table[1, m, half, :] * decay[m] * incoming)

        def block_step(block, state):
            for k in range(SUB):
                t = block * SUB + k
                row = local[t, half, :] + total(state)
                state = tuple(decay[m] * state[m] for m in range(modes))
                long_conv[t, half, :] = row
                modulated = query[t, half, :] * row
                place = pl.ds(pl.multiple_of(t * SUB, SUB), SUB)
                square = modulated * modulated
                cross = scaled[t, half, :] * modulated
                sq[place, :] = square if h == 0 else sq[place, :] + square
                cr[place, :] = cross if h == 0 else cr[place, :] + cross
            return state

        lax.fori_loop(0, rows // SUB, block_step, tuple(start))
    for which, ref in enumerate((sq, cr)):
        blocks = []
        for b in range(rows // SUB):
            blocks.append(
                total(
                    ref[pl.ds(b * SUB * SUB + s, SUB, stride=SUB), :] for s in range(SUB)
                )
            )
        by_row = jnp.concatenate(blocks, axis=0)
        sums[which : which + 1, :] = jnp.sum(jnp.transpose(by_row), axis=0, keepdims=True)


def mixed_kernel(width, sums, table, query, long_conv, scaled, mixed, long_grad, state_out, inv, inv_s, off_s):
    rows = long_conv.shape[0]
    modes, lane_blocks = table.shape[1:3]
    zero = jnp.zeros((SUB, LANES), jnp.float32)
    inverse = lax.rsqrt(sums[0:1, :] / width + EPSILON)
    offset = inverse * inverse * inverse * sums[1:2, :] / width
    inv_s[...] = jnp.transpose(jnp.broadcast_to(inverse, (LANES, rows)))
    off_s[...] = jnp.transpose(jnp.broadcast_to(offset, (LANES, rows)))
    inv[...] = inv_s[...]
    blocks = rows // SUB
    for half in halves(lane_blocks):
        decay = [table[0, m, half, :] for m in range(modes)]

        def block_step(block, state):
            for k in range(SUB):
                t = (blocks - 1 - block) * SUB + SUB - 1 - k
                q = query[t, half, :]
                modulated = q * long_conv[t, half, :]
                mix = (
                    inv_s[pl.ds(t, 1), :] * scaled[t, half, :] - off_s[pl.ds(t, 1), :] * modulated
                )
                mixed[t, half, :] = mix
                lg = mix * q
                long_grad[t, half, :] = lg
                state = tuple(decay[m] * state[m] + lg for m in range(modes))
            return state

        state = lax.fori_loop(0, blocks, block_step, (zero,) * modes)
        for m in range(modes):
            state_out[m, half, :] = state[m]


def back_kernel(table, first_rows, long_conv, mixed, long_grad, local, head):
    rows = long_conv.shape[0]
    modes, lane_blocks = table.shape[1:3]
    reach = head.shape[1]
    blocks = rows // SUB
    zero = jnp.zeros((SUB, LANES), jnp.float32)
    for half in halves(lane_blocks):
        decay = [table[0, m, half, :] for m in range(modes)]
        scale = [table[1, m, half, :] for m in range(modes)]

        def block_step(block, state):
            for k in range(SUB):
                t = (blocks - 1 - block) * SUB + SUB - 1 - k
                lg = long_grad[t, half, :]
                state = tuple(decay[m] * state[m] + lg for m in range(modes))
                local[t, half, :] = total(scale[m] * state[m] for m in range(modes))
            return state

        lax.fori_loop(0, blocks, block_step, (zero,) * modes)
    for t in range(reach):
        head[0, t] = (mixed[t] * long_conv[t]).astype(head.dtype)
        head[1, t] = local[t].astype(head.dtype)
        head[2, t] = first_rows[1, t].astype(head.dtype)
        head[3, t] = first_rows[0, t].astype(head.dtype)


def output_kernel(inv, taps, gain, query, long_conv, mixed, output, finished, last, os, qs):
    rows = long_conv.shape[0]
    lane_blocks = taps.shape[2]
    tap_count = taps.shape[1]
    pitch = rows + SUB
    blocks = rows // SUB
    zero = jnp.zeros((SUB, LANES), jnp.float32)
    for h, half in enumerate(halves(lane_blocks)):
        g = gain[half, :]
        w = [taps[0, i, half, :] for i in range(tap_count)]

        def out_step(block, window):
            window = list(window)
            for k in range(SUB):
                t = (blocks - 1 - block) * SUB + SUB - 1 - k
                long_row = long_conv[t, half, :]
                window.insert(0, mixed[t, half, :] * long_row)
                row = g * (query[t, half, :] * long_row) * inv[pl.ds(t, 1), :]
                os[pl.ds(h * SUB * pitch + t, SUB, stride=pitch), :] = row
                qs[pl.ds(h * SUB * pitch + t, SUB, stride=pitch), :] = total(
                    w[i] * window[i] for i in range(tap_count)
                )
            return tuple(window[: tap_count - 1])

        lax.fori_loop(0, blocks, out_step, (zero,) * (tap_count - 1))
    for lb in range(lane_blocks):
        columns = slice(lb * LANES, (lb + 1) * LANES)
        output[:, columns] = os[pl.ds(lb * pitch, rows), :].astype(output.dtype)
        finished[:, columns] = qs[pl.ds(lb * pitch, rows), :].astype(finished.dtype)
        last[pl.ds(lb * SUB, SUB), :] = qs[pl.ds(lb * pitch + rows - SUB, SUB), :]


def far_rows(table, half, state, rows, reach, fade_first):
    modes = table.shape[1]
    at = [
        table[1, m, half, :]
        * state[m]
        * jnp.exp(table[2, m, half, :] * -float(rows - reach + 1 + fade_first))
        for m in range(modes)
    ]
    found = [None] * reach
    for i in reversed(range(reach)):
        found[i] = total(at)
        if i:
            at = [at[m] * table[0, m, half, :] for m in range(modes)]
    return found


def turn_kernel(rows, reach, lower, near, beyond, table, own, entering, message):
    modes, lane_blocks = own.shape[:2]
    is_lower = jnp.full((SUB, LANES), lower[0]) > 0
    for half in halves(lane_blocks):
        state = []
        for m in range(modes):
            step = jnp.exp(table[2, m, half, :] * -float(2 * rows))
            e = near[m, half, :] + step * beyond[m, half, :]
            entering[m, half, :] = e
            message[m, half, :] = jnp.where(is_lower, e, own[m, half, :] + step * e)
            state.append(jnp.where(is_lower, beyond[m, half, :], e))
        added = far_rows(table, half, state, rows, reach, rows)
        for i in range(reach):
            message[modes + i, half, :] = added[i]
        for i in range(reach, SUB):
            message[modes + i, half, :] = jnp.zeros((SUB, LANES), jnp.float32)


def final_kernel(
    entering, received, table, taps, pair, first_rows, local, query, last, head, grads, cg, os, ls, made, edge, sems
):
    rows = local.shape[0]
    modes, lane_blocks = table.shape[1:3]
    tap_count = taps.shape[1]
    reach = tap_count - 1
    pitch = rows + SUB
    blocks = rows // SUB
    kept = rows - 2 * SUB
    moves = [
        pltpu.make_async_copy(
            query.at[pl.ds(0, kept), :], grads.at[0, pl.ds(0, kept), :], sems.at[0]
        )
    ]
    moves[0].start()
    ls[...] = last[...]
    for h, half in enumerate(halves(lane_blocks)):
        decay = [table[0, m, half, :] for m in range(modes)]
        start = []
        for m in range(modes):
            fade = jnp.exp(table[2, m, half, :] * -float(rows))
            incoming = fade * entering[m, half, :] + received[m, half, :]
            start.append(table[1, m, half, :] * decay[m] * incoming)

        def block_step(source, block, state):
            for k in range(SUB):
                t = (blocks - 1 - block) * SUB + SUB - 1 - k
                gated = local[t, half, :] + total(state)
                state = tuple(decay[m] * state[m] for m in range(modes))
                cg[0, t, :, :] = gated * source[1, t, half, :]
                cg[1, t, :, :] = gated * source[0, t, half, :]
            return state

        state = lax.fori_loop(0, blocks - 1, functools.partial(block_step, pair), tuple(start))
        block_step(first_rows, blocks - 1, state)
        own = far_rows(table, half, [entering[m, half, :] for m in range(modes)], rows, reach, 0)
        beyond = [[], [], []]
        for i in range(reach):
            gated = head[1, i, half, :].astype(jnp.float32) + received[modes + i, half, :] + own[i]
            beyond[0].append(head[0, i, half, :].astype(jnp.float32))
            beyond[1].append(gated * head[2, i, half, :].astype(jnp.float32))
            beyond[2].append(gated * head[3, i, half, :].astype(jnp.float32))
        for t in range(SUB - reach, SUB):
            place = pl.ds(h * SUB * SUB + t, SUB, stride=SUB)
            ls[place, :] += total(
                taps[0, i, half, :] * beyond[0][t + i - SUB] for i in range(SUB - t, tap_count)
            )
        for s in range(1, 3):
            w = [taps[s, i, half, :] for i in range(tap_count)]

            def conv_step(block, window):
                window = list(window)
                for k in range(SUB):
                    t = (blocks - 1 - block) * SUB + SUB - 1 - k
                    window.insert(0, cg[s - 1, t, :, :])
                    os[pl.ds(t, SUB, stride=pitch), :] = total(
                        w[i] * window[i] for i in range(tap_count)
                    )
                return tuple(window[:reach])

            lax.fori_loop(0, blocks, conv_step, tuple(beyond[s]))
            for lb in range(SUB):
                first = (h * SUB + lb) * LANES
                made[s - 1, :, first : first + LANES] = os[pl.ds(lb * pitch, rows), :].astype(made.dtype)
            columns = pl.ds(h * SUB * LANES, SUB * LANES)
            moves.append(
                pltpu.make_async_copy(
                    made.at[s - 1, :, columns], grads.at[s, :, columns], sems.at[len(moves)]
                )
            )
            moves[-1].start()
    for lb in range(lane_blocks):
        columns = slice(lb * LANES, (lb + 1) * LANES)
        ending = jnp.concatenate(
            [query[kept : kept + SUB, columns].astype(jnp.float32), ls[pl.ds(lb * SUB, SUB), :]], axis=0
        )
        edge[:, columns] = ending.astype(edge.dtype)
    moves.append(
        pltpu.make_async_copy(edge, grads.at[0, pl.ds(kept, 2 * SUB), :], sems.at[len(moves)])
    )
    moves[-1].start()
    for move in moves:
        move.wait()


def kept(*shape, dtype=jnp.float32):
    return pltpu.VMEM(shape, dtype)


def run(kernel, ins, outs, scratch=(), work=0, aliases=None):
    ins = [pltpu.with_memory_space_constraint(a, space) for a, space in ins]
    spaces = [getattr(o, "memory_space", pltpu.VMEM) for o in outs]
    return pl.pallas_call(
        kernel,
        out_shape=outs,
        in_specs=[pl.BlockSpec(memory_space=jax.typeof(a).memory_space) for a in ins],
        out_specs=[pl.BlockSpec(memory_space=space) for space in spaces],
        scratch_shapes=[pltpu.VMEM(s, jnp.float32) if isinstance(s, tuple) else s for s in scratch],
        input_output_aliases=aliases or {},
        compiler_params=pltpu.CompilerParams(vmem_limit_bytes=VMEM_LIMIT),
        cost_estimate=pl.CostEstimate(flops=work, bytes_accessed=4 * 1024 * 1024, transcendentals=0),
    )(*ins)


def shifted(block, distance):
    devices = range(lax.axis_size("ctx"))
    route = [(i, i + distance) for i in devices if i + distance in devices]
    return lax.ppermute(block, "ctx", route)


def swapped(block):
    return lax.ppermute(block, "ctx", [(i, i ^ 1) for i in range(lax.axis_size("ctx"))])


def on_device(streams, short_filter, decay_rate, residue, norm_gain, out_grad):
    rows, channels = streams.shape[1:]
    modes = decay_rate.shape[0]
    lane_blocks = channels // LANES
    tap_count = short_filter.shape[2]
    reach = tap_count - 1
    pitch = rows + SUB
    count = lax.axis_size("ctx")
    row_shape = (rows, lane_blocks, LANES)
    state_shape = (modes, lane_blocks, LANES)
    bf16 = jnp.bfloat16

    def v(*arrays):
        return [(a, pltpu.VMEM) for a in arrays]

    def far(*arrays):
        return [(a, pltpu.HBM) for a in arrays]

    (tail,) = run(
        tail_kernel,
        far(streams),
        [jax.ShapeDtypeStruct((3, SUB, channels), bf16)],
        (pltpu.VMEM((3, 2 * SUB, channels), bf16), pltpu.SemaphoreType.DMA(())),
    )
    halo = shifted(tail, 1)
    gain = norm_gain.reshape(lane_blocks, LANES)
    pair_far, taps_far, first_rows, table, taps, ends = run(
        prepare_kernel,
        far(streams, jnp.swapaxes(short_filter, 1, 2), decay_rate, residue),
        [
            pltpu.HBM((2, *row_shape), jnp.float32),
            pltpu.HBM((3, tap_count, lane_blocks, LANES), jnp.float32),
            kept(2, SUB, lane_blocks, LANES),
            kept(3, *state_shape),
            kept(3, tap_count, lane_blocks, LANES),
            kept(*state_shape),
        ],
        (
            pltpu.VMEM((2, rows, channels), bf16),
            pltpu.VMEM((3, tap_count, channels // GROUP), bf16),
            (modes, channels),
            (modes, channels),
            (2, *row_shape),
            (2 * lane_blocks * pitch, LANES),
            (2 * lane_blocks * modes, LANES),
            pltpu.SemaphoreType.DMA((6 + lane_blocks // 4,)),
        ),
        work=10**9,
    )
    first_rows, state = run(
        functools.partial(head_kernel, rows),
        v(first_rows, halo, table, taps, ends),
        [kept(2, SUB, lane_blocks, LANES), jax.ShapeDtypeStruct(state_shape, jnp.float32)],
        ((2 * lane_blocks * SUB, LANES),),
    )
    rate = table[2]
    lower = (1 - lax.axis_index("ctx") % 2).astype(jnp.int32)

    query, scaled = run(
        query_kernel,
        far(streams) + v(halo, taps, gain) + far(out_grad),
        [kept(*row_shape), kept(*row_shape)],
        (
            pltpu.VMEM((rows, channels), bf16),
            pltpu.VMEM((rows, channels), bf16),
            (lane_blocks * pitch, LANES),
            (lane_blocks * pitch, LANES),
            pltpu.SemaphoreType.DMA((2,)),
        ),
        work=2 * 10**9,
    )
    (local,) = run(
        local_kernel, v(pair_far, first_rows, table), [kept(*row_shape)], work=2 * 10**9
    )
    step = jnp.exp(rate * -float(2 * rows))
    inclusive, entering = state, jnp.zeros_like(state)
    width = 1
    while 2 * width < count:
        got = shifted(inclusive, 2 * width)
        if width == 1:
            got, query, scaled = lax.optimization_barrier((got, query, scaled))
            entering = got
        else:
            if 4 * width >= count:
                got, local = lax.optimization_barrier((got, local))
            entering = entering + jnp.exp(rate * -float(2 * rows * (width - 1))) * got
        inclusive = state + step * entering
        width *= 2
    received = swapped(jnp.where(lower > 0, inclusive, entering))
    long_conv, sums = run(
        carry_kernel,
        v(entering, received, table, query, local, scaled),
        [kept(*row_shape), kept(2, rows)],
        ((rows * SUB, LANES), (rows * SUB, LANES)),
    )
    sums = lax.psum(sums, "tp")
    mixed, long_grad, back, inv = run(
        functools.partial(mixed_kernel, float(channels * lax.axis_size("tp"))),
        v(sums, table, query, long_conv, scaled),
        [
            kept(*row_shape),
            kept(*row_shape),
            jax.ShapeDtypeStruct(state_shape, jnp.float32),
            kept(rows, LANES),
        ],
        ((rows, LANES), (rows, LANES)),
    )

    local_back, head = run(
        back_kernel,
        v(table, first_rows, long_conv, mixed, long_grad),
        [kept(*row_shape), kept(4, reach, lane_blocks, LANES, dtype=bf16)],
        work=2 * 10**9,
    )
    output, finished, last = run(
        output_kernel,
        v(inv, taps_far, gain, query, long_conv, mixed),
        [
            jax.ShapeDtypeStruct((rows, channels), bf16),
            kept(rows, channels, dtype=bf16),
            kept(lane_blocks * SUB, LANES),
        ],
        ((lane_blocks * pitch, LANES), (lane_blocks * pitch, LANES)),
        work=2 * 10**9,
    )
    inclusive, near, beyond = back, jnp.zeros_like(back), jnp.zeros_like(back)
    width = 1
    while 2 * width < count:
        got = shifted(inclusive, -2 * width)
        if width == 1:
            got, head = lax.optimization_barrier((got, head))
            near = got
        else:
            if 4 * width >= count:
                got, head, finished = lax.optimization_barrier((got, shifted(head, -1), finished))
            beyond = beyond + jnp.exp(rate * -float(2 * rows * (width - 2))) * got
        inclusive = back + step * (near + step * beyond if width > 1 else near)
        width *= 2
    entering_back, message = run(
        functools.partial(turn_kernel, rows, reach),
        [(lower[None], pltpu.SMEM)] + v(near, beyond, table, back),
        [kept(*state_shape), jax.ShapeDtypeStruct((modes + SUB, lane_blocks, LANES), jnp.float32)],
    )
    received_back = swapped(message)
    (grads,) = run(
        final_kernel,
        v(entering_back, received_back, table, taps_far, pair_far, first_rows, local_back, finished, last, head),
        [pltpu.HBM((3, rows, channels), bf16)],
        (
            (2, rows, SUB, LANES),
            (SUB * pitch, LANES),
            (lane_blocks * SUB, LANES),
            pltpu.VMEM((2, rows, channels), bf16),
            pltpu.VMEM((2 * SUB, channels), bf16),
            pltpu.SemaphoreType.DMA((2 + lane_blocks // 4,)),
        ),
    )
    return output, grads


def solution(mesh):
    return jax.shard_map(
        on_device,
        mesh=mesh,
        in_specs=(
            P(None, "ctx", "tp"),
            P(None, "tp", None),
            P(None, "tp"),
            P(None, "tp"),
            P("tp"),
            P("ctx", "tp"),
        ),
        out_specs=(P("ctx", "tp"), P(None, "ctx", "tp")),
        check_vma=False,
    )
```

time: 91.7 us -> 70 us (0.76)
  local copies, waits for them, and re-layouts: 11.5 us -> 0.03 us
  Pallas kernels: 26.3 us -> 20.5 us
  other arithmetic: 1.83 us -> 0.13 us
  waiting for transfers between devices: 24 us -> 22.5 us
    unnamed x32 -> x12, local copies, waits for them, and re-layouts: 8.51 us -> 0.03 us
    ppermute x6, waiting for transfers between devices: 20.5 us -> 14.2 us  [shifted(): return lax.ppermute(block, 'ctx', route)]
    pallas_call x8 -> x11, Pallas kernels: 26.3 us -> 20.5 us  [run(): pl.pallas_call(kernel, out_shape=outs, in_specs=[pl.BlockSpec(memory_spac...]
    ppermute x2, waiting for transfers between devices: 3.48 us -> 8.24 us  [swapped(): lax.ppermute(block, 'ctx', [(i, i ^ 1) for i in range(lax.axis_size('ctx'...]
    slice x1 -> x0, local copies, waits for them, and re-layouts: 1.54 us -> none  [on_device(): halo = shifted(streams[:, rows - SUB:, :], 1)]
    reshape x1 -> x0, local copies, waits for them, and re-layouts: 1.47 us -> none  [on_device(): short_filter.reshape(stream_count, lane_blocks, SUB, tap_count)]
    select_n x1, other arithmetic: 1.07 us -> 0.04 us  [on_device(): received = swapped(jnp.where(lower > 0, inclusive, entering))]
  transfers between devices with their start and end apart: 8 -> 8, of which waited for: 7 -> 7; matrix products, arithmetic and copies ran while one was open for 2% -> 0% of each run, Pallas kernels for 13% -> 18%
where the time goes in v2:
time: 70 us; the launch traced here: 69.7 us
  waiting for transfers between devices  22.5 us (32%)
  Pallas kernels  20.5 us (29%)
  starting transfers between devices  20.1 us (29%)
  blocking collectives  5.66 us (8%)
  between operations  0.85 us (1%)
    pallas_call x11, Pallas kernels, run(): pl.pallas_call(kernel, out_shape=outs, in_specs=[pl.BlockSpec(memory_spac...  20.5 us
    ppermute x6, starting transfers between devices, shifted(): return lax.ppermute(block, 'ctx', route)  17.6 us
    ppermute x6, waiting for transfers between devices, shifted(): return lax.ppermute(block, 'ctx', route)  14.2 us
    ppermute x2, waiting for transfers between devices, swapped(): lax.ppermute(block, 'ctx', [(i, i ^ 1) for i in range(lax.axis_size('ctx'...  8.24 us
    psum x1, blocking collectives, on_device(): sums = lax.psum(sums, 'tp')  5.66 us
    ppermute x2, starting transfers between devices, swapped(): lax.ppermute(block, 'ctx', [(i, i ^ 1) for i in range(lax.axis_size('ctx'...  2.53 us
  transfers between devices with their start and end apart: 8, of which 7 were waited for; matrix products, arithmetic and copies ran while one was open for 0% of the time, Pallas kernels for 18%

profile of v2, /device:TPU:0, one launch (start us, length us, event | category | flops | bytes accessed | tf_op | source)
XLA Modules:
  0.0 69.7 jit_solution(2648861284926940824)
XLA Ops:
  0.6 0.9 %shard_map.78 = bf16[3,8,2048]{2,1,0:T(8,128)(2,1)S(1)} custom-call(bf16[3,128,2048]{2,1,0:T(8,128)(2,1)} %x_far.3), custom_call_target="tpu_custom_call" | custom-call | bytes 4194304 | tf_op jit(solution)/shard_map/pallas_call | solution.py:474
  1.6 4.8 %collective-permute-start = (bf16[3,8,2048]{2,1,0:T(8,128)(2,1)S(1)}, bf16[3,8,2048]{2,1,0:T(8,128)(2,1)S(1)}, u32[]{:S(2)}, u32[]{:S(2)}) collective-permute-start(bf16[3,8,2048]{2,1,0:T(8,128)(2,1)S(1)} %shard_map.78), channel_id=1, source_target_pairs={{0,4},{4,8},{8,12},{12,16},{16,20},{20,24},{24,28},{1,5},{5,9},{9,... | collective-permute-start | bytes 294920 | tf_op jit(solution)/shard_map/ppermute | solution.py:489
  6.5 0.0 copy-start.5
  6.5 4.1 %shard_map.77 = (f32[2,128,16,128]{3,2,1,0:T(8,128)}, f32[3,7,16,128]{3,2,1,0:T(8,128)}, f32[2,8,16,128]{3,2,1,0:T(8,128)S(1)}, f32[3,16,16,128]{3,2,1,0:T(8,128...) custom-call(bf16[3,128,2048]{2,1,0:T(8,128)(2,1)} %x_far.3, bf16[3,7,128]{2,1,0:T(8,128)(2,1)} %bitcast.23, ...), custom_call_target="tpu_custom_call" | custom-call | flops 1000000000 | bytes 4194304 | tf_op jit(solution)/shard_map/pallas_call | solution.py:474
  10.6 0.0 collective-permute-done.halo
  10.6 0.1 shard_map.79
  10.7 0.0 copy-start.3
  10.7 3.5 %collective-permute-start.1 = (f32[16,16,128]{2,1,0:T(8,128)S(1)}, f32[16,16,128]{2,1,0:T(8,128)S(1)}, u32[]{:S(2)}, u32[]{:S(2)}) collective-permute-start(f32[16,16,128]{2,1,0:T(8,128)S(1)} %get-tuple-element.39), channel_id=1, source_target_pairs={{0,8},{4,12},{8,16},{12,20},{16,24},{20,28},{1,9},{5,13},{9,17},{1... | collective-permute-start | bytes 393224 | tf_op jit(solution)/shard_map/ppermute | solution.py:489
  14.2 0.0 copy-done.5
  14.2 2.1 %shard_map.80 = (f32[128,16,128]{2,1,0:T(8,128)S(1)}, f32[128,16,128]{2,1,0:T(8,128)S(1)}) custom-call(bf16[3,128,2048]{2,1,0:T(8,128)(2,1)} %x_far.3, bf16[3,8,2048]{2,1,0:T(8,128)(2,1)S(1)} %collective-permute-done.halo, f32[3,7,16,128]{3,2,1,0:T(8,128)S(1)} %get-tuple-element.37.taps, f32[16,128]{1,0:T(8,128)S(1)} %bitcast.21, bf16[128,2048]{1,0:T(8,128)(2,1)} %grad_far.1), custom_call_target="tpu_custom_call" | custom-call | flops 2000000000 | bytes 4194304 | tf_op jit(solution)/shard_map/pallas_call | solution.py:474
  16.3 0.4 collective-permute-done.1
  16.7 5.4 %collective-permute-start.2 = (f32[16,16,128]{2,1,0:T(8,128)S(1)}, f32[16,16,128]{2,1,0:T(8,128)S(1)}, u32[]{:S(2)}, u32[]{:S(2)}) collective-permute-start(f32[16,16,128]{2,1,0:T(8,128)S(1)} %fusion), channel_id=1, source_target_pairs={{0,16},{4,20},{8,24},{12,28},{1,17},{5,21},{9,25},{13,29},{2,18},{... | collective-permute-start | bytes 393224 | tf_op jit(solution)/shard_map/ppermute | solution.py:489
  22.1 2.4 %shard_map.81.local = f32[128,16,128]{2,1,0:T(8,128)S(1)} custom-call(f32[2,128,16,128]{3,2,1,0:T(8,128)S(1)} %copy-done, f32[2,8,16,128]{3,2,1,0:T(8,128)S(1)} %get-tuple-element.44.first_rows, f32[3,16,16,128]{3,2,1,0:T(8,128)S(1)} %get-tuple-element.36.table), custom_call_target="tpu_custom_call" | custom-call | flops 2000000000 | bytes 4194304 | tf_op jit(solution)/shard_map/pallas_call | solution.py:474
  24.5 0.1 collective-permute-done.2
  24.7 1.6 %collective-permute-start.3 = (f32[16,16,128]{2,1,0:T(8,128)S(1)}, f32[16,16,128]{2,1,0:T(8,128)S(1)}, u32[]{:S(2)}, u32[]{:S(2)}) collective-permute-start(f32[16,16,128]{2,1,0:T(8,128)S(1)} %get-tuple-element.68), channel_id=1, source_target_pairs={{0,4},{4,0},{8,12},{12,8},{16,20},{20,16},{24,28},{28,24},{1,5},{5... | collective-permute-start | bytes 393224 | tf_op jit(solution)/shard_map/ppermute | solution.py:493
  26.3 3.4 %collective-permute-done.3.received = f32[16,16,128]{2,1,0:T(8,128)S(1)} collective-permute-done((f32[16,16,128]{2,1,0:T(8,128)S(1)}, f32[16,16,128]{2,1,0:T(8,128)S(1)}, u32[]{:S(2)}, u32[]{:S(2)}) %collective-permute-start.3) | collective-permute-done | bytes 131104 | tf_op jit(solution)/shard_map/ppermute | solution.py:493
  29.7 1.6 %shard_map.82 = (f32[128,16,128]{2,1,0:T(8,128)S(1)}, f32[2,128]{1,0:T(2,128)S(1)}) custom-call(f32[16,16,128]{2,1,0:T(8,128)S(1)} %get-tuple-element.69.entering, f32[16,16,128]{2,1,0:T(8,128)S(1)} %collective-permute-done.3.received, f32[3,16,16,128]{3,2,1,0:T(8,128)S(1)} %get-tuple-element.36.table, f32[128,16,128]{2,1,0:T(8,128)S(1)} %get-tuple-element.46.query, ...), custom_call_target="tpu_custom_call" | custom-call | bytes 4194304 | tf_op jit(solution)/shard_map/pallas_call | solution.py:474
  31.3 5.7 %psum.7.sums = f32[2,128]{1,0:T(2,128)S(1)} all-reduce(f32[2,128]{1,0:T(2,128)S(1)} %get-tuple-element.49), channel_id=1, replica_groups=mesh['ctx'=8,'tp'=4] {'tp'}, use_global_device_ids=true, to_apply=%region_0.1 | all-reduce | flops 256 | bytes 2048 | tf_op jit(solution)/shard_map/psum | solution.py:591
  37.0 1.6 %shard_map.83 = (f32[128,16,128]{2,1,0:T(8,128)S(1)}, f32[128,16,128]{2,1,0:T(8,128)S(1)}, f32[16,16,128]{2,1,0:T(8,128)S(1)}, f32[128,128]{1,0:T(8,128)S(1)}) custom-call(f32[2,128]{1,0:T(2,128)S(1)} %psum.7.sums, f32[3,16,16,128]{3,2,1,0:T(8,128)S(1)} %get-tuple-element.36.table, f32[128,16,128]{2,1,0:T(8,128)S(1)} %get-tuple-element.46.query, ...), custom_call_target="tpu_custom_call" | custom-call | bytes 4194304 | tf_op jit(solution)/shard_map/pallas_call | solution.py:474
  38.6 1.3 %collective-permute-start.4 = (f32[16,16,128]{2,1,0:T(8,128)S(1)}, f32[16,16,128]{2,1,0:T(8,128)S(1)}, u32[]{:S(2)}, u32[]{:S(2)}) collective-permute-start(f32[16,16,128]{2,1,0:T(8,128)S(1)} %get-tuple-element.55.own), channel_id=1, source_target_pairs={{8,0},{12,4},{16,8},{20,12},{24,16},{28,20},{9,1},{13,5},{17,9},{2... | collective-permute-start | bytes 393224 | tf_op jit(solution)/shard_map/ppermute | solution.py:489
  39.9 0.0 copy-start.2
  39.9 2.3 %shard_map.85 = (f32[128,16,128]{2,1,0:T(8,128)S(1)}, bf16[4,6,16,128]{3,2,1,0:T(8,128)(2,1)S(1)}) custom-call(f32[3,16,16,128]{3,2,1,0:T(8,128)S(1)} %get-tuple-element.36.table, f32[2,8,16,128]{3,2,1,0:T(8,128)S(1)} %copy-done.4, f32[128,16,128]{2,1,0:T(8,128)S(1)} %get-tuple-element.50.long_conv, f32[128,16,128]{2,1,0:T(8,128)S(1)} %get-tuple-element.53.mixed, ...), custom_call_target="tpu_custom_call" | custom-call | flops 2000000000 | bytes 4194304 | tf_op jit(solution)/shard_map/pallas_call | solution.py:474
  42.2 4.9 %collective-permute-done.4.near = f32[16,16,128]{2,1,0:T(8,128)S(1)} collective-permute-done((f32[16,16,128]{2,1,0:T(8,128)S(1)}, f32[16,16,128]{2,1,0:T(8,128)S(1)}, u32[]{:S(2)}, u32[]{:S(2)}) %collective-permute-start.4) | collective-permute-done | bytes 131104 | tf_op jit(solution)/shard_map/ppermute | solution.py:489
  47.1 1.3 %collective-permute-start.6 = (bf16[4,6,16,128]{3,2,1,0:T(8,128)(2,1)S(1)}, bf16[4,6,16,128]{3,2,1,0:T(8,128)(2,1)S(1)}, u32[]{:S(2)}, u32[]{:S(2)}) collective-permute-start(bf16[4,6,16,128]{3,2,1,0:T(8,128)(2,1)S(1)} %get-tuple-element.59), channel_id=1, source_target_pairs={{4,0},{8,4},{12,8},{16,12},{20,16},{24,20},{28,24},{5,1},{9,5},{13... | collective-permute-start | bytes 294920 | tf_op jit(solution)/shard_map/ppermute | solution.py:489
  48.4 1.3 %collective-permute-start.5 = (f32[16,16,128]{2,1,0:T(8,128)S(1)}, f32[16,16,128]{2,1,0:T(8,128)S(1)}, u32[]{:S(2)}, u32[]{:S(2)}) collective-permute-start(f32[16,16,128]{2,1,0:T(8,128)S(1)} %fusion.4), channel_id=1, source_target_pairs={{16,0},{20,4},{24,8},{28,12},{17,1},{21,5},{25,9},{29,13},{18,2},{... | collective-permute-start | bytes 393224 | tf_op jit(solution)/shard_map/ppermute | solution.py:489
  49.7 1.7 %shard_map.84 = (bf16[128,2048]{1,0:T(8,128)(2,1)}, bf16[128,2048]{1,0:T(8,128)(2,1)S(1)}, f32[128,128]{1,0:T(8,128)S(1)}) custom-call(f32[128,128]{1,0:T(8,128)S(1)} %get-tuple-element.51.inv, f32[3,7,16,128]{3,2,1,0:T(8,128)S(1)} %copy-done.2, f32[16,128]{1,0:T(8,128)S(1)} %bitcast.22, f32[128,16,128]{2,1,0:T(8,128)S(1)} %get-tuple-element.46.query, ...), custom_call_target="tpu_custom_call" | custom-call | flops 2000000000 | bytes 4194304 | tf_op jit(solution)/shard_map/pallas_call | solution.py:474
  51.4 2.2 %collective-permute-done.6.head = bf16[4,6,16,128]{3,2,1,0:T(8,128)(2,1)S(1)} collective-permute-done((bf16[4,6,16,128]{3,2,1,0:T(8,128)(2,1)S(1)}, bf16[4,6,16,128]{3,2,1,0:T(8,128)(2,1)S(1)}, u32[]{:S(2)}, u32[]{:S(2)}) %collective-permute-start.6) | collective-permute-done | bytes 98336 | tf_op jit(solution)/shard_map/ppermute | solution.py:489
  53.6 6.7 %collective-permute-done.5 = f32[16,16,128]{2,1,0:T(8,128)S(1)} collective-permute-done((f32[16,16,128]{2,1,0:T(8,128)S(1)}, f32[16,16,128]{2,1,0:T(8,128)S(1)}, u32[]{:S(2)}, u32[]{:S(2)}) %collective-permute-start.5) | collective-permute-done | bytes 131104 | tf_op jit(solution)/shard_map/ppermute | solution.py:489
  60.3 0.1 shard_map.86
  60.4 0.9 %collective-permute-start.7 = (f32[24,16,128]{2,1,0:T(8,128)S(1)}, f32[24,16,128]{2,1,0:T(8,128)S(1)}, u32[]{:S(2)}, u32[]{:S(2)}) collective-permute-start(f32[24,16,128]{2,1,0:T(8,128)S(1)} %get-tuple-element.63), channel_id=1, source_target_pairs={{0,4},{4,0},{8,12},{12,8},{16,20},{20,16},{24,28},{28,24},{1,5},{5... | collective-permute-start | bytes 589832 | tf_op jit(solution)/shard_map/ppermute | solution.py:493
  61.3 4.8 %collective-permute-done.7.received = f32[24,16,128]{2,1,0:T(8,128)S(1)} collective-permute-done((f32[24,16,128]{2,1,0:T(8,128)S(1)}, f32[24,16,128]{2,1,0:T(8,128)S(1)}, u32[]{:S(2)}, u32[]{:S(2)}) %collective-permute-start.7) | collective-permute-done | bytes 196640 | tf_op jit(solution)/shard_map/ppermute | solution.py:493
  66.1 3.6 %shard_map.87 = bf16[3,128,2048]{2,1,0:T(8,128)(2,1)} custom-call(f32[16,16,128]{2,1,0:T(8,128)S(1)} %get-tuple-element.62.entering, f32[24,16,128]{2,1,0:T(8,128)S(1)} %collective-permute-done.7.received, f32[3,16,16,128]{3,2,1,0:T(8,128)S(1)} %get-tuple-element.36.table, f32[3,7,16,128]{3,2,1,0:T(8,128)S(1)} %copy-done.2, ...), custom_call_target="tpu_custom_call" | custom-call | bytes 4194304 | tf_op jit(solution)/shard_map/pallas_call | solution.py:474
  (12 shorter events, 0.1 us)
Async XLA Ops:
  1.6 9.0 %collective-permute-start = (bf16[3,8,2048]{2,1,0:T(8,128)(2,1)S(1)}, bf16[3,8,2048]{2,1,0:T(8,128)(2,1)S(1)}, u32[]{:S(2)}, u32[]{:S(2)}) collective-permute-start(bf16[3,8,2048]{2,1,0:T(8,128)(2,1)S(1)} %shard_map.78), channel_id=1, source_target_pairs={{0,4},{4,8},{8,12},{12,16},{16,20},{20,24},{24,28},{1,5},{5,9},{9,... | collective-permute-start | bytes 294920 | tf_op jit(solution)/shard_map/ppermute | solution.py:489
  6.5 7.8 %copy-start.5 = (f32[2048]{0:T(1024)S(1)}, f32[2048]{0:T(1024)}, u32[]{:S(2)}) copy-start(f32[2048]{0:T(1024)} %param.10) | copy-start | bytes 24580
  10.7 11.4 %copy-start.3 = (f32[2,8,16,128]{3,2,1,0:T(8,128)}, f32[2,8,16,128]{3,2,1,0:T(8,128)S(1)}, u32[]{:S(2)}) copy-start(f32[2,8,16,128]{3,2,1,0:T(8,128)S(1)} %get-tuple-element.44.first_rows) | copy-start | bytes 393220
  10.7 6.0 %collective-permute-start.1 = (f32[16,16,128]{2,1,0:T(8,128)S(1)}, f32[16,16,128]{2,1,0:T(8,128)S(1)}, u32[]{:S(2)}, u32[]{:S(2)}) collective-permute-start(f32[16,16,128]{2,1,0:T(8,128)S(1)} %get-tuple-element.39), channel_id=1, source_target_pairs={{0,8},{4,12},{8,16},{12,20},{16,24},{20,28},{1,9},{5,13},{9,17},{1... | collective-permute-start | bytes 393224 | tf_op jit(solution)/shard_map/ppermute | solution.py:489
  14.2 7.9 %copy-start = (f32[2,128,16,128]{3,2,1,0:T(8,128)S(1)}, f32[2,128,16,128]{3,2,1,0:T(8,128)}, u32[]{:S(2)}) copy-start(f32[2,128,16,128]{3,2,1,0:T(8,128)} %get-tuple-element.43.pair) | copy-start | bytes 6291460
  16.7 7.9 %collective-permute-start.2 = (f32[16,16,128]{2,1,0:T(8,128)S(1)}, f32[16,16,128]{2,1,0:T(8,128)S(1)}, u32[]{:S(2)}, u32[]{:S(2)}) collective-permute-start(f32[16,16,128]{2,1,0:T(8,128)S(1)} %fusion), channel_id=1, source_target_pairs={{0,16},{4,20},{8,24},{12,28},{1,17},{5,21},{9,25},{13,29},{2,18},{... | collective-permute-start | bytes 393224 | tf_op jit(solution)/shard_map/ppermute | solution.py:489
  24.7 5.0 %collective-permute-start.3 = (f32[16,16,128]{2,1,0:T(8,128)S(1)}, f32[16,16,128]{2,1,0:T(8,128)S(1)}, u32[]{:S(2)}, u32[]{:S(2)}) collective-permute-start(f32[16,16,128]{2,1,0:T(8,128)S(1)} %get-tuple-element.68), channel_id=1, source_target_pairs={{0,4},{4,0},{8,12},{12,8},{16,20},{20,16},{24,28},{28,24},{1,5},{5... | collective-permute-start | bytes 393224 | tf_op jit(solution)/shard_map/ppermute | solution.py:493
  37.0 2.9 %copy-start.4 = (f32[2,8,16,128]{3,2,1,0:T(8,128)S(1)}, f32[2,8,16,128]{3,2,1,0:T(8,128)}, u32[]{:S(2)}) copy-start(f32[2,8,16,128]{3,2,1,0:T(8,128)} %copy-done.3) | copy-start | bytes 393220
  38.6 8.5 %collective-permute-start.4 = (f32[16,16,128]{2,1,0:T(8,128)S(1)}, f32[16,16,128]{2,1,0:T(8,128)S(1)}, u32[]{:S(2)}, u32[]{:S(2)}) collective-permute-start(f32[16,16,128]{2,1,0:T(8,128)S(1)} %get-tuple-element.55.own), channel_id=1, source_target_pairs={{8,0},{12,4},{16,8},{20,12},{24,16},{28,20},{9,1},{13,5},{17,9},{2... | collective-permute-start | bytes 393224 | tf_op jit(solution)/shard_map/ppermute | solution.py:489
  39.9 9.8 %copy-start.2 = (f32[3,7,16,128]{3,2,1,0:T(8,128)S(1)}, f32[3,7,16,128]{3,2,1,0:T(8,128)}, u32[]{:S(2)}) copy-start(f32[3,7,16,128]{3,2,1,0:T(8,128)} %get-tuple-element.52.taps) | copy-start | bytes 516100
  47.1 6.5 %collective-permute-start.6 = (bf16[4,6,16,128]{3,2,1,0:T(8,128)(2,1)S(1)}, bf16[4,6,16,128]{3,2,1,0:T(8,128)(2,1)S(1)}, u32[]{:S(2)}, u32[]{:S(2)}) collective-permute-start(bf16[4,6,16,128]{3,2,1,0:T(8,128)(2,1)S(1)} %get-tuple-element.59), channel_id=1, source_target_pairs={{4,0},{8,4},{12,8},{16,12},{20,16},{24,20},{28,24},{5,1},{9,5},{13... | collective-permute-start | bytes 294920 | tf_op jit(solution)/shard_map/ppermute | solution.py:489
  48.4 11.8 %collective-permute-start.5 = (f32[16,16,128]{2,1,0:T(8,128)S(1)}, f32[16,16,128]{2,1,0:T(8,128)S(1)}, u32[]{:S(2)}, u32[]{:S(2)}) collective-permute-start(f32[16,16,128]{2,1,0:T(8,128)S(1)} %fusion.4), channel_id=1, source_target_pairs={{16,0},{20,4},{24,8},{28,12},{17,1},{21,5},{25,9},{29,13},{18,2},{... | collective-permute-start | bytes 393224 | tf_op jit(solution)/shard_map/ppermute | solution.py:489
  49.7 16.4 %copy-start.1 = (f32[2,128,16,128]{3,2,1,0:T(8,128)S(1)}, f32[2,128,16,128]{3,2,1,0:T(8,128)}, u32[]{:S(2)}) copy-start(f32[2,128,16,128]{3,2,1,0:T(8,128)} %get-tuple-element.43.pair) | copy-start | bytes 6291460
  60.4 5.7 %collective-permute-start.7 = (f32[24,16,128]{2,1,0:T(8,128)S(1)}, f32[24,16,128]{2,1,0:T(8,128)S(1)}, u32[]{:S(2)}, u32[]{:S(2)}) collective-permute-start(f32[24,16,128]{2,1,0:T(8,128)S(1)} %get-tuple-element.63), channel_id=1, source_target_pairs={{0,4},{4,0},{8,12},{12,8},{16,20},{20,16},{24,28},{28,24},{1,5},{5... | collective-permute-start | bytes 589832 | tf_op jit(solution)/shard_map/ppermute | solution.py:493

commit v3 on v2

--- a/solution.py
+++ b/solution.py
@@ -196,10 +196,12 @@
         )
 
 
-def local_kernel(pair, first_rows, table, local):
+def local_kernel(pair, first_rows, table, local, rows_far, sem):
     rows = local.shape[0]
     modes, lane_blocks = table.shape[1:3]
     zero = jnp.zeros((SUB, LANES), jnp.float32)
+    store = pltpu.make_async_copy(first_rows, rows_far, sem)
+    store.start()
     for half in halves(lane_blocks):
         decay = [table[0, m, half, :] for m in range(modes)]
         scale = [table[1, m, half, :] for m in range(modes)]
@@ -214,6 +216,7 @@
 
         state = block_step(first_rows, 0, (zero,) * modes)
         lax.fori_loop(1, rows // SUB, functools.partial(block_step, pair), state)
+    store.wait()
 
 
 def carry_kernel(entering, received, table, query, local, scaled, long_conv, sums, sq, cr):
@@ -254,7 +257,12 @@
         sums[which : which + 1, :] = jnp.sum(jnp.transpose(by_row), axis=0, keepdims=True)
 
 
-def mixed_kernel(width, sums, table, query, long_conv, scaled, mixed, long_grad, state_out, inv, inv_s, off_s):
+def mixed_kernel(
+    width, sums, table, query, long_conv, scaled, rows_far, mixed, long_grad, state_out, inv, head, inv_s, off_s,
+    first_rows, sem,
+):
+    fetch = pltpu.make_async_copy(rows_far, first_rows, sem)
+    fetch.start()
     rows = long_conv.shape[0]
     modes, lane_blocks = table.shape[1:3]
     zero = jnp.zeros((SUB, LANES), jnp.float32)
@@ -267,29 +275,42 @@
     for half in halves(lane_blocks):
         decay = [table[0, m, half, :] for m in range(modes)]
 
+        def row(t, state):
+            q = query[t, half, :]
+            modulated = q * long_conv[t, half, :]
+            mix = inv_s[pl.ds(t, 1), :] * scaled[t, half, :] - off_s[pl.ds(t, 1), :] * modulated
+            mixed[t, half, :] = mix
+            lg = mix * q
+            long_grad[t, half, :] = lg
+            return tuple(decay[m] * state[m] + lg for m in range(modes))
+
         def block_step(block, state):
             for k in range(SUB):
-                t = (blocks - 1 - block) * SUB + SUB - 1 - k
-                q = query[t, half, :]
-                modulated = q * long_conv[t, half, :]
-                mix = (
-                    inv_s[pl.ds(t, 1), :] * scaled[t, half, :] - off_s[pl.ds(t, 1), :] * modulated
+                state = row((blocks - 1 - block) * SUB + SUB - 1 - k, state)
+            return state
+
+        state = lax.fori_loop(0, blocks - 1, block_step, (zero,) * modes)
+        if half.start == 0:
+            fetch.wait()
+        for t in reversed(range(SUB)):
+            state = row(t, state)
+            if t < head.shape[1]:
+                gated = total(table[1, m, half, :] * state[m] for m in range(modes))
+                found = (
+                    mixed[t, half, :] * long_conv[t, half, :],
+                    gated,
+                    first_rows[1, t, half, :],
+                    first_rows[0, t, half, :],
                 )
-                mixed[t, half, :] = mix
-                lg = mix * q
-                long_grad[t, half, :] = lg
-                state = tuple(decay[m] * state[m] + lg for m in range(modes))
-            return state
-
-        state = lax.fori_loop(0, blocks, block_step, (zero,) * modes)
+                for i, value in enumerate(found):
+                    head[i, t, half, :] = value
         for m in range(modes):
             state_out[m, half, :] = state[m]
 
 
-def back_kernel(table, first_rows, long_conv, mixed, long_grad, local, head):
-    rows = long_conv.shape[0]
+def back_kernel(table, long_grad, local):
+    rows = long_grad.shape[0]
     modes, lane_blocks = table.shape[1:3]
-    reach = head.shape[1]
     blocks = rows // SUB
     zero = jnp.zeros((SUB, LANES), jnp.float32)
     for half in halves(lane_blocks):
@@ -305,14 +326,9 @@
             return state
 
         lax.fori_loop(0, blocks, block_step, (zero,) * modes)
-    for t in range(reach):
-        head[0, t] = (mixed[t] * long_conv[t]).astype(head.dtype)
-        head[1, t] = local[t].astype(head.dtype)
-        head[2, t] = first_rows[1, t].astype(head.dtype)
-        head[3, t] = first_rows[0, t].astype(head.dtype)
-
-
-def output_kernel(inv, taps, gain, query, long_conv, mixed, output, finished, last, os, qs):
+
+def output_kernel(inv, taps, gain, query, long_conv, mixed, head_in, output, finished, last, head, os, qs):
+    head[...] = head_in[...].astype(head.dtype)
     rows = long_conv.shape[0]
     lane_blocks = taps.shape[2]
     tap_count = taps.shape[1]
@@ -360,26 +376,85 @@
     return found
 
 
-def turn_kernel(rows, reach, lower, near, beyond, table, own, entering, message):
-    modes, lane_blocks = own.shape[:2]
-    is_lower = jnp.full((SUB, LANES), lower[0]) > 0
+def join_kernel(rows, span, place, table, state, entering, gathered, got, entering_out, message):
+    modes, lane_blocks = state.shape[:2]
+    column = lax.div(place[0], 2)
+    upper = jnp.full((SUB, LANES), lax.rem(lax.div(column, span), 2)) > 0
+    offset = lax.rem(column, span).astype(jnp.float32) * float(2 * rows)
+    is_lower = jnp.full((SUB, LANES), lax.rem(place[0], 2)) == 0
+    last = message.dtype == jnp.float32
     for half in halves(lane_blocks):
-        state = []
         for m in range(modes):
-            step = jnp.exp(table[2, m, half, :] * -float(2 * rows))
-            e = near[m, half, :] + step * beyond[m, half, :]
-            entering[m, half, :] = e
-            message[m, half, :] = jnp.where(is_lower, e, own[m, half, :] + step * e)
-            state.append(jnp.where(is_lower, beyond[m, half, :], e))
-        added = far_rows(table, half, state, rows, reach, rows)
+            rate = table[2, m, half, :]
+            other = got[m, half, :].astype(jnp.float32)
+            e = jnp.where(upper, jnp.exp(rate * -offset) * other, 0.0)
+            if span > 1:
+                e = entering[m, half, :] + e
+            entering_out[m, half, :] = e
+            if last:
+                joined = jnp.exp(rate * -float(2 * rows)) * e + state[m, half, :]
+                message[m, half, :] = jnp.where(is_lower, joined, e)
+            else:
+                mine = gathered[m, half, :].astype(jnp.float32)
+                fade = jnp.exp(rate * -float(2 * rows * span))
+                message[m, half, :] = (
+                    jnp.where(upper, mine, other) + fade * jnp.where(upper, other, mine)
+                ).astype(message.dtype)
+
+
+def join_back_kernel(
+    rows, reach, span, place, table, state, entering, beyond, added, gathered, got,
+    entering_out, beyond_out, added_out, message, *extra,
+):
+    modes, lane_blocks = state.shape[:2]
+    column = lax.div(place[0], 2)
+    within = lax.rem(column, span)
+    upper = jnp.full((SUB, LANES), lax.rem(lax.div(column, span), 2)) > 0
+    is_last = jnp.full((SUB, LANES), within) == span - 1
+    to_end = (span - 1 - within).astype(jnp.float32) * float(2 * rows)
+    is_lower = jnp.full((SUB, LANES), lax.rem(place[0], 2)) == 0
+    last = message.dtype == jnp.float32
+    for half in halves(lane_blocks):
+        sent = []
+        for m in range(modes):
+            rate = table[2, m, half, :]
+            other = got[m, half, :].astype(jnp.float32)
+            reached = jnp.where(upper, 0.0, jnp.exp(rate * -to_end) * other)
+            e, f = reached, jnp.zeros((SUB, LANES), jnp.float32)
+            if span > 1:
+                e = entering[m, half, :] + e
+                onward = jnp.exp(rate * -jnp.maximum(to_end - float(2 * rows), 0.0)) * other
+                f = beyond[m, half, :] + jnp.where(upper | is_last, 0.0, onward)
+            entering_out[m, half, :] = e
+            beyond_out[m, half, :] = f
+            if last:
+                joined = jnp.exp(rate * -float(2 * rows)) * e + state[m, half, :]
+                message[m, half, :] = jnp.where(is_lower, e, joined)
+                sent.append(jnp.where(is_lower, f, e))
+            else:
+                mine = gathered[m, half, :].astype(jnp.float32)
+                low, high = jnp.where(upper, other, mine), jnp.where(upper, mine, other)
+                fade = jnp.exp(rate * -float(2 * rows * span))
+                message[m, half, :] = (low + fade * high).astype(message.dtype)
+                fade = jnp.exp(rate * -float(2 * rows * (span - 1)))
+                sent.append(fade * high)
+        found = far_rows(table, half, sent, rows, reach, rows)
         for i in range(reach):
-            message[modes + i, half, :] = added[i]
-        for i in range(reach, SUB):
-            message[modes + i, half, :] = jnp.zeros((SUB, LANES), jnp.float32)
+            here = jnp.zeros((SUB, LANES), jnp.float32)
+            if span > 1:
+                mine, other = gathered[modes + i, half, :], got[modes + i, half, :]
+                here = added[i, half, :] + jnp.where(upper | ~is_last, 0.0, other.astype(jnp.float32))
+                low = jnp.where(upper, other.astype(jnp.float32), mine.astype(jnp.float32))
+            added_out[i, half, :] = here
+            if last:
+                extra[0][i, half, :] = (found[i] + jnp.where(is_lower, here, 0.0)).astype(extra[0].dtype)
+            else:
+                rest = found[i] if span == 1 else found[i] + low
+                message[modes + i, half, :] = rest.astype(message.dtype)
 
 
 def final_kernel(
-    entering, received, table, taps, pair, first_rows, local, query, last, head, grads, cg, os, ls, made, edge, sems
+    entering, received, received_rows, table, taps, pair, first_rows, local, query, last, head, grads, cg, os, ls, made, edge, sems
 ):
     rows = local.shape[0]
     modes, lane_blocks = table.shape[1:3]
@@ -417,7 +492,7 @@
         own = far_rows(table, half, [entering[m, half, :] for m in range(modes)], rows, reach, 0)
         beyond = [[], [], []]
         for i in range(reach):
-            gated = head[1, i, half, :].astype(jnp.float32) + received[modes + i, half, :] + own[i]
+            gated = head[1, i, half, :].astype(jnp.float32) + received_rows[i, half, :].astype(jnp.float32) + own[i]
             beyond[0].append(head[0, i, half, :].astype(jnp.float32))
             beyond[1].append(gated * head[2, i, half, :].astype(jnp.float32))
             beyond[2].append(gated * head[3, i, half, :].astype(jnp.float32))
@@ -489,8 +564,8 @@
     return lax.ppermute(block, "ctx", route)
 
 
-def swapped(block):
-    return lax.ppermute(block, "ctx", [(i, i ^ 1) for i in range(lax.axis_size("ctx"))])
+def swapped(block, distance):
+    return lax.ppermute(block, "ctx", [(i, i ^ distance) for i in range(lax.axis_size("ctx"))])
 
 
 def on_device(streams, short_filter, decay_rate, residue, norm_gain, out_grad):
@@ -548,8 +623,7 @@
         [kept(2, SUB, lane_blocks, LANES), jax.ShapeDtypeStruct(state_shape, jnp.float32)],
         ((2 * lane_blocks * SUB, LANES),),
     )
-    rate = table[2]
-    lower = (1 - lax.axis_index("ctx") % 2).astype(jnp.int32)
+    place = lax.axis_index("ctx").astype(jnp.int32)[None]
 
     query, scaled = run(
         query_kernel,
@@ -564,82 +638,105 @@
         ),
         work=2 * 10**9,
     )
-    (local,) = run(
-        local_kernel, v(pair_far, first_rows, table), [kept(*row_shape)], work=2 * 10**9
-    )
-    step = jnp.exp(rate * -float(2 * rows))
-    inclusive, entering = state, jnp.zeros_like(state)
-    width = 1
-    while 2 * width < count:
-        got = shifted(inclusive, 2 * width)
-        if width == 1:
+    local, rows_far = run(
+        local_kernel,
+        v(pair_far, first_rows, table),
+        [kept(*row_shape), pltpu.HBM((2, SUB, lane_blocks, LANES), jnp.float32)],
+        (pltpu.SemaphoreType.DMA(()),),
+        work=2 * 10**9,
+    )
+    entering = gathered = state
+    span = 1
+    while 2 * span < count:
+        got = swapped(gathered, 2 * span)
+        if span == 1:
             got, query, scaled = lax.optimization_barrier((got, query, scaled))
-            entering = got
-        else:
-            if 4 * width >= count:
-                got, local = lax.optimization_barrier((got, local))
-            entering = entering + jnp.exp(rate * -float(2 * rows * (width - 1))) * got
-        inclusive = state + step * entering
-        width *= 2
-    received = swapped(jnp.where(lower > 0, inclusive, entering))
+        if 4 * span >= count:
+            got, local = lax.optimization_barrier((got, local))
+        entering, gathered = run(
+            functools.partial(join_kernel, rows, span),
+            [(place, pltpu.SMEM)] + v(table, state, entering, gathered, got),
+            [
+                kept(*state_shape),
+                jax.ShapeDtypeStruct(state_shape, jnp.float32 if 4 * span >= count else bf16),
+            ],
+        )
+        span *= 2
+    received = swapped(gathered, 1)
     long_conv, sums = run(
         carry_kernel,
         v(entering, received, table, query, local, scaled),
         [kept(*row_shape), kept(2, rows)],
         ((rows * SUB, LANES), (rows * SUB, LANES)),
+        aliases={4: 0},
     )
     sums = lax.psum(sums, "tp")
-    mixed, long_grad, back, inv = run(
+    mixed, long_grad, back, inv, head = run(
         functools.partial(mixed_kernel, float(channels * lax.axis_size("tp"))),
-        v(sums, table, query, long_conv, scaled),
+        v(sums, table, query, long_conv, scaled) + far(rows_far),
         [
             kept(*row_shape),
             kept(*row_shape),
             jax.ShapeDtypeStruct(state_shape, jnp.float32),
             kept(rows, LANES),
+            kept(4, reach, lane_blocks, LANES),
         ],
-        ((rows, LANES), (rows, LANES)),
-    )
-
-    local_back, head = run(
-        back_kernel,
-        v(table, first_rows, long_conv, mixed, long_grad),
-        [kept(*row_shape), kept(4, reach, lane_blocks, LANES, dtype=bf16)],
-        work=2 * 10**9,
-    )
-    output, finished, last = run(
+        (
+            (rows, LANES),
+            (rows, LANES),
+            (2, SUB, lane_blocks, LANES),
+            pltpu.SemaphoreType.DMA(()),
+        ),
+        aliases={4: 0},
+    )
+
+    (local_back,) = run(
+        back_kernel, v(table, long_grad), [kept(*row_shape)], work=2 * 10**9
+    )
+    output, finished, last, head = run(
         output_kernel,
-        v(inv, taps_far, gain, query, long_conv, mixed),
+        v(inv, taps_far, gain, query, long_conv, mixed, head),
         [
             jax.ShapeDtypeStruct((rows, channels), bf16),
             kept(rows, channels, dtype=bf16),
             kept(lane_blocks * SUB, LANES),
+            jax.ShapeDtypeStruct(head.shape, bf16),
         ],
         ((lane_blocks * pitch, LANES), (lane_blocks * pitch, LANES)),
         work=2 * 10**9,
     )
-    inclusive, near, beyond = back, jnp.zeros_like(back), jnp.zeros_like(back)
-    width = 1
-    while 2 * width < count:
-        got = shifted(inclusive, -2 * width)
-        if width == 1:
-            got, head = lax.optimization_barrier((got, head))
-            near = got
-        else:
-            if 4 * width >= count:
-                got, head, finished = lax.optimization_barrier((got, shifted(head, -1), finished))
-            beyond = beyond + jnp.exp(rate * -float(2 * rows * (width - 2))) * got
-        inclusive = back + step * (near + step * beyond if width > 1 else near)
-        width *= 2
-    entering_back, message = run(
-        functools.partial(turn_kernel, rows, reach),
-        [(lower[None], pltpu.SMEM)] + v(near, beyond, table, back),
-        [kept(*state_shape), jax.ShapeDtypeStruct((modes + SUB, lane_blocks, LANES), jnp.float32)],
-    )
-    received_back = swapped(message)
+    entering = beyond = added = gathered = back
+    message_shape = (modes + reach, lane_blocks, LANES)
+    span = 1
+    while 2 * span < count:
+        got = swapped(gathered, 2 * span)
+        if span == 1:
+            got, local_back = lax.optimization_barrier((got, local_back))
+        if 4 * span >= count:
+            got, finished = lax.optimization_barrier((got, finished))
+        entering, beyond, added, gathered, *extra = run(
+            functools.partial(join_back_kernel, rows, reach, span),
+            [(place, pltpu.SMEM)] + v(table, back, entering, beyond, added, gathered, got),
+            [
+                kept(*state_shape),
+                kept(*state_shape),
+                kept(reach, lane_blocks, LANES),
+            ]
+            + (
+                [
+                    jax.ShapeDtypeStruct(state_shape, jnp.float32),
+                    jax.ShapeDtypeStruct((reach, lane_blocks, LANES), bf16),
+                ]
+                if 4 * span >= count
+                else [jax.ShapeDtypeStruct(message_shape, bf16)]
+            ),
+        )
+        span *= 2
+    head = shifted(head, -1)
+    received_back, received_rows = swapped(gathered, 1), swapped(extra[0], 1)
     (grads,) = run(
         final_kernel,
-        v(entering_back, received_back, table, taps_far, pair_far, first_rows, local_back, finished, last, head),
+        v(entering, received_back, received_rows, table, taps_far, pair_far, rows_far, local_back, finished, last, head),
         [pltpu.HBM((3, rows, channels), bf16)],
         (
             (2, rows, SUB, LANES),

time: 70 us -> 59.4 us (0.85)
  waiting for transfers between devices: 22.5 us -> 11.4 us
  Pallas kernels: 20.5 us -> 21.8 us
    ppermute x6 -> x2, waiting for transfers between devices: 14.2 us -> 2.51 us  [shifted(): return lax.ppermute(block, 'ctx', route)]
    ppermute x6 -> x2, starting transfers between devices: 17.6 us -> 6.13 us  [shifted(): return lax.ppermute(block, 'ctx', route)]
    ppermute x2 -> x7, starting transfers between devices: 2.53 us -> 13.3 us  [swapped(): lax.ppermute(block, 'ctx', [(i, i ^ distance) for i in range(lax.axis_siz...]
    pallas_call x11 -> x14, Pallas kernels: 20.5 us -> 21.8 us  [run(): pl.pallas_call(kernel, out_shape=outs, in_specs=[pl.BlockSpec(memory_spac...]
    ppermute x2 -> x7, waiting for transfers between devices: 8.24 us -> 8.92 us  [swapped(): lax.ppermute(block, 'ctx', [(i, i ^ distance) for i in range(lax.axis_siz...]
  transfers between devices with their start and end apart: 8 -> 9, of which waited for: 7 -> 7; matrix products, arithmetic and copies ran while one was open for 0% -> 0% of each run, Pallas kernels for 18% -> 21%
where the time goes in v3:
time: 59.4 us; the launch traced here: 59.1 us
  Pallas kernels  21.8 us (37%)
  starting transfers between devices  19.5 us (33%)
  waiting for transfers between devices  11.4 us (19%)
  blocking collectives  5.66 us (10%)
  between operations  0.74 us (1%)
    pallas_call x14, Pallas kernels, run(): pl.pallas_call(kernel, out_shape=outs, in_specs=[pl.BlockSpec(memory_spac...  21.8 us
    ppermute x7, starting transfers between devices, swapped(): lax.ppermute(block, 'ctx', [(i, i ^ distance) for i in range(lax.axis_siz...  13.3 us
    ppermute x7, waiting for transfers between devices, swapped(): lax.ppermute(block, 'ctx', [(i, i ^ distance) for i in range(lax.axis_siz...  8.92 us
    ppermute x2, starting transfers between devices, shifted(): return lax.ppermute(block, 'ctx', route)  6.13 us
    psum x1, blocking collectives, on_device(): sums = lax.psum(sums, 'tp')  5.66 us
    ppermute x2, waiting for transfers between devices, shifted(): return lax.ppermute(block, 'ctx', route)  2.51 us
  transfers between devices with their start and end apart: 9, of which 7 were waited for; matrix products, arithmetic and copies ran while one was open for 0% of the time, Pallas kernels for 21%

profile of v3, /device:TPU:0, one launch (start us, length us, event | category | flops | bytes accessed | tf_op | source)
XLA Modules:
  0.0 59.1 jit_solution(13165206150498203883)
XLA Ops:
  0.6 0.9 %shard_map.78 = bf16[3,8,2048]{2,1,0:T(8,128)(2,1)S(1)} custom-call(bf16[3,128,2048]{2,1,0:T(8,128)(2,1)} %x_far.3), custom_call_target="tpu_custom_call" | custom-call | bytes 4194304 | tf_op jit(solution)/shard_map/pallas_call | solution.py:549
  1.6 4.8 %collective-permute-start = (bf16[3,8,2048]{2,1,0:T(8,128)(2,1)S(1)}, bf16[3,8,2048]{2,1,0:T(8,128)(2,1)S(1)}, u32[]{:S(2)}, u32[]{:S(2)}) collective-permute-start(bf16[3,8,2048]{2,1,0:T(8,128)(2,1)S(1)} %shard_map.78), channel_id=1, source_target_pairs={{0,4},{4,8},{8,12},{12,16},{16,20},{20,24},{24,28},{1,5},{5,9},{9,... | collective-permute-start | bytes 294920 | tf_op jit(solution)/shard_map/ppermute | solution.py:564
  6.4 0.0 copy-start.4
  6.5 4.1 %shard_map.77 = (f32[2,128,16,128]{3,2,1,0:T(8,128)}, f32[3,7,16,128]{3,2,1,0:T(8,128)}, f32[2,8,16,128]{3,2,1,0:T(8,128)S(1)}, f32[3,16,16,128]{3,2,1,0:T(8,128...) custom-call(bf16[3,128,2048]{2,1,0:T(8,128)(2,1)} %x_far.3, bf16[3,7,128]{2,1,0:T(8,128)(2,1)} %bitcast.5, ...), custom_call_target="tpu_custom_call" | custom-call | flops 1000000000 | bytes 4194304 | tf_op jit(solution)/shard_map/pallas_call | solution.py:549
  10.6 0.1 shard_map.79
  10.7 1.6 %collective-permute-start.1 = (f32[16,16,128]{2,1,0:T(8,128)S(1)}, f32[16,16,128]{2,1,0:T(8,128)S(1)}, u32[]{:S(2)}, u32[]{:S(2)}) collective-permute-start(f32[16,16,128]{2,1,0:T(8,128)S(1)} %get-tuple-element.49.state.entering.gathered), channel_id=1, source_target_pairs={{0,8},{4,12},{8,0},{12,4},{16,24},{20,28},{24,16},{28,20},{1,9},{5... | collective-permute-start | bytes 393224 | tf_op jit(solution)/shard_map/ppermute | solution.py:568
  12.3 2.1 %shard_map.80 = (f32[128,16,128]{2,1,0:T(8,128)S(1)}, f32[128,16,128]{2,1,0:T(8,128)S(1)}) custom-call(bf16[3,128,2048]{2,1,0:T(8,128)(2,1)} %x_far.3, bf16[3,8,2048]{2,1,0:T(8,128)(2,1)S(1)} %collective-permute-done.halo, f32[3,7,16,128]{3,2,1,0:T(8,128)S(1)} %get-tuple-element.47.taps, f32[16,128]{1,0:T(8,128)S(1)} %bitcast.3, bf16[128,2048]{1,0:T(8,128)(2,1)} %grad_far.1), custom_call_target="tpu_custom_call" | custom-call | flops 2000000000 | bytes 4194304 | tf_op jit(solution)/shard_map/pallas_call | solution.py:549
  14.4 1.3 %collective-permute-done.1.got = f32[16,16,128]{2,1,0:T(8,128)S(1)} collective-permute-done((f32[16,16,128]{2,1,0:T(8,128)S(1)}, f32[16,16,128]{2,1,0:T(8,128)S(1)}, u32[]{:S(2)}, u32[]{:S(2)}) %collective-permute-start.1) | collective-permute-done | bytes 131104 | tf_op jit(solution)/shard_map/ppermute | solution.py:568
  15.7 0.1 shard_map.81
  15.8 2.7 %collective-permute-start.2 = (bf16[16,16,128]{2,1,0:T(8,128)(2,1)S(1)}, bf16[16,16,128]{2,1,0:T(8,128)(2,1)S(1)}, u32[]{:S(2)}, u32[]{:S(2)}) collective-permute-start(bf16[16,16,128]{2,1,0:T(8,128)(2,1)S(1)} %get-tuple-element.54.gathered), channel_id=1, source_target_pairs={{0,16},{4,20},{8,24},{12,28},{16,0},{20,4},{24,8},{28,12},{1,17},{... | collective-permute-start | bytes 196616 | tf_op jit(solution)/shard_map/ppermute | solution.py:568
  18.5 2.4 %shard_map.82 = (f32[128,16,128]{2,1,0:T(8,128)S(1)}, f32[2,8,16,128]{3,2,1,0:T(8,128)}) custom-call(f32[2,128,16,128]{3,2,1,0:T(8,128)S(1)} %copy-done, f32[2,8,16,128]{3,2,1,0:T(8,128)S(1)} %get-tuple-element.56.first_rows, f32[3,16,16,128]{3,2,1,0:T(8,128)S(1)} %get-tuple-element.45.table), custom_call_target="tpu_custom_call" | custom-call | flops 2000000000 | bytes 4194304 | tf_op jit(solution)/shard_map/pallas_call | solution.py:549
  20.8 0.2 collective-permute-done.2.got
  21.0 0.1 shard_map.83
  21.1 1.6 %collective-permute-start.3 = (f32[16,16,128]{2,1,0:T(8,128)S(1)}, f32[16,16,128]{2,1,0:T(8,128)S(1)}, u32[]{:S(2)}, u32[]{:S(2)}) collective-permute-start(f32[16,16,128]{2,1,0:T(8,128)S(1)} %get-tuple-element.60), channel_id=1, source_target_pairs={{0,4},{4,0},{8,12},{12,8},{16,20},{20,16},{24,28},{28,24},{1,5},{5... | collective-permute-start | bytes 393224 | tf_op jit(solution)/shard_map/ppermute | solution.py:568
  22.7 3.4 %collective-permute-done.3.received = f32[16,16,128]{2,1,0:T(8,128)S(1)} collective-permute-done((f32[16,16,128]{2,1,0:T(8,128)S(1)}, f32[16,16,128]{2,1,0:T(8,128)S(1)}, u32[]{:S(2)}, u32[]{:S(2)}) %collective-permute-start.3) | collective-permute-done | bytes 131104 | tf_op jit(solution)/shard_map/ppermute | solution.py:568
  26.1 1.7 %shard_map.84 = (f32[128,16,128]{2,1,0:T(8,128)S(1)}, f32[2,128]{1,0:T(2,128)S(1)}) custom-call(f32[16,16,128]{2,1,0:T(8,128)S(1)} %get-tuple-element.59.entering, f32[16,16,128]{2,1,0:T(8,128)S(1)} %collective-permute-done.3.received, f32[3,16,16,128]{3,2,1,0:T(8,128)S(1)} %get-tuple-element.45.table, ...), custom_call_target="tpu_custom_call", output_to_operand_aliasing={{0}: (4, {})} | custom-call | bytes 4194304 | tf_op jit(solution)/shard_map/pallas_call | solution.py:549
  27.8 5.7 %psum.7.sums = f32[2,128]{1,0:T(2,128)S(1)} all-reduce(f32[2,128]{1,0:T(2,128)S(1)} %get-tuple-element.64), channel_id=1, replica_groups=mesh['ctx'=8,'tp'=4] {'tp'}, use_global_device_ids=true, to_apply=%region_0.0 | all-reduce | flops 256 | bytes 2048 | tf_op jit(solution)/shard_map/psum | solution.py:673
  33.5 1.9 %shard_map.85 = (f32[128,16,128]{2,1,0:T(8,128)S(1)}, f32[128,16,128]{2,1,0:T(8,128)S(1)}, f32[16,16,128]{2,1,0:T(8,128)S(1)}, f32[128,128]{1,0:T(8,128)S(1)}, f32[4,6,16,128]{3,2,1,0:T(8,128)S(1)}) custom-call(f32[2,128]{1,0:T(2,128)S(1)} %psum.7.sums, f32[3,16,16,128]{3,2,1,0:T(8,128)S(1)} %get-tuple-element.45.table, ...), custom_call_target="tpu_custom_call", output_to_operand_aliasing={{0}: (4, {})} | custom-call | bytes 4194304 | tf_op jit(solution)/shard_map/pallas_call | solution.py:549
  35.4 1.6 %collective-permute-start.4 = (f32[16,16,128]{2,1,0:T(8,128)S(1)}, f32[16,16,128]{2,1,0:T(8,128)S(1)}, u32[]{:S(2)}, u32[]{:S(2)}) collective-permute-start(f32[16,16,128]{2,1,0:T(8,128)S(1)} %get-tuple-element.72.state.entering.beyond.added.gathered), channel_id=1, source_target_pairs={{0,8},{4,12},{8,0},{12,4},{16,24},{20,28},{24,16},{28,20},{1,9},{5... | collective-permute-start | bytes 393224 | tf_op jit(solution)/shard_map/ppermute | solution.py:568
  37.0 2.3 %shard_map.87.local = f32[128,16,128]{2,1,0:T(8,128)S(1)} custom-call(f32[3,16,16,128]{3,2,1,0:T(8,128)S(1)} %get-tuple-element.45.table, f32[128,16,128]{2,1,0:T(8,128)S(1)} %get-tuple-element.73.long_grad), custom_call_target="tpu_custom_call" | custom-call | flops 2000000000 | bytes 4194304 | tf_op jit(solution)/shard_map/pallas_call | solution.py:549
  39.3 1.4 %collective-permute-done.4.got = f32[16,16,128]{2,1,0:T(8,128)S(1)} collective-permute-done((f32[16,16,128]{2,1,0:T(8,128)S(1)}, f32[16,16,128]{2,1,0:T(8,128)S(1)}, u32[]{:S(2)}, u32[]{:S(2)}) %collective-permute-start.4) | collective-permute-done | bytes 131104 | tf_op jit(solution)/shard_map/ppermute | solution.py:568
  40.7 0.2 shard_map.88
  40.9 3.1 %collective-permute-start.5 = (bf16[22,16,128]{2,1,0:T(8,128)(2,1)S(1)}, bf16[22,16,128]{2,1,0:T(8,128)(2,1)S(1)}, u32[]{:S(2)}, u32[]{:S(2)}) collective-permute-start(bf16[22,16,128]{2,1,0:T(8,128)(2,1)S(1)} %get-tuple-element.78.gathered), channel_id=1, source_target_pairs={{0,16},{4,20},{8,24},{12,28},{16,0},{20,4},{24,8},{28,12},{1,17},{... | collective-permute-start | bytes 270344 | tf_op jit(solution)/shard_map/ppermute | solution.py:568
  44.0 1.7 %shard_map.86 = (bf16[128,2048]{1,0:T(8,128)(2,1)}, bf16[128,2048]{1,0:T(8,128)(2,1)S(1)}, f32[128,128]{1,0:T(8,128)S(1)}, bf16[4,6,16,128]{3,2,1,0:T(8,128)(2,1)S(1)}) custom-call(f32[128,128]{1,0:T(8,128)S(1)} %get-tuple-element.67.inv, f32[3,7,16,128]{3,2,1,0:T(8,128)S(1)} %copy-done.3, f32[16,128]{1,0:T(8,128)S(1)} %bitcast.4, ...), custom_call_target="tpu_custom_call" | custom-call | flops 2000000000 | bytes 4194304 | tf_op jit(solution)/shard_map/pallas_call | solution.py:549
  45.7 2.3 %collective-permute-done.5.got = bf16[22,16,128]{2,1,0:T(8,128)(2,1)S(1)} collective-permute-done((bf16[22,16,128]{2,1,0:T(8,128)(2,1)S(1)}, bf16[22,16,128]{2,1,0:T(8,128)(2,1)S(1)}, u32[]{:S(2)}, u32[]{:S(2)}) %collective-permute-start.5) | collective-permute-done | bytes 90144 | tf_op jit(solution)/shard_map/ppermute | solution.py:568
  48.0 0.8 %shard_map.89 = (f32[16,16,128]{2,1,0:T(8,128)S(1)}, f32[16,16,128]{2,1,0:T(8,128)}, f32[6,16,128]{2,1,0:T(8,128)}, f32[16,16,128]{2,1,0:T(8,128)S(1)}, bf16[6,16,128]{2,1,0:T(8,128)(2,1)S(1)}) custom-call(s32[1]{0:T(128)} %bitcast.place, f32[3,16,16,128]{3,2,1,0:T(8,128)S(1)} %get-tuple-element.45.table, ...), custom_call_target="tpu_custom_call" | custom-call | bytes 4194304 | tf_op jit(solution)/shard_map/pallas_call | solution.py:549
  48.8 1.3 %collective-permute-start.8 = (bf16[4,6,16,128]{3,2,1,0:T(8,128)(2,1)S(1)}, bf16[4,6,16,128]{3,2,1,0:T(8,128)(2,1)S(1)}, u32[]{:S(2)}, u32[]{:S(2)}) collective-permute-start(bf16[4,6,16,128]{3,2,1,0:T(8,128)(2,1)S(1)} %get-tuple-element.87), channel_id=1, source_target_pairs={{4,0},{8,4},{12,8},{16,12},{20,16},{24,20},{28,24},{5,1},{9,5},{13... | collective-permute-start | bytes 294920 | tf_op jit(solution)/shard_map/ppermute | solution.py:564
  50.1 2.7 %collective-permute-start.7 = (bf16[6,16,128]{2,1,0:T(8,128)(2,1)S(1)}, bf16[6,16,128]{2,1,0:T(8,128)(2,1)S(1)}, u32[]{:S(2)}, u32[]{:S(2)}) collective-permute-start(bf16[6,16,128]{2,1,0:T(8,128)(2,1)S(1)} %get-tuple-element.83), channel_id=1, source_target_pairs={{0,4},{4,0},{8,12},{12,8},{16,20},{20,16},{24,28},{28,24},{1,5},{5... | collective-permute-start | bytes 73736 | tf_op jit(solution)/shard_map/ppermute | solution.py:568
  52.8 2.5 %collective-permute-done.8.head = bf16[4,6,16,128]{3,2,1,0:T(8,128)(2,1)S(1)} collective-permute-done((bf16[4,6,16,128]{3,2,1,0:T(8,128)(2,1)S(1)}, bf16[4,6,16,128]{3,2,1,0:T(8,128)(2,1)S(1)}, u32[]{:S(2)}, u32[]{:S(2)}) %collective-permute-start.8) | collective-permute-done | bytes 98336 | tf_op jit(solution)/shard_map/ppermute | solution.py:564
  55.3 0.3 collective-permute-done.7.received_rows
  55.6 0.0 collective-permute-done.6.received
  55.6 3.6 %shard_map.90 = bf16[3,128,2048]{2,1,0:T(8,128)(2,1)} custom-call(f32[16,16,128]{2,1,0:T(8,128)S(1)} %get-tuple-element.81.entering, f32[16,16,128]{2,1,0:T(8,128)S(1)} %collective-permute-done.6.received, bf16[6,16,128]{2,1,0:T(8,128)(2,1)S(1)} %collective-permute-done.7.received_rows, f32[3,16,16,128]{3,2,1,0:T(8,128)S(1)} %get-tuple-element.45.table, ...), custom_call_target="tpu_custom_call" | custom-call | bytes 4194304 | tf_op jit(solution)/shard_map/pallas_call | solution.py:549
  (11 shorter events, 0.0 us)
Async XLA Ops:
  1.6 9.0 %collective-permute-start = (bf16[3,8,2048]{2,1,0:T(8,128)(2,1)S(1)}, bf16[3,8,2048]{2,1,0:T(8,128)(2,1)S(1)}, u32[]{:S(2)}, u32[]{:S(2)}) collective-permute-start(bf16[3,8,2048]{2,1,0:T(8,128)(2,1)S(1)} %shard_map.78), channel_id=1, source_target_pairs={{0,4},{4,8},{8,12},{12,16},{16,20},{20,24},{24,28},{1,5},{5,9},{9,... | collective-permute-start | bytes 294920 | tf_op jit(solution)/shard_map/ppermute | solution.py:564
  6.4 5.9 %copy-start.4 = (f32[2048]{0:T(1024)S(1)}, f32[2048]{0:T(1024)}, u32[]{:S(2)}) copy-start(f32[2048]{0:T(1024)} %param.10) | copy-start | bytes 24580
  10.7 5.0 %collective-permute-start.1 = (f32[16,16,128]{2,1,0:T(8,128)S(1)}, f32[16,16,128]{2,1,0:T(8,128)S(1)}, u32[]{:S(2)}, u32[]{:S(2)}) collective-permute-start(f32[16,16,128]{2,1,0:T(8,128)S(1)} %get-tuple-element.49.state.entering.gathered), channel_id=1, source_target_pairs={{0,8},{4,12},{8,0},{12,4},{16,24},{20,28},{24,16},{28,20},{1,9},{5... | collective-permute-start | bytes 393224 | tf_op jit(solution)/shard_map/ppermute | solution.py:568
  12.3 6.1 %copy-start = (f32[2,128,16,128]{3,2,1,0:T(8,128)S(1)}, f32[2,128,16,128]{3,2,1,0:T(8,128)}, u32[]{:S(2)}) copy-start(f32[2,128,16,128]{3,2,1,0:T(8,128)} %get-tuple-element.55.pair) | copy-start | bytes 6291460
  15.8 5.2 %collective-permute-start.2 = (bf16[16,16,128]{2,1,0:T(8,128)(2,1)S(1)}, bf16[16,16,128]{2,1,0:T(8,128)(2,1)S(1)}, u32[]{:S(2)}, u32[]{:S(2)}) collective-permute-start(bf16[16,16,128]{2,1,0:T(8,128)(2,1)S(1)} %get-tuple-element.54.gathered), channel_id=1, source_target_pairs={{0,16},{4,20},{8,24},{12,28},{16,0},{20,4},{24,8},{28,12},{1,17},{... | collective-permute-start | bytes 196616 | tf_op jit(solution)/shard_map/ppermute | solution.py:568
  21.1 5.0 %collective-permute-start.3 = (f32[16,16,128]{2,1,0:T(8,128)S(1)}, f32[16,16,128]{2,1,0:T(8,128)S(1)}, u32[]{:S(2)}, u32[]{:S(2)}) collective-permute-start(f32[16,16,128]{2,1,0:T(8,128)S(1)} %get-tuple-element.60), channel_id=1, source_target_pairs={{0,4},{4,0},{8,12},{12,8},{16,20},{20,16},{24,28},{28,24},{1,5},{5... | collective-permute-start | bytes 393224 | tf_op jit(solution)/shard_map/ppermute | solution.py:568
  35.4 5.3 %collective-permute-start.4 = (f32[16,16,128]{2,1,0:T(8,128)S(1)}, f32[16,16,128]{2,1,0:T(8,128)S(1)}, u32[]{:S(2)}, u32[]{:S(2)}) collective-permute-start(f32[16,16,128]{2,1,0:T(8,128)S(1)} %get-tuple-element.72.state.entering.beyond.added.gathered), channel_id=1, source_target_pairs={{0,8},{4,12},{8,0},{12,4},{16,24},{20,28},{24,16},{28,20},{1,9},{5... | collective-permute-start | bytes 393224 | tf_op jit(solution)/shard_map/ppermute | solution.py:568
  37.0 6.9 %copy-start.3 = (f32[3,7,16,128]{3,2,1,0:T(8,128)S(1)}, f32[3,7,16,128]{3,2,1,0:T(8,128)}, u32[]{:S(2)}) copy-start(f32[3,7,16,128]{3,2,1,0:T(8,128)} %get-tuple-element.68.taps) | copy-start | bytes 516100
  40.9 7.1 %collective-permute-start.5 = (bf16[22,16,128]{2,1,0:T(8,128)(2,1)S(1)}, bf16[22,16,128]{2,1,0:T(8,128)(2,1)S(1)}, u32[]{:S(2)}, u32[]{:S(2)}) collective-permute-start(bf16[22,16,128]{2,1,0:T(8,128)(2,1)S(1)} %get-tuple-element.78.gathered), channel_id=1, source_target_pairs={{0,16},{4,20},{8,24},{12,28},{16,0},{20,4},{24,8},{28,12},{1,17},{... | collective-permute-start | bytes 270344 | tf_op jit(solution)/shard_map/ppermute | solution.py:568
  44.0 11.6 %copy-start.1 = (f32[2,128,16,128]{3,2,1,0:T(8,128)S(1)}, f32[2,128,16,128]{3,2,1,0:T(8,128)}, u32[]{:S(2)}) copy-start(f32[2,128,16,128]{3,2,1,0:T(8,128)} %get-tuple-element.55.pair) | copy-start | bytes 6291460
  44.0 11.6 %copy-start.2 = (f32[2,8,16,128]{3,2,1,0:T(8,128)S(1)}, f32[2,8,16,128]{3,2,1,0:T(8,128)}, u32[]{:S(2)}) copy-start(f32[2,8,16,128]{3,2,1,0:T(8,128)} %get-tuple-element.66.rows_far.first_rows) | copy-start | bytes 393220
  48.8 6.8 %collective-permute-start.6 = (f32[16,16,128]{2,1,0:T(8,128)S(1)}, f32[16,16,128]{2,1,0:T(8,128)S(1)}, u32[]{:S(2)}, u32[]{:S(2)}) collective-permute-start(f32[16,16,128]{2,1,0:T(8,128)S(1)} %get-tuple-element.82), channel_id=1, source_target_pairs={{0,4},{4,0},{8,12},{12,8},{16,20},{20,16},{24,28},{28,24},{1,5},{5... | collective-permute-start | bytes 393224 | tf_op jit(solution)/shard_map/ppermute | solution.py:568
  48.8 6.5 %collective-permute-start.8 = (bf16[4,6,16,128]{3,2,1,0:T(8,128)(2,1)S(1)}, bf16[4,6,16,128]{3,2,1,0:T(8,128)(2,1)S(1)}, u32[]{:S(2)}, u32[]{:S(2)}) collective-permute-start(bf16[4,6,16,128]{3,2,1,0:T(8,128)(2,1)S(1)} %get-tuple-element.87), channel_id=1, source_target_pairs={{4,0},{8,4},{12,8},{16,12},{20,16},{24,20},{28,24},{5,1},{9,5},{13... | collective-permute-start | bytes 294920 | tf_op jit(solution)/shard_map/ppermute | solution.py:564
  50.1 5.5 %collective-permute-start.7 = (bf16[6,16,128]{2,1,0:T(8,128)(2,1)S(1)}, bf16[6,16,128]{2,1,0:T(8,128)(2,1)S(1)}, u32[]{:S(2)}, u32[]{:S(2)}) collective-permute-start(bf16[6,16,128]{2,1,0:T(8,128)(2,1)S(1)} %get-tuple-element.83), channel_id=1, source_target_pairs={{0,4},{4,0},{8,12},{12,8},{16,20},{20,16},{24,28},{28,24},{1,5},{5... | collective-permute-start | bytes 73736 | tf_op jit(solution)/shard_map/ppermute | solution.py:568

commit v4 on v3

--- a/solution.py
+++ b/solution.py
@@ -31,6 +31,32 @@
     for lb in range(lane_blocks):
         tile = source[:, lb * LANES : (lb + 1) * LANES]
         target[pl.ds(first + lb * pitch, rows), :] = tile.astype(jnp.float32)
+
+
+def to_send(table, half, states, lag):
+    modes = table.shape[1]
+    down, off_down, up, off_up, chosen, off = [], [], [], [], [], []
+    for m in range(modes):
+        x = states[m]
+        near = x.astype(jnp.bfloat16).astype(jnp.float32)
+        other = (x + jnp.where(near < x, 0.00390625, -0.00390625) * jnp.abs(x)).astype(jnp.bfloat16).astype(jnp.float32)
+        weight = table[1, m, half, :] * jnp.exp(table[2, m, half, :] * -float(lag))
+        down.append(near)
+        up.append(other)
+        off_down.append(weight * (near - x))
+        off_up.append(weight * (other - x))
+    sum_off = jnp.zeros((SUB, LANES), jnp.float32)
+    for turn in range(2):
+        for m in range(modes):
+            base = sum_off if turn == 0 else sum_off - off[m]
+            first, second = base + off_down[m], base + off_up[m]
+            take = jnp.abs(second) < jnp.abs(first)
+            sum_off = jnp.where(take, second, first)
+            if turn == 0:
+                off.append(jnp.where(take, off_up[m], off_down[m]))
+            else:
+                chosen.append(jnp.where(take, up[m], down[m]).astype(jnp.bfloat16))
+    return chosen
 
 
 def row_at(ref, first, pitch, half, place):
@@ -134,7 +160,7 @@
         store.wait()
 
 
-def head_kernel(rows, first_in, halo, table, taps, ends, first_rows, state_out, hs):
+def head_kernel(rows, first_in, halo, table, taps, ends, first_rows, state_out, message, hs):
     modes, lane_blocks = ends.shape[:2]
     reach = taps.shape[1] - 1
     for s in range(2):
@@ -153,13 +179,17 @@
                 first_rows[s, t, half, :] = row
             heads.append(head)
         product = [heads[0][t] * heads[1][t] for t in range(reach)]
+        states = []
         for m in range(modes):
             decay = table[0, m, half, :]
             state = product[0]
             for t in range(1, reach):
                 state = decay * state + product[t]
             fade = jnp.exp(table[2, m, half, :] * -float(rows - reach))
-            state_out[m, half, :] = ends[m, half, :] + fade * state
+            states.append(ends[m, half, :] + fade * state)
+            state_out[m, half, :] = states[m]
+        for m, value in enumerate(to_send(table, half, states, rows)):
+            message[m, half, :] = value
 
 
 def query_kernel(x_far, halo, taps, gain, grad_far, query, scaled, x, grad, xs, gs, sems):
@@ -227,7 +257,7 @@
         start = []
         for m in range(modes):
             fade = jnp.exp(table[2, m, half, :] * -float(rows))
-            incoming = fade * entering[m, half, :] + received[m, half, :]
+            incoming = fade * entering[m, half, :] + received[m, half, :].astype(jnp.float32)
             start.append(table[1, m, half, :] * decay[m] * incoming)
 
         def block_step(block, state):
@@ -258,7 +288,7 @@
 
 
 def mixed_kernel(
-    width, sums, table, query, long_conv, scaled, rows_far, mixed, long_grad, state_out, inv, head, inv_s, off_s,
+    width, sums, table, query, long_conv, scaled, rows_far, mixed, long_grad, state_out, message, inv, head, inv_s, off_s,
     first_rows, sem,
 ):
     fetch = pltpu.make_async_copy(rows_far, first_rows, sem)
@@ -304,8 +334,9 @@
                 )
                 for i, value in enumerate(found):
                     head[i, t, half, :] = value
-        for m in range(modes):
+        for m, value in enumerate(to_send(table, half, state, rows)):
             state_out[m, half, :] = state[m]
+            message[m, half, :] = value
 
 
 def back_kernel(table, long_grad, local):
@@ -376,14 +407,14 @@
     return found
 
 
-def join_kernel(rows, span, place, table, state, entering, gathered, got, entering_out, message):
+def join_kernel(rows, span, last, place, table, state, entering, gathered, got, entering_out, message, *gathered_out):
     modes, lane_blocks = state.shape[:2]
     column = lax.div(place[0], 2)
     upper = jnp.full((SUB, LANES), lax.rem(lax.div(column, span), 2)) > 0
     offset = lax.rem(column, span).astype(jnp.float32) * float(2 * rows)
     is_lower = jnp.full((SUB, LANES), lax.rem(place[0], 2)) == 0
-    last = message.dtype == jnp.float32
     for half in halves(lane_blocks):
+        sent = []
         for m in range(modes):
             rate = table[2, m, half, :]
             other = got[m, half, :].astype(jnp.float32)
@@ -393,18 +424,19 @@
             entering_out[m, half, :] = e
             if last:
                 joined = jnp.exp(rate * -float(2 * rows)) * e + state[m, half, :]
-                message[m, half, :] = jnp.where(is_lower, joined, e)
+                sent.append(jnp.where(is_lower, joined, e))
             else:
-                mine = gathered[m, half, :].astype(jnp.float32)
+                mine = gathered[m, half, :]
                 fade = jnp.exp(rate * -float(2 * rows * span))
-                message[m, half, :] = (
-                    jnp.where(upper, mine, other) + fade * jnp.where(upper, other, mine)
-                ).astype(message.dtype)
+                sent.append(jnp.where(upper, mine, other) + fade * jnp.where(upper, other, mine))
+                gathered_out[0][m, half, :] = sent[m]
+        for m, value in enumerate(to_send(table, half, sent, rows // 2 if last else rows)):
+            message[m, half, :] = value
 
 
 def join_back_kernel(
-    rows, reach, span, place, table, state, entering, beyond, added, gathered, got,
-    entering_out, beyond_out, added_out, message, *extra,
+    rows, reach, span, last, place, table, state, entering, beyond, added, gathered, got,
+    entering_out, message, *kept_out,
 ):
     modes, lane_blocks = state.shape[:2]
     column = lax.div(place[0], 2)
@@ -413,48 +445,50 @@
     is_last = jnp.full((SUB, LANES), within) == span - 1
     to_end = (span - 1 - within).astype(jnp.float32) * float(2 * rows)
     is_lower = jnp.full((SUB, LANES), lax.rem(place[0], 2)) == 0
-    last = message.dtype == jnp.float32
     for half in halves(lane_blocks):
-        sent = []
+        sent, far_on = [], []
         for m in range(modes):
             rate = table[2, m, half, :]
             other = got[m, half, :].astype(jnp.float32)
-            reached = jnp.where(upper, 0.0, jnp.exp(rate * -to_end) * other)
-            e, f = reached, jnp.zeros((SUB, LANES), jnp.float32)
+            e, f = jnp.where(upper, 0.0, jnp.exp(rate * -to_end) * other), jnp.zeros((SUB, LANES), jnp.float32)
             if span > 1:
                 e = entering[m, half, :] + e
                 onward = jnp.exp(rate * -jnp.maximum(to_end - float(2 * rows), 0.0)) * other
                 f = beyond[m, half, :] + jnp.where(upper | is_last, 0.0, onward)
             entering_out[m, half, :] = e
-            beyond_out[m, half, :] = f
+            if not last:
+                kept_out[0][m, half, :] = f
             if last:
                 joined = jnp.exp(rate * -float(2 * rows)) * e + state[m, half, :]
-                message[m, half, :] = jnp.where(is_lower, e, joined)
-                sent.append(jnp.where(is_lower, f, e))
+                sent.append(jnp.where(is_lower, e, joined))
+                far_on.append(jnp.where(is_lower, f, e))
             else:
-                mine = gathered[m, half, :].astype(jnp.float32)
+                mine = gathered[m, half, :]
                 low, high = jnp.where(upper, other, mine), jnp.where(upper, mine, other)
                 fade = jnp.exp(rate * -float(2 * rows * span))
-                message[m, half, :] = (low + fade * high).astype(message.dtype)
+                sent.append(low + fade * high)
+                kept_out[2][m, half, :] = sent[m]
                 fade = jnp.exp(rate * -float(2 * rows * (span - 1)))
-                sent.append(fade * high)
-        found = far_rows(table, half, sent, rows, reach, rows)
+                far_on.append(fade * high)
+        for m, value in enumerate(to_send(table, half, sent, rows // 2 if last else rows)):
+            message[m, half, :] = value
+        found = far_rows(table, half, far_on, rows, reach, rows)
         for i in range(reach):
-            here = jnp.zeros((SUB, LANES), jnp.float32)
+            here, rest = jnp.zeros((SUB, LANES), jnp.float32), found[i]
             if span > 1:
-                mine, other = gathered[modes + i, half, :], got[modes + i, half, :]
-                here = added[i, half, :] + jnp.where(upper | ~is_last, 0.0, other.astype(jnp.float32))
-                low = jnp.where(upper, other.astype(jnp.float32), mine.astype(jnp.float32))
-            added_out[i, half, :] = here
+                mine, other = gathered[modes + i, half, :], got[modes + i, half, :].astype(jnp.float32)
+                here = added[i, half, :] + jnp.where(upper | ~is_last, 0.0, other)
+                rest = rest + jnp.where(upper, other, mine)
             if last:
-                extra[0][i, half, :] = (found[i] + jnp.where(is_lower, here, 0.0)).astype(extra[0].dtype)
+                message[modes + i, half, :] = (found[i] + jnp.where(is_lower, here, 0.0)).astype(message.dtype)
             else:
-                rest = found[i] if span == 1 else found[i] + low
                 message[modes + i, half, :] = rest.astype(message.dtype)
+                kept_out[1][i, half, :] = here
+                kept_out[2][modes + i, half, :] = rest
 
 
 def final_kernel(
-    entering, received, received_rows, table, taps, pair, first_rows, local, query, last, head, grads, cg, os, ls, made, edge, sems
+    entering, received, table, taps, pair, first_rows, local, query, last, head, grads, cg, os, ls, made, edge, sems
 ):
     rows = local.shape[0]
     modes, lane_blocks = table.shape[1:3]
@@ -475,7 +509,7 @@
         start = []
         for m in range(modes):
             fade = jnp.exp(table[2, m, half, :] * -float(rows))
-            incoming = fade * entering[m, half, :] + received[m, half, :]
+            incoming = fade * entering[m, half, :] + received[m, half, :].astype(jnp.float32)
             start.append(table[1, m, half, :] * decay[m] * incoming)
 
         def block_step(source, block, state):
@@ -492,7 +526,7 @@
         own = far_rows(table, half, [entering[m, half, :] for m in range(modes)], rows, reach, 0)
         beyond = [[], [], []]
         for i in range(reach):
-            gated = head[1, i, half, :].astype(jnp.float32) + received_rows[i, half, :].astype(jnp.float32) + own[i]
+            gated = head[1, i, half, :].astype(jnp.float32) + received[modes + i, half, :].astype(jnp.float32) + own[i]
             beyond[0].append(head[0, i, half, :].astype(jnp.float32))
             beyond[1].append(gated * head[2, i, half, :].astype(jnp.float32))
             beyond[2].append(gated * head[3, i, half, :].astype(jnp.float32))
@@ -617,10 +651,10 @@
         ),
         work=10**9,
     )
-    first_rows, state = run(
+    first_rows, state, message = run(
         functools.partial(head_kernel, rows),
         v(first_rows, halo, table, taps, ends),
-        [kept(2, SUB, lane_blocks, LANES), jax.ShapeDtypeStruct(state_shape, jnp.float32)],
+        [kept(2, SUB, lane_blocks, LANES), kept(*state_shape), jax.ShapeDtypeStruct(state_shape, bf16)],
         ((2 * lane_blocks * SUB, LANES),),
     )
     place = lax.axis_index("ctx").astype(jnp.int32)[None]
@@ -648,21 +682,24 @@
     entering = gathered = state
     span = 1
     while 2 * span < count:
-        got = swapped(gathered, 2 * span)
+        final = 4 * span >= count
+        got = swapped(message, 2 * span)
         if span == 1:
             got, query, scaled = lax.optimization_barrier((got, query, scaled))
-        if 4 * span >= count:
+        if final:
             got, local = lax.optimization_barrier((got, local))
-        entering, gathered = run(
-            functools.partial(join_kernel, rows, span),
+        entering, message, *more = run(
+            functools.partial(join_kernel, rows, span, final),
             [(place, pltpu.SMEM)] + v(table, state, entering, gathered, got),
             [
                 kept(*state_shape),
-                jax.ShapeDtypeStruct(state_shape, jnp.float32 if 4 * span >= count else bf16),
-            ],
+                jax.ShapeDtypeStruct(state_shape, bf16),
+            ]
+            + ([] if final else [kept(*state_shape)]),
         )
+        gathered = None if final else more[0]
         span *= 2
-    received = swapped(gathered, 1)
+    received = swapped(message, 1)
     long_conv, sums = run(
         carry_kernel,
         v(entering, received, table, query, local, scaled),
@@ -671,13 +708,14 @@
         aliases={4: 0},
     )
     sums = lax.psum(sums, "tp")
-    mixed, long_grad, back, inv, head = run(
+    mixed, long_grad, back, message, inv, head = run(
         functools.partial(mixed_kernel, float(channels * lax.axis_size("tp"))),
         v(sums, table, query, long_conv, scaled) + far(rows_far),
         [
             kept(*row_shape),
             kept(*row_shape),
-            jax.ShapeDtypeStruct(state_shape, jnp.float32),
+            kept(*state_shape),
+            jax.ShapeDtypeStruct(state_shape, bf16),
             kept(rows, LANES),
             kept(4, reach, lane_blocks, LANES),
         ],
@@ -709,34 +747,32 @@
     message_shape = (modes + reach, lane_blocks, LANES)
     span = 1
     while 2 * span < count:
-        got = swapped(gathered, 2 * span)
+        final = 4 * span >= count
+        got = swapped(message, 2 * span)
         if span == 1:
             got, local_back = lax.optimization_barrier((got, local_back))
-        if 4 * span >= count:
+        if final:
             got, finished = lax.optimization_barrier((got, finished))
-        entering, beyond, added, gathered, *extra = run(
-            functools.partial(join_back_kernel, rows, reach, span),
+        entering, message, *more = run(
+            functools.partial(join_back_kernel, rows, reach, span, final),
             [(place, pltpu.SMEM)] + v(table, back, entering, beyond, added, gathered, got),
             [
                 kept(*state_shape),
-                kept(*state_shape),
-                kept(reach, lane_blocks, LANES),
+                jax.ShapeDtypeStruct(message_shape, bf16),
             ]
             + (
-                [
-                    jax.ShapeDtypeStruct(state_shape, jnp.float32),
-                    jax.ShapeDtypeStruct((reach, lane_blocks, LANES), bf16),
-                ]
-                if 4 * span >= count
-                else [jax.ShapeDtypeStruct(message_shape, bf16)]
+                []
+                if final
+                else [kept(*state_shape), kept(reach, lane_blocks, LANES), kept(*message_shape)]
             ),
         )
+        beyond, added, gathered = (None,) * 3 if final else more
         span *= 2
     head = shifted(head, -1)
-    received_back, received_rows = swapped(gathered, 1), swapped(extra[0], 1)
+    received = swapped(message, 1)
     (grads,) = run(
         final_kernel,
-        v(entering, received_back, received_rows, table, taps_far, pair_far, rows_far, local_back, finished, last, head),
+        v(entering, received, table, taps_far, pair_far, rows_far, local_back, finished, last, head),
         [pltpu.HBM((3, rows, channels), bf16)],
         (
             (2, rows, SUB, LANES),

time: 59.4 us -> 55.7 us (0.938)
  waiting for transfers between devices: 11.4 us -> 8.68 us
  starting transfers between devices: 19.5 us -> 17.9 us
  Pallas kernels: 21.8 us -> 22.5 us
    ppermute x7 -> x6, waiting for transfers between devices: 8.92 us -> 6.2 us  [swapped(): lax.ppermute(block, 'ctx', [(i, i ^ distance) for i in range(lax.axis_siz...]
    ppermute x7 -> x6, starting transfers between devices: 13.3 us -> 11.8 us  [swapped(): lax.ppermute(block, 'ctx', [(i, i ^ distance) for i in range(lax.axis_siz...]
    pallas_call x14, Pallas kernels: 21.8 us -> 22.5 us  [run(): pl.pallas_call(kernel, out_shape=outs, in_specs=[pl.BlockSpec(memory_spac...]
  transfers between devices with their start and end apart: 9 -> 8, of which waited for: 7 -> 7; matrix products, arithmetic and copies ran while one was open for 0% -> 0% of each run, Pallas kernels for 21% -> 23%
where the time goes in v4:
time: 55.7 us; the launch traced here: 55.5 us
  Pallas kernels  22.5 us (40%)
  starting transfers between devices  17.9 us (32%)
  waiting for transfers between devices  8.68 us (16%)
  blocking collectives  5.66 us (10%)
  between operations  0.73 us (1%)
    pallas_call x14, Pallas kernels, run(): pl.pallas_call(kernel, out_shape=outs, in_specs=[pl.BlockSpec(memory_spac...  22.5 us
    ppermute x6, starting transfers between devices, swapped(): lax.ppermute(block, 'ctx', [(i, i ^ distance) for i in range(lax.axis_siz...  11.8 us
    ppermute x6, waiting for transfers between devices, swapped(): lax.ppermute(block, 'ctx', [(i, i ^ distance) for i in range(lax.axis_siz...  6.2 us
    ppermute x2, starting transfers between devices, shifted(): return lax.ppermute(block, 'ctx', route)  6.13 us
    psum x1, blocking collectives, on_device(): sums = lax.psum(sums, 'tp')  5.66 us
    ppermute x2, waiting for transfers between devices, shifted(): return lax.ppermute(block, 'ctx', route)  2.48 us
  transfers between devices with their start and end apart: 8, of which 7 were waited for; matrix products, arithmetic and copies ran while one was open for 0% of the time, Pallas kernels for 23%

profile of v4, /device:TPU:0, one launch (start us, length us, event | category | flops | bytes accessed | tf_op | source)
XLA Modules:
  0.0 55.5 jit_solution(1811379582283783624)
XLA Ops:
  0.6 0.9 %shard_map.78 = bf16[3,8,2048]{2,1,0:T(8,128)(2,1)S(1)} custom-call(bf16[3,128,2048]{2,1,0:T(8,128)(2,1)} %x_far.3), custom_call_target="tpu_custom_call" | custom-call | bytes 4194304 | tf_op jit(solution)/shard_map/pallas_call | solution.py:583
  1.6 4.8 %collective-permute-start = (bf16[3,8,2048]{2,1,0:T(8,128)(2,1)S(1)}, bf16[3,8,2048]{2,1,0:T(8,128)(2,1)S(1)}, u32[]{:S(2)}, u32[]{:S(2)}) collective-permute-start(bf16[3,8,2048]{2,1,0:T(8,128)(2,1)S(1)} %shard_map.78), channel_id=1, source_target_pairs={{0,4},{4,8},{8,12},{12,16},{16,20},{20,24},{24,28},{1,5},{5,9},{9,... | collective-permute-start | bytes 294920 | tf_op jit(solution)/shard_map/ppermute | solution.py:598
  6.4 0.0 copy-start.4
  6.5 4.1 %shard_map.77 = (f32[2,128,16,128]{3,2,1,0:T(8,128)}, f32[3,7,16,128]{3,2,1,0:T(8,128)}, f32[2,8,16,128]{3,2,1,0:T(8,128)S(1)}, f32[3,16,16,128]{3,2,1,0:T(8,128...) custom-call(bf16[3,128,2048]{2,1,0:T(8,128)(2,1)} %x_far.3, bf16[3,7,128]{2,1,0:T(8,128)(2,1)} %bitcast.5, ...), custom_call_target="tpu_custom_call" | custom-call | flops 1000000000 | bytes 4194304 | tf_op jit(solution)/shard_map/pallas_call | solution.py:583
  10.6 0.0 collective-permute-done.halo
  10.6 0.3 shard_map.79
  10.9 1.6 %collective-permute-start.1 = (bf16[16,16,128]{2,1,0:T(8,128)(2,1)S(1)}, bf16[16,16,128]{2,1,0:T(8,128)(2,1)S(1)}, u32[]{:S(2)}, u32[]{:S(2)}) collective-permute-start(bf16[16,16,128]{2,1,0:T(8,128)(2,1)S(1)} %get-tuple-element.53), channel_id=1, source_target_pairs={{0,8},{4,12},{8,0},{12,4},{16,24},{20,28},{24,16},{28,20},{1,9},{5... | collective-permute-start | bytes 196616 | tf_op jit(solution)/shard_map/ppermute | solution.py:602
  12.6 2.1 %shard_map.80 = (f32[128,16,128]{2,1,0:T(8,128)S(1)}, f32[128,16,128]{2,1,0:T(8,128)S(1)}) custom-call(bf16[3,128,2048]{2,1,0:T(8,128)(2,1)} %x_far.3, bf16[3,8,2048]{2,1,0:T(8,128)(2,1)S(1)} %collective-permute-done.halo, f32[3,7,16,128]{3,2,1,0:T(8,128)S(1)} %get-tuple-element.50.taps, f32[16,128]{1,0:T(8,128)S(1)} %bitcast.3, bf16[128,2048]{1,0:T(8,128)(2,1)} %grad_far.1), custom_call_target="tpu_custom_call" | custom-call | flops 2000000000 | bytes 4194304 | tf_op jit(solution)/shard_map/pallas_call | solution.py:583
  14.7 0.6 %collective-permute-done.1.got = bf16[16,16,128]{2,1,0:T(8,128)(2,1)S(1)} collective-permute-done((bf16[16,16,128]{2,1,0:T(8,128)(2,1)S(1)}, bf16[16,16,128]{2,1,0:T(8,128)(2,1)S(1)}, u32[]{:S(2)}, u32[]{:S(2)}) %collective-permute-start.1) | collective-permute-done | bytes 65568 | tf_op jit(solution)/shard_map/ppermute | solution.py:602
  15.2 0.3 shard_map.81
  15.5 2.7 %collective-permute-start.2 = (bf16[16,16,128]{2,1,0:T(8,128)(2,1)S(1)}, bf16[16,16,128]{2,1,0:T(8,128)(2,1)S(1)}, u32[]{:S(2)}, u32[]{:S(2)}) collective-permute-start(bf16[16,16,128]{2,1,0:T(8,128)(2,1)S(1)} %get-tuple-element.59), channel_id=1, source_target_pairs={{0,16},{4,20},{8,24},{12,28},{16,0},{20,4},{24,8},{28,12},{1,17},{... | collective-permute-start | bytes 196616 | tf_op jit(solution)/shard_map/ppermute | solution.py:602
  18.2 2.4 %shard_map.82 = (f32[128,16,128]{2,1,0:T(8,128)S(1)}, f32[2,8,16,128]{3,2,1,0:T(8,128)}) custom-call(f32[2,128,16,128]{3,2,1,0:T(8,128)S(1)} %copy-done, f32[2,8,16,128]{3,2,1,0:T(8,128)S(1)} %get-tuple-element.61.first_rows, f32[3,16,16,128]{3,2,1,0:T(8,128)S(1)} %get-tuple-element.48.table), custom_call_target="tpu_custom_call" | custom-call | flops 2000000000 | bytes 4194304 | tf_op jit(solution)/shard_map/pallas_call | solution.py:583
  20.5 0.2 collective-permute-done.2.got
  20.7 0.3 shard_map.83
  21.0 1.6 %collective-permute-start.3 = (bf16[16,16,128]{2,1,0:T(8,128)(2,1)S(1)}, bf16[16,16,128]{2,1,0:T(8,128)(2,1)S(1)}, u32[]{:S(2)}, u32[]{:S(2)}) collective-permute-start(bf16[16,16,128]{2,1,0:T(8,128)(2,1)S(1)} %get-tuple-element.65), channel_id=1, source_target_pairs={{0,4},{4,0},{8,12},{12,8},{16,20},{20,16},{24,28},{28,24},{1,5},{5... | collective-permute-start | bytes 196616 | tf_op jit(solution)/shard_map/ppermute | solution.py:602
  22.6 2.7 %collective-permute-done.3.received = bf16[16,16,128]{2,1,0:T(8,128)(2,1)S(1)} collective-permute-done((bf16[16,16,128]{2,1,0:T(8,128)(2,1)S(1)}, bf16[16,16,128]{2,1,0:T(8,128)(2,1)S(1)}, u32[]{:S(2)}, u32[]{:S(2)}) %collective-permute-start.3) | collective-permute-done | bytes 65568 | tf_op jit(solution)/shard_map/ppermute | solution.py:602
  25.4 1.7 %shard_map.84 = (f32[128,16,128]{2,1,0:T(8,128)S(1)}, f32[2,128]{1,0:T(2,128)S(1)}) custom-call(f32[16,16,128]{2,1,0:T(8,128)S(1)} %get-tuple-element.64.entering, bf16[16,16,128]{2,1,0:T(8,128)(2,1)S(1)} %collective-permute-done.3.received, f32[3,16,16,128]{3,2,1,0:T(8,128)S(1)} %get-tuple-element.48.table, ...), custom_call_target="tpu_custom_call", output_to_operand_aliasing={{0}: (4, {})} | custom-call | bytes 4194304 | tf_op jit(solution)/shard_map/pallas_call | solution.py:583
  27.1 5.7 %psum.7.sums = f32[2,128]{1,0:T(2,128)S(1)} all-reduce(f32[2,128]{1,0:T(2,128)S(1)} %get-tuple-element.69), channel_id=1, replica_groups=mesh['ctx'=8,'tp'=4] {'tp'}, use_global_device_ids=true, to_apply=%region_0.0 | all-reduce | flops 256 | bytes 2048 | tf_op jit(solution)/shard_map/psum | solution.py:710
  32.7 2.2 %shard_map.85 = (f32[128,16,128]{2,1,0:T(8,128)S(1)}, f32[128,16,128]{2,1,0:T(8,128)S(1)}, f32[16,16,128]{2,1,0:T(8,128)S(1)}, bf16[16,16,128]{2,1,0:T(8,128)(2,...) custom-call(f32[2,128]{1,0:T(2,128)S(1)} %psum.7.sums, ...), custom_call_target="tpu_custom_call", output_to_operand_aliasing={{0}: (4, {})} | custom-call | bytes 4194304 | tf_op jit(solution)/shard_map/pallas_call | solution.py:583
  34.9 1.6 %collective-permute-start.4 = (bf16[16,16,128]{2,1,0:T(8,128)(2,1)S(1)}, bf16[16,16,128]{2,1,0:T(8,128)(2,1)S(1)}, u32[]{:S(2)}, u32[]{:S(2)}) collective-permute-start(bf16[16,16,128]{2,1,0:T(8,128)(2,1)S(1)} %get-tuple-element.78), channel_id=1, source_target_pairs={{0,8},{4,12},{8,0},{12,4},{16,24},{20,28},{24,16},{28,20},{1,9},{5... | collective-permute-start | bytes 196616 | tf_op jit(solution)/shard_map/ppermute | solution.py:602
  36.5 2.3 %shard_map.87.local = f32[128,16,128]{2,1,0:T(8,128)S(1)} custom-call(f32[3,16,16,128]{3,2,1,0:T(8,128)S(1)} %get-tuple-element.48.table, f32[128,16,128]{2,1,0:T(8,128)S(1)} %get-tuple-element.79.long_grad), custom_call_target="tpu_custom_call" | custom-call | flops 2000000000 | bytes 4194304 | tf_op jit(solution)/shard_map/pallas_call | solution.py:583
  38.8 0.4 collective-permute-done.4.got
  39.2 0.3 shard_map.88
  39.6 2.8 %collective-permute-start.5 = (bf16[22,16,128]{2,1,0:T(8,128)(2,1)S(1)}, bf16[22,16,128]{2,1,0:T(8,128)(2,1)S(1)}, u32[]{:S(2)}, u32[]{:S(2)}) collective-permute-start(bf16[22,16,128]{2,1,0:T(8,128)(2,1)S(1)} %get-tuple-element.85), channel_id=1, source_target_pairs={{0,16},{4,20},{8,24},{12,28},{16,0},{20,4},{24,8},{28,12},{1,17},{... | collective-permute-start | bytes 270344 | tf_op jit(solution)/shard_map/ppermute | solution.py:602
  42.4 1.7 %shard_map.86 = (bf16[128,2048]{1,0:T(8,128)(2,1)}, bf16[128,2048]{1,0:T(8,128)(2,1)S(1)}, f32[128,128]{1,0:T(8,128)S(1)}, bf16[4,6,16,128]{3,2,1,0:T(8,128)(2,1)S(1)}) custom-call(f32[128,128]{1,0:T(8,128)S(1)} %get-tuple-element.72.inv, f32[3,7,16,128]{3,2,1,0:T(8,128)S(1)} %copy-done.3, f32[16,128]{1,0:T(8,128)S(1)} %bitcast.4, ...), custom_call_target="tpu_custom_call" | custom-call | flops 2000000000 | bytes 4194304 | tf_op jit(solution)/shard_map/pallas_call | solution.py:583
  44.1 1.3 %collective-permute-start.7 = (bf16[4,6,16,128]{3,2,1,0:T(8,128)(2,1)S(1)}, bf16[4,6,16,128]{3,2,1,0:T(8,128)(2,1)S(1)}, u32[]{:S(2)}, u32[]{:S(2)}) collective-permute-start(bf16[4,6,16,128]{3,2,1,0:T(8,128)(2,1)S(1)} %get-tuple-element.93), channel_id=1, source_target_pairs={{4,0},{8,4},{12,8},{16,12},{20,16},{24,20},{28,24},{5,1},{9,5},{13... | collective-permute-start | bytes 294920 | tf_op jit(solution)/shard_map/ppermute | solution.py:598
  45.4 1.3 %collective-permute-done.5.got = bf16[22,16,128]{2,1,0:T(8,128)(2,1)S(1)} collective-permute-done((bf16[22,16,128]{2,1,0:T(8,128)(2,1)S(1)}, bf16[22,16,128]{2,1,0:T(8,128)(2,1)S(1)}, u32[]{:S(2)}, u32[]{:S(2)}) %collective-permute-start.5) | collective-permute-done | bytes 90144 | tf_op jit(solution)/shard_map/ppermute | solution.py:602
  46.7 0.4 shard_map.89
  47.1 1.4 %collective-permute-start.6 = (bf16[22,16,128]{2,1,0:T(8,128)(2,1)S(1)}, bf16[22,16,128]{2,1,0:T(8,128)(2,1)S(1)}, u32[]{:S(2)}, u32[]{:S(2)}) collective-permute-start(bf16[22,16,128]{2,1,0:T(8,128)(2,1)S(1)} %get-tuple-element.89), channel_id=1, source_target_pairs={{0,4},{4,0},{8,12},{12,8},{16,20},{20,16},{24,28},{28,24},{1,5},{5... | collective-permute-start | bytes 270344 | tf_op jit(solution)/shard_map/ppermute | solution.py:602
  48.5 2.5 %collective-permute-done.7.head = bf16[4,6,16,128]{3,2,1,0:T(8,128)(2,1)S(1)} collective-permute-done((bf16[4,6,16,128]{3,2,1,0:T(8,128)(2,1)S(1)}, bf16[4,6,16,128]{3,2,1,0:T(8,128)(2,1)S(1)}, u32[]{:S(2)}, u32[]{:S(2)}) %collective-permute-start.7) | collective-permute-done | bytes 98336 | tf_op jit(solution)/shard_map/ppermute | solution.py:598
  51.0 1.0 %collective-permute-done.6.received = bf16[22,16,128]{2,1,0:T(8,128)(2,1)S(1)} collective-permute-done((bf16[22,16,128]{2,1,0:T(8,128)(2,1)S(1)}, bf16[22,16,128]{2,1,0:T(8,128)(2,1)S(1)}, u32[]{:S(2)}, u32[]{:S(2)}) %collective-permute-start.6) | collective-permute-done | bytes 90144 | tf_op jit(solution)/shard_map/ppermute | solution.py:602
  51.9 3.5 %shard_map.90 = bf16[3,128,2048]{2,1,0:T(8,128)(2,1)} custom-call(f32[16,16,128]{2,1,0:T(8,128)S(1)} %get-tuple-element.88.entering, bf16[22,16,128]{2,1,0:T(8,128)(2,1)S(1)} %collective-permute-done.6.received, f32[3,16,16,128]{3,2,1,0:T(8,128)S(1)} %get-tuple-element.48.table, f32[3,7,16,128]{3,2,1,0:T(8,128)S(1)} %copy-done.3, ...), custom_call_target="tpu_custom_call" | custom-call | bytes 4194304 | tf_op jit(solution)/shard_map/pallas_call | solution.py:583
  (9 shorter events, 0.0 us)
Async XLA Ops:
  1.6 9.0 %collective-permute-start = (bf16[3,8,2048]{2,1,0:T(8,128)(2,1)S(1)}, bf16[3,8,2048]{2,1,0:T(8,128)(2,1)S(1)}, u32[]{:S(2)}, u32[]{:S(2)}) collective-permute-start(bf16[3,8,2048]{2,1,0:T(8,128)(2,1)S(1)} %shard_map.78), channel_id=1, source_target_pairs={{0,4},{4,8},{8,12},{12,16},{16,20},{20,24},{24,28},{1,5},{5,9},{9,... | collective-permute-start | bytes 294920 | tf_op jit(solution)/shard_map/ppermute | solution.py:598
  6.4 6.1 %copy-start.4 = (f32[2048]{0:T(1024)S(1)}, f32[2048]{0:T(1024)}, u32[]{:S(2)}) copy-start(f32[2048]{0:T(1024)} %param.10) | copy-start | bytes 24580
  10.9 4.3 %collective-permute-start.1 = (bf16[16,16,128]{2,1,0:T(8,128)(2,1)S(1)}, bf16[16,16,128]{2,1,0:T(8,128)(2,1)S(1)}, u32[]{:S(2)}, u32[]{:S(2)}) collective-permute-start(bf16[16,16,128]{2,1,0:T(8,128)(2,1)S(1)} %get-tuple-element.53), channel_id=1, source_target_pairs={{0,8},{4,12},{8,0},{12,4},{16,24},{20,28},{24,16},{28,20},{1,9},{5... | collective-permute-start | bytes 196616 | tf_op jit(solution)/shard_map/ppermute | solution.py:602
  12.5 5.6 %copy-start = (f32[2,128,16,128]{3,2,1,0:T(8,128)S(1)}, f32[2,128,16,128]{3,2,1,0:T(8,128)}, u32[]{:S(2)}) copy-start(f32[2,128,16,128]{3,2,1,0:T(8,128)} %get-tuple-element.60.pair) | copy-start | bytes 6291460
  15.5 5.2 %collective-permute-start.2 = (bf16[16,16,128]{2,1,0:T(8,128)(2,1)S(1)}, bf16[16,16,128]{2,1,0:T(8,128)(2,1)S(1)}, u32[]{:S(2)}, u32[]{:S(2)}) collective-permute-start(bf16[16,16,128]{2,1,0:T(8,128)(2,1)S(1)} %get-tuple-element.59), channel_id=1, source_target_pairs={{0,16},{4,20},{8,24},{12,28},{16,0},{20,4},{24,8},{28,12},{1,17},{... | collective-permute-start | bytes 196616 | tf_op jit(solution)/shard_map/ppermute | solution.py:602
  21.0 4.3 %collective-permute-start.3 = (bf16[16,16,128]{2,1,0:T(8,128)(2,1)S(1)}, bf16[16,16,128]{2,1,0:T(8,128)(2,1)S(1)}, u32[]{:S(2)}, u32[]{:S(2)}) collective-permute-start(bf16[16,16,128]{2,1,0:T(8,128)(2,1)S(1)} %get-tuple-element.65), channel_id=1, source_target_pairs={{0,4},{4,0},{8,12},{12,8},{16,20},{20,16},{24,28},{28,24},{1,5},{5... | collective-permute-start | bytes 196616 | tf_op jit(solution)/shard_map/ppermute | solution.py:602
  34.9 4.3 %collective-permute-start.4 = (bf16[16,16,128]{2,1,0:T(8,128)(2,1)S(1)}, bf16[16,16,128]{2,1,0:T(8,128)(2,1)S(1)}, u32[]{:S(2)}, u32[]{:S(2)}) collective-permute-start(bf16[16,16,128]{2,1,0:T(8,128)(2,1)S(1)} %get-tuple-element.78), channel_id=1, source_target_pairs={{0,8},{4,12},{8,0},{12,4},{16,24},{20,28},{24,16},{28,20},{1,9},{5... | collective-permute-start | bytes 196616 | tf_op jit(solution)/shard_map/ppermute | solution.py:602
  36.5 5.9 %copy-start.3 = (f32[3,7,16,128]{3,2,1,0:T(8,128)S(1)}, f32[3,7,16,128]{3,2,1,0:T(8,128)}, u32[]{:S(2)}) copy-start(f32[3,7,16,128]{3,2,1,0:T(8,128)} %get-tuple-element.73.taps) | copy-start | bytes 516100
  39.6 7.1 %collective-permute-start.5 = (bf16[22,16,128]{2,1,0:T(8,128)(2,1)S(1)}, bf16[22,16,128]{2,1,0:T(8,128)(2,1)S(1)}, u32[]{:S(2)}, u32[]{:S(2)}) collective-permute-start(bf16[22,16,128]{2,1,0:T(8,128)(2,1)S(1)} %get-tuple-element.85), channel_id=1, source_target_pairs={{0,16},{4,20},{8,24},{12,28},{16,0},{20,4},{24,8},{28,12},{1,17},{... | collective-permute-start | bytes 270344 | tf_op jit(solution)/shard_map/ppermute | solution.py:602
  42.4 9.5 %copy-start.1 = (f32[2,128,16,128]{3,2,1,0:T(8,128)S(1)}, f32[2,128,16,128]{3,2,1,0:T(8,128)}, u32[]{:S(2)}) copy-start(f32[2,128,16,128]{3,2,1,0:T(8,128)} %get-tuple-element.60.pair) | copy-start | bytes 6291460
  42.4 9.5 %copy-start.2 = (f32[2,8,16,128]{3,2,1,0:T(8,128)S(1)}, f32[2,8,16,128]{3,2,1,0:T(8,128)}, u32[]{:S(2)}) copy-start(f32[2,8,16,128]{3,2,1,0:T(8,128)} %get-tuple-element.71.rows_far.first_rows) | copy-start | bytes 393220
  44.1 6.8 %collective-permute-start.7 = (bf16[4,6,16,128]{3,2,1,0:T(8,128)(2,1)S(1)}, bf16[4,6,16,128]{3,2,1,0:T(8,128)(2,1)S(1)}, u32[]{:S(2)}, u32[]{:S(2)}) collective-permute-start(bf16[4,6,16,128]{3,2,1,0:T(8,128)(2,1)S(1)} %get-tuple-element.93), channel_id=1, source_target_pairs={{4,0},{8,4},{12,8},{16,12},{20,16},{24,20},{28,24},{5,1},{9,5},{13... | collective-permute-start | bytes 294920 | tf_op jit(solution)/shard_map/ppermute | solution.py:598
  47.1 4.8 %collective-permute-start.6 = (bf16[22,16,128]{2,1,0:T(8,128)(2,1)S(1)}, bf16[22,16,128]{2,1,0:T(8,128)(2,1)S(1)}, u32[]{:S(2)}, u32[]{:S(2)}) collective-permute-start(bf16[22,16,128]{2,1,0:T(8,128)(2,1)S(1)} %get-tuple-element.89), channel_id=1, source_target_pairs={{0,4},{4,0},{8,12},{12,8},{16,20},{20,16},{24,28},{28,24},{1,5},{5... | collective-permute-start | bytes 270344 | tf_op jit(solution)/shard_map/ppermute | solution.py:602

commit v5 on v4

--- a/solution.py
+++ b/solution.py
@@ -33,8 +33,10 @@
         target[pl.ds(first + lb * pitch, rows), :] = tile.astype(jnp.float32)
 
 
-def to_send(table, half, states, lag):
+def to_send(table, half, states, lag, dtype):
     modes = table.shape[1]
+    if dtype != jnp.bfloat16:
+        return states
     down, off_down, up, off_up, chosen, off = [], [], [], [], [], []
     for m in range(modes):
         x = states[m]
@@ -188,7 +190,7 @@
             fade = jnp.exp(table[2, m, half, :] * -float(rows - reach))
             states.append(ends[m, half, :] + fade * state)
             state_out[m, half, :] = states[m]
-        for m, value in enumerate(to_send(table, half, states, rows)):
+        for m, value in enumerate(to_send(table, half, states, rows // 2, message.dtype)):
             message[m, half, :] = value
 
 
@@ -249,15 +251,15 @@
     store.wait()
 
 
-def carry_kernel(entering, received, table, query, local, scaled, long_conv, sums, sq, cr):
+def carry_kernel(span, place, entering, got, table, query, local, scaled, long_conv, sums, sq, cr):
     rows = local.shape[0]
     modes, lane_blocks = table.shape[1:3]
     for h, half in enumerate(halves(lane_blocks)):
         decay = [table[0, m, half, :] for m in range(modes)]
         start = []
         for m in range(modes):
-            fade = jnp.exp(table[2, m, half, :] * -float(rows))
-            incoming = fade * entering[m, half, :] + received[m, half, :].astype(jnp.float32)
+            other = got[m, half, :].astype(jnp.float32)
+            incoming = entering[m, half, :] + joined_term(rows, span, place, table[2, m, half, :], other)
             start.append(table[1, m, half, :] * decay[m] * incoming)
 
         def block_step(block, state):
@@ -334,12 +336,13 @@
                 )
                 for i, value in enumerate(found):
                     head[i, t, half, :] = value
-        for m, value in enumerate(to_send(table, half, state, rows)):
+        for m, value in enumerate(to_send(table, half, state, rows // 2, message.dtype)):
             state_out[m, half, :] = state[m]
             message[m, half, :] = value
 
 
-def back_kernel(table, long_grad, local):
+def back_kernel(table, long_grad, head_in, local, head):
+    head[...] = head_in[...].astype(head.dtype)
     rows = long_grad.shape[0]
     modes, lane_blocks = table.shape[1:3]
     blocks = rows // SUB
@@ -358,8 +361,7 @@
 
         lax.fori_loop(0, blocks, block_step, (zero,) * modes)
 
-def output_kernel(inv, taps, gain, query, long_conv, mixed, head_in, output, finished, last, head, os, qs):
-    head[...] = head_in[...].astype(head.dtype)
+def output_kernel(inv, taps, gain, query, long_conv, mixed, output, finished, last, os, qs):
     rows = long_conv.shape[0]
     lane_blocks = taps.shape[2]
     tap_count = taps.shape[1]
@@ -391,12 +393,12 @@
         last[pl.ds(lb * SUB, SUB), :] = qs[pl.ds(lb * pitch + rows - SUB, SUB), :]
 
 
-def far_rows(table, half, state, rows, reach, fade_first):
+def far_rows(table, half, state, rows, reach):
     modes = table.shape[1]
     at = [
         table[1, m, half, :]
         * state[m]
-        * jnp.exp(table[2, m, half, :] * -float(rows - reach + 1 + fade_first))
+        * jnp.exp(table[2, m, half, :] * -float(rows - reach + 1))
         for m in range(modes)
     ]
     found = [None] * reach
@@ -407,88 +409,141 @@
     return found
 
 
-def join_kernel(rows, span, last, place, table, state, entering, gathered, got, entering_out, message, *gathered_out):
+def gather_kernel(rows, place, table, state, first, second, third, entering, message, *whole):
     modes, lane_blocks = state.shape[:2]
-    column = lax.div(place[0], 2)
-    upper = jnp.full((SUB, LANES), lax.rem(lax.div(column, span), 2)) > 0
-    offset = lax.rem(column, span).astype(jnp.float32) * float(2 * rows)
-    is_lower = jnp.full((SUB, LANES), lax.rem(place[0], 2)) == 0
+    inside = lax.rem(place[0], 4)
     for half in halves(lane_blocks):
         sent = []
         for m in range(modes):
             rate = table[2, m, half, :]
-            other = got[m, half, :].astype(jnp.float32)
-            e = jnp.where(upper, jnp.exp(rate * -offset) * other, 0.0)
-            if span > 1:
-                e = entering[m, half, :] + e
-            entering_out[m, half, :] = e
-            if last:
-                joined = jnp.exp(rate * -float(2 * rows)) * e + state[m, half, :]
-                sent.append(jnp.where(is_lower, joined, e))
-            else:
-                mine = gathered[m, half, :]
-                fade = jnp.exp(rate * -float(2 * rows * span))
-                sent.append(jnp.where(upper, mine, other) + fade * jnp.where(upper, other, mine))
-                gathered_out[0][m, half, :] = sent[m]
-        for m, value in enumerate(to_send(table, half, sent, rows // 2 if last else rows)):
+            found = None
+            at_end = jnp.exp(rate * -steps(3 - inside, rows)) * state[m, half, :]
+            for k, got in enumerate((first, second, third)):
+                other = got[m, half, :].astype(jnp.float32)
+                other_inside = inside ^ (k + 1)
+                at_end = at_end + jnp.exp(rate * -steps(3 - other_inside, rows)) * other
+                ahead = inside - other_inside
+                term = jnp.where(above(ahead, 0), jnp.exp(rate * -steps(ahead - 1, rows)) * other, 0.0)
+                found = term if found is None else found + term
+            entering[m, half, :] = found
+            sent.append(at_end)
+            if whole:
+                whole[0][m, half, :] = at_end
+        for m, value in enumerate(to_send(table, half, sent, rows // 2, message.dtype)):
             message[m, half, :] = value
 
 
+def join_kernel(rows, span, place, table, entering, whole, got, entering_out, message, whole_out):
+    modes, lane_blocks = entering.shape[:2]
+    upper = above(lax.rem(lax.div(place[0], span), 2), 0)
+    for half in halves(lane_blocks):
+        sent = []
+        for m in range(modes):
+            rate = table[2, m, half, :]
+            other, mine = got[m, half, :].astype(jnp.float32), whole[m, half, :]
+            entering_out[m, half, :] = entering[m, half, :] + joined_term(rows, span, place, rate, other)
+            fade = jnp.exp(rate * -float(rows * span))
+            sent.append(jnp.where(upper, mine, other) + fade * jnp.where(upper, other, mine))
+            whole_out[m, half, :] = sent[m]
+        for m, value in enumerate(to_send(table, half, sent, rows // 2, message.dtype)):
+            message[m, half, :] = value
+
+
+def steps(shards, rows):
+    return jnp.maximum(shards, 0).astype(jnp.float32) * float(rows)
+
+
+def above(value, bound):
+    return jnp.full((SUB, LANES), value) > bound
+
+
+def joined_term(rows, span, place, rate, other):
+    upper = above(lax.rem(lax.div(place[0], span), 2), 0)
+    return jnp.where(upper, jnp.exp(rate * -steps(lax.rem(place[0], span), rows)) * other, 0.0)
+
+
+def joined_back_terms(rows, span, place, rate, other):
+    lower = ~above(lax.rem(lax.div(place[0], span), 2), 0)
+    to_end = span - 1 - lax.rem(place[0], span)
+    here = jnp.where(lower, jnp.exp(rate * -steps(to_end, rows)) * other, 0.0)
+    onward = jnp.where(lower & above(to_end, 0), jnp.exp(rate * -steps(to_end - 1, rows)) * other, 0.0)
+    return here, onward
+
+
+def joined_rows(span, place, other):
+    lower = ~above(lax.rem(lax.div(place[0], span), 2), 0)
+    at_end = ~above(span - 1 - lax.rem(place[0], span), 0)
+    return jnp.where(lower & at_end, other, 0.0)
+
+
+def gather_back_kernel(rows, reach, place, table, state, first, second, third, entering, beyond, added, message, *whole):
+    modes, lane_blocks = state.shape[:2]
+    inside = lax.rem(place[0], 4)
+    for half in halves(lane_blocks):
+        sent, rest = [], []
+        for m in range(modes):
+            rate = table[2, m, half, :]
+            mine = state[m, half, :]
+            at_start = jnp.exp(rate * -steps(inside, rows)) * mine
+            after_first = jnp.where(above(inside, 0), jnp.exp(rate * -steps(inside - 1, rows)) * mine, 0.0)
+            here = onward = jnp.zeros((SUB, LANES), jnp.float32)
+            for k, got in enumerate((first, second, third)):
+                other = got[m, half, :].astype(jnp.float32)
+                other_inside = inside ^ (k + 1)
+                at_start = at_start + jnp.exp(rate * -steps(other_inside, rows)) * other
+                after_first = after_first + jnp.where(
+                    above(other_inside, 0), jnp.exp(rate * -steps(other_inside - 1, rows)) * other, 0.0
+                )
+                ahead = other_inside - inside
+                here = here + jnp.where(above(ahead, 0), jnp.exp(rate * -steps(ahead - 1, rows)) * other, 0.0)
+                onward = onward + jnp.where(above(ahead, 1), jnp.exp(rate * -steps(ahead - 2, rows)) * other, 0.0)
+            entering[m, half, :] = here
+            beyond[m, half, :] = onward
+            sent.append(at_start)
+            rest.append(after_first)
+            if whole:
+                whole[0][m, half, :] = at_start
+        for m, value in enumerate(to_send(table, half, sent, rows // 2, message.dtype)):
+            message[m, half, :] = value
+        found = far_rows(table, half, rest, rows, reach)
+        for i in range(reach):
+            added[i, half, :] = jnp.zeros((SUB, LANES), jnp.float32)
+            message[modes + i, half, :] = found[i].astype(message.dtype)
+            if whole:
+                whole[0][modes + i, half, :] = found[i]
+
+
 def join_back_kernel(
-    rows, reach, span, last, place, table, state, entering, beyond, added, gathered, got,
-    entering_out, message, *kept_out,
+    rows, reach, span, place, table, entering, beyond, added, whole, got,
+    entering_out, beyond_out, added_out, message, whole_out,
 ):
-    modes, lane_blocks = state.shape[:2]
-    column = lax.div(place[0], 2)
-    within = lax.rem(column, span)
-    upper = jnp.full((SUB, LANES), lax.rem(lax.div(column, span), 2)) > 0
-    is_last = jnp.full((SUB, LANES), within) == span - 1
-    to_end = (span - 1 - within).astype(jnp.float32) * float(2 * rows)
-    is_lower = jnp.full((SUB, LANES), lax.rem(place[0], 2)) == 0
+    modes, lane_blocks = entering.shape[:2]
+    upper = above(lax.rem(lax.div(place[0], span), 2), 0)
     for half in halves(lane_blocks):
-        sent, far_on = [], []
+        sent, rest = [], []
         for m in range(modes):
             rate = table[2, m, half, :]
-            other = got[m, half, :].astype(jnp.float32)
-            e, f = jnp.where(upper, 0.0, jnp.exp(rate * -to_end) * other), jnp.zeros((SUB, LANES), jnp.float32)
-            if span > 1:
-                e = entering[m, half, :] + e
-                onward = jnp.exp(rate * -jnp.maximum(to_end - float(2 * rows), 0.0)) * other
-                f = beyond[m, half, :] + jnp.where(upper | is_last, 0.0, onward)
-            entering_out[m, half, :] = e
-            if not last:
-                kept_out[0][m, half, :] = f
-            if last:
-                joined = jnp.exp(rate * -float(2 * rows)) * e + state[m, half, :]
-                sent.append(jnp.where(is_lower, e, joined))
-                far_on.append(jnp.where(is_lower, f, e))
-            else:
-                mine = gathered[m, half, :]
-                low, high = jnp.where(upper, other, mine), jnp.where(upper, mine, other)
-                fade = jnp.exp(rate * -float(2 * rows * span))
-                sent.append(low + fade * high)
-                kept_out[2][m, half, :] = sent[m]
-                fade = jnp.exp(rate * -float(2 * rows * (span - 1)))
-                far_on.append(fade * high)
-        for m, value in enumerate(to_send(table, half, sent, rows // 2 if last else rows)):
+            other, mine = got[m, half, :].astype(jnp.float32), whole[m, half, :]
+            here, onward = joined_back_terms(rows, span, place, rate, other)
+            entering_out[m, half, :] = entering[m, half, :] + here
+            beyond_out[m, half, :] = beyond[m, half, :] + onward
+            low, high = jnp.where(upper, other, mine), jnp.where(upper, mine, other)
+            sent.append(low + jnp.exp(rate * -float(rows * span)) * high)
+            rest.append(jnp.exp(rate * -float(rows * (span - 1))) * high)
+            whole_out[m, half, :] = sent[m]
+        for m, value in enumerate(to_send(table, half, sent, rows // 2, message.dtype)):
             message[m, half, :] = value
-        found = far_rows(table, half, far_on, rows, reach, rows)
+        found = far_rows(table, half, rest, rows, reach)
         for i in range(reach):
-            here, rest = jnp.zeros((SUB, LANES), jnp.float32), found[i]
-            if span > 1:
-                mine, other = gathered[modes + i, half, :], got[modes + i, half, :].astype(jnp.float32)
-                here = added[i, half, :] + jnp.where(upper | ~is_last, 0.0, other)
-                rest = rest + jnp.where(upper, other, mine)
-            if last:
-                message[modes + i, half, :] = (found[i] + jnp.where(is_lower, here, 0.0)).astype(message.dtype)
-            else:
-                message[modes + i, half, :] = rest.astype(message.dtype)
-                kept_out[1][i, half, :] = here
-                kept_out[2][modes + i, half, :] = rest
+            other, mine = got[modes + i, half, :].astype(jnp.float32), whole[modes + i, half, :]
+            added_out[i, half, :] = added[i, half, :] + joined_rows(span, place, other)
+            value = jnp.where(upper, other, mine) + found[i]
+            message[modes + i, half, :] = value.astype(message.dtype)
+            whole_out[modes + i, half, :] = value
 
 
 def final_kernel(
-    entering, received, table, taps, pair, first_rows, local, query, last, head, grads, cg, os, ls, made, edge, sems
+    span, place, entering, beyond_in, added, got, table, taps, pair, first_rows, local, query, last, head, grads, cg, os, ls, made, edge, sems
 ):
     rows = local.shape[0]
     modes, lane_blocks = table.shape[1:3]
@@ -506,11 +561,12 @@
     ls[...] = last[...]
     for h, half in enumerate(halves(lane_blocks)):
         decay = [table[0, m, half, :] for m in range(modes)]
-        start = []
-        for m in range(modes):
-            fade = jnp.exp(table[2, m, half, :] * -float(rows))
-            incoming = fade * entering[m, half, :] + received[m, half, :].astype(jnp.float32)
-            start.append(table[1, m, half, :] * decay[m] * incoming)
+        start, onward = [], []
+        for m in range(modes):
+            other = got[m, half, :].astype(jnp.float32)
+            here, later = joined_back_terms(rows, span, place, table[2, m, half, :], other)
+            start.append(table[1, m, half, :] * decay[m] * (entering[m, half, :] + here))
+            onward.append(beyond_in[m, half, :] + later)
 
         def block_step(source, block, state):
             for k in range(SUB):
@@ -523,16 +579,17 @@
 
         state = lax.fori_loop(0, blocks - 1, functools.partial(block_step, pair), tuple(start))
         block_step(first_rows, blocks - 1, state)
-        own = far_rows(table, half, [entering[m, half, :] for m in range(modes)], rows, reach, 0)
+        own = far_rows(table, half, onward, rows, reach)
         beyond = [[], [], []]
         for i in range(reach):
-            gated = head[1, i, half, :].astype(jnp.float32) + received[modes + i, half, :].astype(jnp.float32) + own[i]
+            rows_there = joined_rows(span, place, got[modes + i, half, :].astype(jnp.float32))
+            gated = head[1, i, half, :].astype(jnp.float32) + own[i] + added[i, half, :] + rows_there
             beyond[0].append(head[0, i, half, :].astype(jnp.float32))
             beyond[1].append(gated * head[2, i, half, :].astype(jnp.float32))
             beyond[2].append(gated * head[3, i, half, :].astype(jnp.float32))
         for t in range(SUB - reach, SUB):
-            place = pl.ds(h * SUB * SUB + t, SUB, stride=SUB)
-            ls[place, :] += total(
+            edge_rows = pl.ds(h * SUB * SUB + t, SUB, stride=SUB)
+            ls[edge_rows, :] += total(
                 taps[0, i, half, :] * beyond[0][t + i - SUB] for i in range(SUB - t, tap_count)
             )
         for s in range(1, 3):
@@ -613,6 +670,8 @@
     row_shape = (rows, lane_blocks, LANES)
     state_shape = (modes, lane_blocks, LANES)
     bf16 = jnp.bfloat16
+    single = count <= 8
+    wire = bf16 if single else jnp.float32
 
     def v(*arrays):
         return [(a, pltpu.VMEM) for a in arrays]
@@ -654,7 +713,7 @@
     first_rows, state, message = run(
         functools.partial(head_kernel, rows),
         v(first_rows, halo, table, taps, ends),
-        [kept(2, SUB, lane_blocks, LANES), kept(*state_shape), jax.ShapeDtypeStruct(state_shape, bf16)],
+        [kept(2, SUB, lane_blocks, LANES), kept(*state_shape), jax.ShapeDtypeStruct(state_shape, wire)],
         ((2 * lane_blocks * SUB, LANES),),
     )
     place = lax.axis_index("ctx").astype(jnp.int32)[None]
@@ -679,33 +738,31 @@
         (pltpu.SemaphoreType.DMA(()),),
         work=2 * 10**9,
     )
-    entering = gathered = state
-    span = 1
+    got = [swapped(message, k) for k in (1, 2, 3)]
+    *got, query, scaled = lax.optimization_barrier((*got, query, scaled))
+    entering, message, *whole = run(
+        functools.partial(gather_kernel, rows),
+        [(place, pltpu.SMEM)] + v(table, state, *got),
+        [kept(*state_shape), jax.ShapeDtypeStruct(state_shape, wire)]
+        + ([] if single else [kept(*state_shape)]),
+    )
+    span = 4
+    got = swapped(message, span)
     while 2 * span < count:
-        final = 4 * span >= count
-        got = swapped(message, 2 * span)
-        if span == 1:
-            got, query, scaled = lax.optimization_barrier((got, query, scaled))
-        if final:
-            got, local = lax.optimization_barrier((got, local))
-        entering, message, *more = run(
-            functools.partial(join_kernel, rows, span, final),
-            [(place, pltpu.SMEM)] + v(table, state, entering, gathered, got),
-            [
-                kept(*state_shape),
-                jax.ShapeDtypeStruct(state_shape, bf16),
-            ]
-            + ([] if final else [kept(*state_shape)]),
+        entering, message, *whole = run(
+            functools.partial(join_kernel, rows, span),
+            [(place, pltpu.SMEM)] + v(table, entering, *whole, got),
+            [kept(*state_shape), jax.ShapeDtypeStruct(state_shape, wire), kept(*state_shape)],
         )
-        gathered = None if final else more[0]
         span *= 2
-    received = swapped(message, 1)
+        got = swapped(message, span)
+    got, local = lax.optimization_barrier((got, local))
     long_conv, sums = run(
-        carry_kernel,
-        v(entering, received, table, query, local, scaled),
+        functools.partial(carry_kernel, span),
+        [(place, pltpu.SMEM)] + v(entering, got, table, query, local, scaled),
         [kept(*row_shape), kept(2, rows)],
         ((rows * SUB, LANES), (rows * SUB, LANES)),
-        aliases={4: 0},
+        aliases={5: 0},
     )
     sums = lax.psum(sums, "tp")
     mixed, long_grad, back, message, inv, head = run(
@@ -715,7 +772,7 @@
             kept(*row_shape),
             kept(*row_shape),
             kept(*state_shape),
-            jax.ShapeDtypeStruct(state_shape, bf16),
+            jax.ShapeDtypeStruct(state_shape, wire),
             kept(rows, LANES),
             kept(4, reach, lane_blocks, LANES),
         ],
@@ -728,51 +785,48 @@
         aliases={4: 0},
     )
 
-    (local_back,) = run(
-        back_kernel, v(table, long_grad), [kept(*row_shape)], work=2 * 10**9
-    )
-    output, finished, last, head = run(
+    local_back, head = run(
+        back_kernel,
+        v(table, long_grad, head),
+        [kept(*row_shape), jax.ShapeDtypeStruct(head.shape, bf16)],
+        work=2 * 10**9,
+    )
+    message_shape = (modes + reach, lane_blocks, LANES)
+    adjoint = [kept(*state_shape), kept(*state_shape), kept(reach, lane_blocks, LANES)]
+    adjoint.append(jax.ShapeDtypeStruct(message_shape, wire))
+    got = [swapped(message, k) for k in (1, 2, 3)]
+    *got, local_back, mixed = lax.optimization_barrier((*got, local_back, mixed))
+    output, finished, last = run(
         output_kernel,
-        v(inv, taps_far, gain, query, long_conv, mixed, head),
+        v(inv, taps_far, gain, query, long_conv, mixed),
         [
             jax.ShapeDtypeStruct((rows, channels), bf16),
             kept(rows, channels, dtype=bf16),
             kept(lane_blocks * SUB, LANES),
-            jax.ShapeDtypeStruct(head.shape, bf16),
         ],
         ((lane_blocks * pitch, LANES), (lane_blocks * pitch, LANES)),
         work=2 * 10**9,
     )
-    entering = beyond = added = gathered = back
-    message_shape = (modes + reach, lane_blocks, LANES)
-    span = 1
+    entering, beyond, added, message, *whole = run(
+        functools.partial(gather_back_kernel, rows, reach),
+        [(place, pltpu.SMEM)] + v(table, back, *got),
+        adjoint + ([] if single else [kept(*message_shape)]),
+    )
+    span = 4
+    got = swapped(message, span)
     while 2 * span < count:
-        final = 4 * span >= count
-        got = swapped(message, 2 * span)
-        if span == 1:
-            got, local_back = lax.optimization_barrier((got, local_back))
-        if final:
-            got, finished = lax.optimization_barrier((got, finished))
-        entering, message, *more = run(
-            functools.partial(join_back_kernel, rows, reach, span, final),
-            [(place, pltpu.SMEM)] + v(table, back, entering, beyond, added, gathered, got),
-            [
-                kept(*state_shape),
-                jax.ShapeDtypeStruct(message_shape, bf16),
-            ]
-            + (
-                []
-                if final
-                else [kept(*state_shape), kept(reach, lane_blocks, LANES), kept(*message_shape)]
-            ),
+        entering, beyond, added, message, *whole = run(
+            functools.partial(join_back_kernel, rows, reach, span),
+            [(place, pltpu.SMEM)] + v(table, entering, beyond, added, *whole, got),
+            adjoint + [kept(*message_shape)],
         )
-        beyond, added, gathered = (None,) * 3 if final else more
         span *= 2
+        got = swapped(message, span)
     head = shifted(head, -1)
-    received = swapped(message, 1)
+    got, finished = lax.optimization_barrier((got, finished))
     (grads,) = run(
-        final_kernel,
-        v(entering, received, table, taps_far, pair_far, rows_far, local_back, finished, last, head),
+        functools.partial(final_kernel, span),
+        [(place, pltpu.SMEM)] + v(entering, beyond, added, got, table, taps_far, pair_far, rows_far, local_back, finished, last, head),
         [pltpu.HBM((3, rows, channels), bf16)],
         (
             (2, rows, SUB, LANES),

time: 55.7 us -> 53.2 us (0.955)
  waiting for transfers between devices: 8.68 us -> 7.06 us
  starting transfers between devices: 17.9 us -> 17.2 us
    ppermute x2, waiting for transfers between devices: 2.48 us -> 0.01 us  [shifted(): return lax.ppermute(block, 'ctx', route)]
    ppermute x6 -> x8, waiting for transfers between devices: 6.2 us -> 7.06 us  [swapped(): lax.ppermute(block, 'ctx', [(i, i ^ distance) for i in range(lax.axis_siz...]
    ppermute x6 -> x8, starting transfers between devices: 11.8 us -> 11 us  [swapped(): lax.ppermute(block, 'ctx', [(i, i ^ distance) for i in range(lax.axis_siz...]
    pallas_call x14 -> x12, Pallas kernels: 22.5 us -> 22.3 us  [run(): pl.pallas_call(kernel, out_shape=outs, in_specs=[pl.BlockSpec(memory_spac...]
  transfers between devices with their start and end apart: 8 -> 10, of which waited for: 7 -> 4; matrix products, arithmetic and copies ran while one was open for 0% -> 0% of each run, Pallas kernels for 23% -> 25%
where the time goes in v5:
time: 53.2 us; the launch traced here: 52.9 us
  Pallas kernels  22.3 us (42%)
  starting transfers between devices  17.2 us (32%)
  waiting for transfers between devices  7.06 us (13%)
  blocking collectives  5.66 us (11%)
  between operations  0.76 us (1%)
    pallas_call x12, Pallas kernels, run(): pl.pallas_call(kernel, out_shape=outs, in_specs=[pl.BlockSpec(memory_spac...  22.3 us
    ppermute x8, starting transfers between devices, swapped(): lax.ppermute(block, 'ctx', [(i, i ^ distance) for i in range(lax.axis_siz...  11 us
    ppermute x8, waiting for transfers between devices, swapped(): lax.ppermute(block, 'ctx', [(i, i ^ distance) for i in range(lax.axis_siz...  7.06 us
    ppermute x2, starting transfers between devices, shifted(): return lax.ppermute(block, 'ctx', route)  6.14 us
    psum x1, blocking collectives, on_device(): sums = lax.psum(sums, 'tp')  5.66 us
  transfers between devices with their start and end apart: 10, of which 4 were waited for; matrix products, arithmetic and copies ran while one was open for 0% of the time, Pallas kernels for 25%

profile of v5, /device:TPU:0, one launch (start us, length us, event | category | flops | bytes accessed | tf_op | source)
XLA Modules:
  0.0 52.9 jit_solution(5300859276307720162)
XLA Ops:
  0.6 0.9 %shard_map.78 = bf16[3,8,2048]{2,1,0:T(8,128)(2,1)S(1)} custom-call(bf16[3,128,2048]{2,1,0:T(8,128)(2,1)} %x_far.3), custom_call_target="tpu_custom_call" | custom-call | bytes 4194304 | tf_op jit(solution)/shard_map/pallas_call | solution.py:640
  1.6 4.8 %collective-permute-start = (bf16[3,8,2048]{2,1,0:T(8,128)(2,1)S(1)}, bf16[3,8,2048]{2,1,0:T(8,128)(2,1)S(1)}, u32[]{:S(2)}, u32[]{:S(2)}) collective-permute-start(bf16[3,8,2048]{2,1,0:T(8,128)(2,1)S(1)} %shard_map.78), channel_id=1, source_target_pairs={{0,4},{4,8},{8,12},{12,16},{16,20},{20,24},{24,28},{1,5},{5,9},{9,... | collective-permute-start | bytes 294920 | tf_op jit(solution)/shard_map/ppermute | solution.py:655
  6.4 0.0 copy-start.4
  6.5 4.1 %shard_map.77 = (f32[2,128,16,128]{3,2,1,0:T(8,128)}, f32[3,7,16,128]{3,2,1,0:T(8,128)}, f32[2,8,16,128]{3,2,1,0:T(8,128)S(1)}, f32[3,16,16,128]{3,2,1,0:T(8,128...) custom-call(bf16[3,128,2048]{2,1,0:T(8,128)(2,1)} %x_far.3, bf16[3,7,128]{2,1,0:T(8,128)(2,1)} %bitcast.5, ...), custom_call_target="tpu_custom_call" | custom-call | flops 1000000000 | bytes 4194304 | tf_op jit(solution)/shard_map/pallas_call | solution.py:640
  10.6 0.0 collective-permute-done.halo
  10.6 0.3 shard_map.79
  10.9 1.6 %collective-permute-start.1 = (bf16[16,16,128]{2,1,0:T(8,128)(2,1)S(1)}, bf16[16,16,128]{2,1,0:T(8,128)(2,1)S(1)}, u32[]{:S(2)}, u32[]{:S(2)}) collective-permute-start(bf16[16,16,128]{2,1,0:T(8,128)(2,1)S(1)} %get-tuple-element.53), channel_id=1, source_target_pairs={{0,4},{4,0},{8,12},{12,8},{16,20},{20,16},{24,28},{28,24},{1,5},{5... | collective-permute-start | bytes 196616 | tf_op jit(solution)/shard_map/ppermute | solution.py:659
  12.5 1.6 %collective-permute-start.2 = (bf16[16,16,128]{2,1,0:T(8,128)(2,1)S(1)}, bf16[16,16,128]{2,1,0:T(8,128)(2,1)S(1)}, u32[]{:S(2)}, u32[]{:S(2)}) collective-permute-start(bf16[16,16,128]{2,1,0:T(8,128)(2,1)S(1)} %get-tuple-element.53), channel_id=1, source_target_pairs={{0,8},{4,12},{8,0},{12,4},{16,24},{20,28},{24,16},{28,20},{1,9},{5... | collective-permute-start | bytes 196616 | tf_op jit(solution)/shard_map/ppermute | solution.py:659
  14.1 0.4 collective-permute-start.3
  14.5 2.1 %shard_map.80 = (f32[128,16,128]{2,1,0:T(8,128)S(1)}, f32[128,16,128]{2,1,0:T(8,128)S(1)}) custom-call(bf16[3,128,2048]{2,1,0:T(8,128)(2,1)} %x_far.3, bf16[3,8,2048]{2,1,0:T(8,128)(2,1)S(1)} %collective-permute-done.halo, f32[3,7,16,128]{3,2,1,0:T(8,128)S(1)} %get-tuple-element.50.taps, f32[16,128]{1,0:T(8,128)S(1)} %bitcast.3, bf16[128,2048]{1,0:T(8,128)(2,1)} %grad_far.1), custom_call_target="tpu_custom_call" | custom-call | flops 2000000000 | bytes 4194304 | tf_op jit(solution)/shard_map/pallas_call | solution.py:640
  16.6 0.0 collective-permute-done.1.first
  16.6 0.4 collective-permute-done.2.second
  17.0 2.3 %collective-permute-done.3.third = bf16[16,16,128]{2,1,0:T(8,128)(2,1)S(1)} collective-permute-done((bf16[16,16,128]{2,1,0:T(8,128)(2,1)S(1)}, bf16[16,16,128]{2,1,0:T(8,128)(2,1)S(1)}, u32[]{:S(2)}, u32[]{:S(2)}) %collective-permute-start.3) | collective-permute-done | bytes 65568 | tf_op jit(solution)/shard_map/ppermute | solution.py:659
  19.3 0.4 shard_map.81
  19.7 1.6 %collective-permute-start.4 = (bf16[16,16,128]{2,1,0:T(8,128)(2,1)S(1)}, bf16[16,16,128]{2,1,0:T(8,128)(2,1)S(1)}, u32[]{:S(2)}, u32[]{:S(2)}) collective-permute-start(bf16[16,16,128]{2,1,0:T(8,128)(2,1)S(1)} %get-tuple-element.60), channel_id=1, source_target_pairs={{0,16},{4,20},{8,24},{12,28},{16,0},{20,4},{24,8},{28,12},{1,17},{... | collective-permute-start | bytes 196616 | tf_op jit(solution)/shard_map/ppermute | solution.py:659
  21.2 2.4 %shard_map.82 = (f32[128,16,128]{2,1,0:T(8,128)S(1)}, f32[2,8,16,128]{3,2,1,0:T(8,128)}) custom-call(f32[2,128,16,128]{3,2,1,0:T(8,128)S(1)} %copy-done, f32[2,8,16,128]{3,2,1,0:T(8,128)S(1)} %get-tuple-element.62.first_rows, f32[3,16,16,128]{3,2,1,0:T(8,128)S(1)} %get-tuple-element.48.table), custom_call_target="tpu_custom_call" | custom-call | flops 2000000000 | bytes 4194304 | tf_op jit(solution)/shard_map/pallas_call | solution.py:640
  23.6 1.9 %collective-permute-done.4.got = bf16[16,16,128]{2,1,0:T(8,128)(2,1)S(1)} collective-permute-done((bf16[16,16,128]{2,1,0:T(8,128)(2,1)S(1)}, bf16[16,16,128]{2,1,0:T(8,128)(2,1)S(1)}, u32[]{:S(2)}, u32[]{:S(2)}) %collective-permute-start.4) | collective-permute-done | bytes 65568 | tf_op jit(solution)/shard_map/ppermute | solution.py:659
  25.5 1.7 %shard_map.83 = (f32[128,16,128]{2,1,0:T(8,128)S(1)}, f32[2,128]{1,0:T(2,128)S(1)}) custom-call(s32[1]{0:T(128)} %bitcast.place, f32[16,16,128]{2,1,0:T(8,128)S(1)} %get-tuple-element.59.entering, bf16[16,16,128]{2,1,0:T(8,128)(2,1)S(1)} %collective-permute-done.4.got, ...), custom_call_target="tpu_custom_call", output_to_operand_aliasing={{0}: (5, {})} | custom-call | bytes 4194304 | tf_op jit(solution)/shard_map/pallas_call | solution.py:640
  27.2 5.7 %psum.7.sums = f32[2,128]{1,0:T(2,128)S(1)} all-reduce(f32[2,128]{1,0:T(2,128)S(1)} %get-tuple-element.68), channel_id=1, replica_groups=mesh['ctx'=8,'tp'=4] {'tp'}, use_global_device_ids=true, to_apply=%region_0.0 | all-reduce | flops 256 | bytes 2048 | tf_op jit(solution)/shard_map/psum | solution.py:767
  32.9 2.2 %shard_map.84 = (f32[128,16,128]{2,1,0:T(8,128)S(1)}, f32[128,16,128]{2,1,0:T(8,128)S(1)}, f32[16,16,128]{2,1,0:T(8,128)S(1)}, bf16[16,16,128]{2,1,0:T(8,128)(2,...) custom-call(f32[2,128]{1,0:T(2,128)S(1)} %psum.7.sums, ...), custom_call_target="tpu_custom_call", output_to_operand_aliasing={{0}: (4, {})} | custom-call | bytes 4194304 | tf_op jit(solution)/shard_map/pallas_call | solution.py:640
  35.0 0.7 %collective-permute-start.5 = (bf16[16,16,128]{2,1,0:T(8,128)(2,1)S(1)}, bf16[16,16,128]{2,1,0:T(8,128)(2,1)S(1)}, u32[]{:S(2)}, u32[]{:S(2)}) collective-permute-start(bf16[16,16,128]{2,1,0:T(8,128)(2,1)S(1)} %get-tuple-element.73), channel_id=1, source_target_pairs={{0,4},{4,0},{8,12},{12,8},{16,20},{20,16},{24,28},{28,24},{1,5},{5... | collective-permute-start | bytes 196616 | tf_op jit(solution)/shard_map/ppermute | solution.py:659
  35.7 0.2 collective-permute-start.6
  35.9 2.7 %collective-permute-start.7 = (bf16[16,16,128]{2,1,0:T(8,128)(2,1)S(1)}, bf16[16,16,128]{2,1,0:T(8,128)(2,1)S(1)}, u32[]{:S(2)}, u32[]{:S(2)}) collective-permute-start(bf16[16,16,128]{2,1,0:T(8,128)(2,1)S(1)} %get-tuple-element.73), channel_id=1, source_target_pairs={{0,12},{4,8},{8,4},{12,0},{16,28},{20,24},{24,20},{28,16},{1,13},{... | collective-permute-start | bytes 196616 | tf_op jit(solution)/shard_map/ppermute | solution.py:659
  38.6 2.3 %shard_map.85 = (f32[128,16,128]{2,1,0:T(8,128)S(1)}, bf16[4,6,16,128]{3,2,1,0:T(8,128)(2,1)S(1)}) custom-call(f32[3,16,16,128]{3,2,1,0:T(8,128)S(1)} %get-tuple-element.48.table, f32[128,16,128]{2,1,0:T(8,128)S(1)} %get-tuple-element.74.long_grad, f32[4,6,16,128]{3,2,1,0:T(8,128)S(1)} %get-tuple-element.75.head_in), custom_call_target="tpu_custom_call" | custom-call | flops 2000000000 | bytes 4194304 | tf_op jit(solution)/shard_map/pallas_call | solution.py:640
  40.9 1.3 %collective-permute-start.9 = (bf16[4,6,16,128]{3,2,1,0:T(8,128)(2,1)S(1)}, bf16[4,6,16,128]{3,2,1,0:T(8,128)(2,1)S(1)}, u32[]{:S(2)}, u32[]{:S(2)}) collective-permute-start(bf16[4,6,16,128]{3,2,1,0:T(8,128)(2,1)S(1)} %get-tuple-element.93), channel_id=1, source_target_pairs={{4,0},{8,4},{12,8},{16,12},{20,16},{24,20},{28,24},{5,1},{9,5},{13... | collective-permute-start | bytes 294920 | tf_op jit(solution)/shard_map/ppermute | solution.py:655
  42.2 0.0 collective-permute-done.6.second
  42.2 0.0 collective-permute-done.7.third
  42.2 0.6 %shard_map.87 = (f32[16,16,128]{2,1,0:T(8,128)S(1)}, f32[16,16,128]{2,1,0:T(8,128)S(1)}, f32[6,16,128]{2,1,0:T(8,128)S(1)}, bf16[22,16,128]{2,1,0:T(8,128)(2,1)S(1)}) custom-call(s32[1]{0:T(128)} %bitcast.place, f32[3,16,16,128]{3,2,1,0:T(8,128)S(1)} %get-tuple-element.48.table, f32[16,16,128]{2,1,0:T(8,128)S(1)} %get-tuple-element.80.state, ...), custom_call_target="tpu_custom_call" | custom-call | bytes 4194304 | tf_op jit(solution)/shard_map/pallas_call | solution.py:640
  42.8 2.4 %collective-permute-start.8 = (bf16[22,16,128]{2,1,0:T(8,128)(2,1)S(1)}, bf16[22,16,128]{2,1,0:T(8,128)(2,1)S(1)}, u32[]{:S(2)}, u32[]{:S(2)}) collective-permute-start(bf16[22,16,128]{2,1,0:T(8,128)(2,1)S(1)} %get-tuple-element.87), channel_id=1, source_target_pairs={{0,16},{4,20},{8,24},{12,28},{16,0},{20,4},{24,8},{28,12},{1,17},{... | collective-permute-start | bytes 270344 | tf_op jit(solution)/shard_map/ppermute | solution.py:659
  45.2 1.7 %shard_map.86 = (bf16[128,2048]{1,0:T(8,128)(2,1)}, bf16[128,2048]{1,0:T(8,128)(2,1)S(1)}, f32[128,128]{1,0:T(8,128)S(1)}) custom-call(f32[128,128]{1,0:T(8,128)S(1)} %get-tuple-element.71.inv, f32[3,7,16,128]{3,2,1,0:T(8,128)S(1)} %copy-done.3, f32[16,128]{1,0:T(8,128)S(1)} %bitcast.4, f32[128,16,128]{2,1,0:T(8,128)S(1)} %get-tuple-element.65.query, ...), custom_call_target="tpu_custom_call" | custom-call | flops 2000000000 | bytes 4194304 | tf_op jit(solution)/shard_map/pallas_call | solution.py:640
  46.9 2.5 %collective-permute-done.8.got = bf16[22,16,128]{2,1,0:T(8,128)(2,1)S(1)} collective-permute-done((bf16[22,16,128]{2,1,0:T(8,128)(2,1)S(1)}, bf16[22,16,128]{2,1,0:T(8,128)(2,1)S(1)}, u32[]{:S(2)}, u32[]{:S(2)}) %collective-permute-start.8) | collective-permute-done | bytes 90144 | tf_op jit(solution)/shard_map/ppermute | solution.py:659
  49.3 3.6 %shard_map.88 = bf16[3,128,2048]{2,1,0:T(8,128)(2,1)} custom-call(s32[1]{0:T(128)} %bitcast.place, f32[16,16,128]{2,1,0:T(8,128)S(1)} %get-tuple-element.84.entering, f32[16,16,128]{2,1,0:T(8,128)S(1)} %get-tuple-element.85.beyond_in, f32[6,16,128]{2,1,0:T(8,128)S(1)} %get-tuple-element.86.added, bf16[22,16,128]{2,1,0:T(8,128)(2,1)S(1)} %collective-permute-done.8.got, ...), custom_call_target="tpu_custom_call" | custom-call | bytes 4194304 | tf_op jit(solution)/shard_map/pallas_call | solution.py:640
  (11 shorter events, 0.0 us)
Async XLA Ops:
  1.6 9.0 %collective-permute-start = (bf16[3,8,2048]{2,1,0:T(8,128)(2,1)S(1)}, bf16[3,8,2048]{2,1,0:T(8,128)(2,1)S(1)}, u32[]{:S(2)}, u32[]{:S(2)}) collective-permute-start(bf16[3,8,2048]{2,1,0:T(8,128)(2,1)S(1)} %shard_map.78), channel_id=1, source_target_pairs={{0,4},{4,8},{8,12},{12,16},{16,20},{20,24},{24,28},{1,5},{5,9},{9,... | collective-permute-start | bytes 294920 | tf_op jit(solution)/shard_map/ppermute | solution.py:655
  6.4 8.0 %copy-start.4 = (f32[2048]{0:T(1024)S(1)}, f32[2048]{0:T(1024)}, u32[]{:S(2)}) copy-start(f32[2048]{0:T(1024)} %param.10) | copy-start | bytes 24580
  10.9 5.7 %collective-permute-start.1 = (bf16[16,16,128]{2,1,0:T(8,128)(2,1)S(1)}, bf16[16,16,128]{2,1,0:T(8,128)(2,1)S(1)}, u32[]{:S(2)}, u32[]{:S(2)}) collective-permute-start(bf16[16,16,128]{2,1,0:T(8,128)(2,1)S(1)} %get-tuple-element.53), channel_id=1, source_target_pairs={{0,4},{4,0},{8,12},{12,8},{16,20},{20,16},{24,28},{28,24},{1,5},{5... | collective-permute-start | bytes 196616 | tf_op jit(solution)/shard_map/ppermute | solution.py:659
  12.5 4.5 %collective-permute-start.2 = (bf16[16,16,128]{2,1,0:T(8,128)(2,1)S(1)}, bf16[16,16,128]{2,1,0:T(8,128)(2,1)S(1)}, u32[]{:S(2)}, u32[]{:S(2)}) collective-permute-start(bf16[16,16,128]{2,1,0:T(8,128)(2,1)S(1)} %get-tuple-element.53), channel_id=1, source_target_pairs={{0,8},{4,12},{8,0},{12,4},{16,24},{20,28},{24,16},{28,20},{1,9},{5... | collective-permute-start | bytes 196616 | tf_op jit(solution)/shard_map/ppermute | solution.py:659
  14.1 5.2 %collective-permute-start.3 = (bf16[16,16,128]{2,1,0:T(8,128)(2,1)S(1)}, bf16[16,16,128]{2,1,0:T(8,128)(2,1)S(1)}, u32[]{:S(2)}, u32[]{:S(2)}) collective-permute-start(bf16[16,16,128]{2,1,0:T(8,128)(2,1)S(1)} %get-tuple-element.53), channel_id=1, source_target_pairs={{0,12},{4,8},{8,4},{12,0},{16,28},{20,24},{24,20},{28,16},{1,13},{... | collective-permute-start | bytes 196616 | tf_op jit(solution)/shard_map/ppermute | solution.py:659
  14.5 6.8 %copy-start = (f32[2,128,16,128]{3,2,1,0:T(8,128)S(1)}, f32[2,128,16,128]{3,2,1,0:T(8,128)}, u32[]{:S(2)}) copy-start(f32[2,128,16,128]{3,2,1,0:T(8,128)} %get-tuple-element.61.pair) | copy-start | bytes 6291460
  19.7 5.8 %collective-permute-start.4 = (bf16[16,16,128]{2,1,0:T(8,128)(2,1)S(1)}, bf16[16,16,128]{2,1,0:T(8,128)(2,1)S(1)}, u32[]{:S(2)}, u32[]{:S(2)}) collective-permute-start(bf16[16,16,128]{2,1,0:T(8,128)(2,1)S(1)} %get-tuple-element.60), channel_id=1, source_target_pairs={{0,16},{4,20},{8,24},{12,28},{16,0},{20,4},{24,8},{28,12},{1,17},{... | collective-permute-start | bytes 196616 | tf_op jit(solution)/shard_map/ppermute | solution.py:659
  35.0 7.1 %collective-permute-start.5 = (bf16[16,16,128]{2,1,0:T(8,128)(2,1)S(1)}, bf16[16,16,128]{2,1,0:T(8,128)(2,1)S(1)}, u32[]{:S(2)}, u32[]{:S(2)}) collective-permute-start(bf16[16,16,128]{2,1,0:T(8,128)(2,1)S(1)} %get-tuple-element.73), channel_id=1, source_target_pairs={{0,4},{4,0},{8,12},{12,8},{16,20},{20,16},{24,28},{28,24},{1,5},{5... | collective-permute-start | bytes 196616 | tf_op jit(solution)/shard_map/ppermute | solution.py:659
  35.7 6.5 %collective-permute-start.6 = (bf16[16,16,128]{2,1,0:T(8,128)(2,1)S(1)}, bf16[16,16,128]{2,1,0:T(8,128)(2,1)S(1)}, u32[]{:S(2)}, u32[]{:S(2)}) collective-permute-start(bf16[16,16,128]{2,1,0:T(8,128)(2,1)S(1)} %get-tuple-element.73), channel_id=1, source_target_pairs={{0,8},{4,12},{8,0},{12,4},{16,24},{20,28},{24,16},{28,20},{1,9},{5... | collective-permute-start | bytes 196616 | tf_op jit(solution)/shard_map/ppermute | solution.py:659
  35.9 6.3 %collective-permute-start.7 = (bf16[16,16,128]{2,1,0:T(8,128)(2,1)S(1)}, bf16[16,16,128]{2,1,0:T(8,128)(2,1)S(1)}, u32[]{:S(2)}, u32[]{:S(2)}) collective-permute-start(bf16[16,16,128]{2,1,0:T(8,128)(2,1)S(1)} %get-tuple-element.73), channel_id=1, source_target_pairs={{0,12},{4,8},{8,4},{12,0},{16,28},{20,24},{24,20},{28,16},{1,13},{... | collective-permute-start | bytes 196616 | tf_op jit(solution)/shard_map/ppermute | solution.py:659
  38.6 6.6 %copy-start.3 = (f32[3,7,16,128]{3,2,1,0:T(8,128)S(1)}, f32[3,7,16,128]{3,2,1,0:T(8,128)}, u32[]{:S(2)}) copy-start(f32[3,7,16,128]{3,2,1,0:T(8,128)} %get-tuple-element.72.taps) | copy-start | bytes 516100
  40.9 8.5 %collective-permute-start.9 = (bf16[4,6,16,128]{3,2,1,0:T(8,128)(2,1)S(1)}, bf16[4,6,16,128]{3,2,1,0:T(8,128)(2,1)S(1)}, u32[]{:S(2)}, u32[]{:S(2)}) collective-permute-start(bf16[4,6,16,128]{3,2,1,0:T(8,128)(2,1)S(1)} %get-tuple-element.93), channel_id=1, source_target_pairs={{4,0},{8,4},{12,8},{16,12},{20,16},{24,20},{28,24},{5,1},{9,5},{13... | collective-permute-start | bytes 294920 | tf_op jit(solution)/shard_map/ppermute | solution.py:655
  42.8 6.5 %collective-permute-start.8 = (bf16[22,16,128]{2,1,0:T(8,128)(2,1)S(1)}, bf16[22,16,128]{2,1,0:T(8,128)(2,1)S(1)}, u32[]{:S(2)}, u32[]{:S(2)}) collective-permute-start(bf16[22,16,128]{2,1,0:T(8,128)(2,1)S(1)} %get-tuple-element.87), channel_id=1, source_target_pairs={{0,16},{4,20},{8,24},{12,28},{16,0},{20,4},{24,8},{28,12},{1,17},{... | collective-permute-start | bytes 270344 | tf_op jit(solution)/shard_map/ppermute | solution.py:659
  45.2 4.2 %copy-start.1 = (f32[2,128,16,128]{3,2,1,0:T(8,128)S(1)}, f32[2,128,16,128]{3,2,1,0:T(8,128)}, u32[]{:S(2)}) copy-start(f32[2,128,16,128]{3,2,1,0:T(8,128)} %get-tuple-element.61.pair) | copy-start | bytes 6291460
  45.2 4.2 %copy-start.2 = (f32[2,8,16,128]{3,2,1,0:T(8,128)S(1)}, f32[2,8,16,128]{3,2,1,0:T(8,128)}, u32[]{:S(2)}) copy-start(f32[2,8,16,128]{3,2,1,0:T(8,128)} %get-tuple-element.70.rows_far.first_rows) | copy-start | bytes 393220

commit v6 on v5

--- a/solution.py
+++ b/solution.py
@@ -82,11 +82,17 @@
     lane_blocks = channels // LANES
     tap_count = taps.shape[1]
     pitch = rows + SUB
+    count = lane_blocks // SUB
+    width = SUB * LANES
     fetches = [
         pltpu.make_async_copy(source, target, sems.at[i])
         for i, (source, target) in enumerate(
             [(filt_far, filt), (rate_far, rate), (res_far, res)]
-            + [(x_far.at[1 + s], x.at[s]) for s in range(2)]
+            + [
+                (x_far.at[1 + s, :, pl.ds(h * width, width)], x.at[s, :, pl.ds(h * width, width)])
+                for h in range(count)
+                for s in range(2)
+            ]
         )
     ]
     for fetch in fetches:
@@ -103,7 +109,7 @@
         for h, half in enumerate(halves(lane_blocks)):
             for i in range(tap_count):
                 taps[s, i, half, :] = row_at(ps, 0, SUB, h, i)
-    stores = [pltpu.make_async_copy(taps, taps_far, sems.at[5])]
+    stores = [pltpu.make_async_copy(taps, taps_far, sems.at[3 + 2 * count])]
     stores[0].start()
     fetches[1].wait()
     fetches[2].wait()
@@ -117,11 +123,11 @@
             table[1, m, half, :] = c * jnp.sqrt(2.0 * r)
             table[2, m, half, :] = r
     zero = jnp.zeros((SUB, LANES), jnp.float32)
-    for s in range(2):
-        fetches[3 + s].wait()
-        spread_rows(x.at[s], xs, s * lane_blocks * pitch, pitch, lane_blocks)
     for h, half in enumerate(halves(lane_blocks)):
         for s in range(2):
+            fetches[3 + 2 * h + s].wait()
+            part = x.at[s, :, pl.ds(h * width, width)]
+            spread_rows(part, xs, (s * lane_blocks + h * SUB) * pitch, pitch, SUB)
             w = [taps[1 + s, i, half, :] for i in range(tap_count)]
 
             def body(block, window):
@@ -135,11 +141,12 @@
             lax.fori_loop(0, rows // SUB, body, (zero,) * (tap_count - 1))
             stores.append(
                 pltpu.make_async_copy(
-                    pair.at[s, :, half, :], pair_far.at[s, :, half, :], sems.at[6 + 2 * h + s]
+                    pair.at[s, :, half, :], pair_far.at[s, :, half, :], sems.at[4 + 2 * count + 2 * h + s]
                 )
             )
             stores[-1].start()
             first_rows[s, :, half, :] = pair[s, :SUB, half, :]
+    for half in halves(lane_blocks):
         decay = [table[0, m, half, :] for m in range(modes)]
 
         def step(t, state):
@@ -560,6 +567,23 @@
     moves[0].start()
     ls[...] = last[...]
     for h, half in enumerate(halves(lane_blocks)):
+        later = [head[0, i, half, :].astype(jnp.float32) for i in range(reach)]
+        for t in range(SUB - reach, SUB):
+            edge_rows = pl.ds(h * SUB * SUB + t, SUB, stride=SUB)
+            ls[edge_rows, :] += total(
+                taps[0, i, half, :] * later[t + i - SUB] for i in range(SUB - t, tap_count)
+            )
+    for lb in range(lane_blocks):
+        columns = slice(lb * LANES, (lb + 1) * LANES)
+        ending = jnp.concatenate(
+            [query[kept : kept + SUB, columns].astype(jnp.float32), ls[pl.ds(lb * SUB, SUB), :]], axis=0
+        )
+        edge[:, columns] = ending.astype(edge.dtype)
+    moves.append(
+        pltpu.make_async_copy(edge, grads.at[0, pl.ds(kept, 2 * SUB), :], sems.at[len(moves)])
+    )
+    moves[-1].start()
+    for h, half in enumerate(halves(lane_blocks)):
         decay = [table[0, m, half, :] for m in range(modes)]
         start, onward = [], []
         for m in range(modes):
@@ -580,18 +604,12 @@
         state = lax.fori_loop(0, blocks - 1, functools.partial(block_step, pair), tuple(start))
         block_step(first_rows, blocks - 1, state)
         own = far_rows(table, half, onward, rows, reach)
-        beyond = [[], [], []]
+        beyond = [None, [], []]
         for i in range(reach):
             rows_there = joined_rows(span, place, got[modes + i, half, :].astype(jnp.float32))
             gated = head[1, i, half, :].astype(jnp.float32) + own[i] + added[i, half, :] + rows_there
-            beyond[0].append(head[0, i, half, :].astype(jnp.float32))
             beyond[1].append(gated * head[2, i, half, :].astype(jnp.float32))
             beyond[2].append(gated * head[3, i, half, :].astype(jnp.float32))
-        for t in range(SUB - reach, SUB):
-            edge_rows = pl.ds(h * SUB * SUB + t, SUB, stride=SUB)
-            ls[edge_rows, :] += total(
-                taps[0, i, half, :] * beyond[0][t + i - SUB] for i in range(SUB - t, tap_count)
-            )
         for s in range(1, 3):
             w = [taps[s, i, half, :] for i in range(tap_count)]
 
@@ -616,16 +634,6 @@
                 )
             )
             moves[-1].start()
-    for lb in range(lane_blocks):
-        columns = slice(lb * LANES, (lb + 1) * LANES)
-        ending = jnp.concatenate(
-            [query[kept : kept + SUB, columns].astype(jnp.float32), ls[pl.ds(lb * SUB, SUB), :]], axis=0
-        )
-        edge[:, columns] = ending.astype(edge.dtype)
-    moves.append(
-        pltpu.make_async_copy(edge, grads.at[0, pl.ds(kept, 2 * SUB), :], sems.at[len(moves)])
-    )
-    moves[-1].start()
     for move in moves:
         move.wait()
 
@@ -706,7 +714,7 @@
             (2, *row_shape),
             (2 * lane_blocks * pitch, LANES),
             (2 * lane_blocks * modes, LANES),
-            pltpu.SemaphoreType.DMA((6 + lane_blocks // 4,)),
+            pltpu.SemaphoreType.DMA((4 + lane_blocks // 2,)),
         ),
         work=10**9,
     )
@@ -762,7 +770,6 @@
         [(place, pltpu.SMEM)] + v(entering, got, table, query, local, scaled),
         [kept(*row_shape), kept(2, rows)],
         ((rows * SUB, LANES), (rows * SUB, LANES)),
-        aliases={5: 0},
     )
     sums = lax.psum(sums, "tp")
     mixed, long_grad, back, message, inv, head = run(
@@ -782,7 +789,6 @@
             (2, SUB, lane_blocks, LANES),
             pltpu.SemaphoreType.DMA(()),
         ),
-        aliases={4: 0},
     )
 
     local_back, head = run(

time: 53.2 us -> 52.6 us (0.989)
  Pallas kernels: 22.3 us -> 21.7 us
    pallas_call x12, Pallas kernels: 22.3 us -> 21.7 us  [run(): pl.pallas_call(kernel, out_shape=outs, in_specs=[pl.BlockSpec(memory_spac...]
  transfers between devices with their start and end apart: 10 -> 10, of which waited for: 4 -> 4; matrix products, arithmetic and copies ran while one was open for 0% -> 0% of each run, Pallas kernels for 25% -> 24%
where the time goes in v6:
time: 52.6 us; the launch traced here: 52.4 us
  Pallas kernels  21.7 us (41%)
  starting transfers between devices  17.4 us (33%)
  waiting for transfers between devices  6.77 us (13%)
  blocking collectives  5.66 us (11%)
  between operations  0.76 us (1%)
    pallas_call x12, Pallas kernels, run(): pl.pallas_call(kernel, out_shape=outs, in_specs=[pl.BlockSpec(memory_spac...  21.7 us
    ppermute x8, starting transfers between devices, swapped(): lax.ppermute(block, 'ctx', [(i, i ^ distance) for i in range(lax.axis_siz...  11.3 us
    ppermute x8, waiting for transfers between devices, swapped(): lax.ppermute(block, 'ctx', [(i, i ^ distance) for i in range(lax.axis_siz...  6.77 us
    ppermute x2, starting transfers between devices, shifted(): return lax.ppermute(block, 'ctx', route)  6.14 us
    psum x1, blocking collectives, on_device(): sums = lax.psum(sums, 'tp')  5.66 us
  transfers between devices with their start and end apart: 10, of which 4 were waited for; matrix products, arithmetic and copies ran while one was open for 0% of the time, Pallas kernels for 24%

profile of v6, /device:TPU:0, one launch (start us, length us, event | category | flops | bytes accessed | tf_op | source)
XLA Modules:
  0.0 52.4 jit_solution(12705069939533212325)
XLA Ops:
  0.6 0.9 %shard_map.78 = bf16[3,8,2048]{2,1,0:T(8,128)(2,1)S(1)} custom-call(bf16[3,128,2048]{2,1,0:T(8,128)(2,1)} %x_far.3), custom_call_target="tpu_custom_call" | custom-call | bytes 4194304 | tf_op jit(solution)/shard_map/pallas_call | solution.py:648
  1.6 4.8 %collective-permute-start = (bf16[3,8,2048]{2,1,0:T(8,128)(2,1)S(1)}, bf16[3,8,2048]{2,1,0:T(8,128)(2,1)S(1)}, u32[]{:S(2)}, u32[]{:S(2)}) collective-permute-start(bf16[3,8,2048]{2,1,0:T(8,128)(2,1)S(1)} %shard_map.78), channel_id=1, source_target_pairs={{0,4},{4,8},{8,12},{12,16},{16,20},{20,24},{24,28},{1,5},{5,9},{9,... | collective-permute-start | bytes 294920 | tf_op jit(solution)/shard_map/ppermute | solution.py:663
  6.4 0.0 copy-start.4
  6.5 3.8 %shard_map.77 = (f32[2,128,16,128]{3,2,1,0:T(8,128)}, f32[3,7,16,128]{3,2,1,0:T(8,128)}, f32[2,8,16,128]{3,2,1,0:T(8,128)S(1)}, f32[3,16,16,128]{3,2,1,0:T(8,128...) custom-call(bf16[3,128,2048]{2,1,0:T(8,128)(2,1)} %x_far.3, bf16[3,7,128]{2,1,0:T(8,128)(2,1)} %bitcast.5, ...), custom_call_target="tpu_custom_call" | custom-call | flops 1000000000 | bytes 4194304 | tf_op jit(solution)/shard_map/pallas_call | solution.py:648
  10.3 0.0 collective-permute-done.halo
  10.3 0.3 shard_map.79
  10.6 1.6 %collective-permute-start.1 = (bf16[16,16,128]{2,1,0:T(8,128)(2,1)S(1)}, bf16[16,16,128]{2,1,0:T(8,128)(2,1)S(1)}, u32[]{:S(2)}, u32[]{:S(2)}) collective-permute-start(bf16[16,16,128]{2,1,0:T(8,128)(2,1)S(1)} %get-tuple-element.53), channel_id=1, source_target_pairs={{0,4},{4,0},{8,12},{12,8},{16,20},{20,16},{24,28},{28,24},{1,5},{5... | collective-permute-start | bytes 196616 | tf_op jit(solution)/shard_map/ppermute | solution.py:667
  12.2 1.6 %collective-permute-start.2 = (bf16[16,16,128]{2,1,0:T(8,128)(2,1)S(1)}, bf16[16,16,128]{2,1,0:T(8,128)(2,1)S(1)}, u32[]{:S(2)}, u32[]{:S(2)}) collective-permute-start(bf16[16,16,128]{2,1,0:T(8,128)(2,1)S(1)} %get-tuple-element.53), channel_id=1, source_target_pairs={{0,8},{4,12},{8,0},{12,4},{16,24},{20,28},{24,16},{28,20},{1,9},{5... | collective-permute-start | bytes 196616 | tf_op jit(solution)/shard_map/ppermute | solution.py:667
  13.8 0.4 collective-permute-start.3
  14.2 2.1 %shard_map.80 = (f32[128,16,128]{2,1,0:T(8,128)S(1)}, f32[128,16,128]{2,1,0:T(8,128)S(1)}) custom-call(bf16[3,128,2048]{2,1,0:T(8,128)(2,1)} %x_far.3, bf16[3,8,2048]{2,1,0:T(8,128)(2,1)S(1)} %collective-permute-done.halo, f32[3,7,16,128]{3,2,1,0:T(8,128)S(1)} %get-tuple-element.50.taps, f32[16,128]{1,0:T(8,128)S(1)} %bitcast.3, bf16[128,2048]{1,0:T(8,128)(2,1)} %grad_far.1), custom_call_target="tpu_custom_call" | custom-call | flops 2000000000 | bytes 4194304 | tf_op jit(solution)/shard_map/pallas_call | solution.py:648
  16.3 0.0 collective-permute-done.1.first
  16.3 0.4 collective-permute-done.2.second
  16.7 2.3 %collective-permute-done.3.third = bf16[16,16,128]{2,1,0:T(8,128)(2,1)S(1)} collective-permute-done((bf16[16,16,128]{2,1,0:T(8,128)(2,1)S(1)}, bf16[16,16,128]{2,1,0:T(8,128)(2,1)S(1)}, u32[]{:S(2)}, u32[]{:S(2)}) %collective-permute-start.3) | collective-permute-done | bytes 65568 | tf_op jit(solution)/shard_map/ppermute | solution.py:667
  19.0 0.4 shard_map.81
  19.4 1.8 %collective-permute-start.4 = (bf16[16,16,128]{2,1,0:T(8,128)(2,1)S(1)}, bf16[16,16,128]{2,1,0:T(8,128)(2,1)S(1)}, u32[]{:S(2)}, u32[]{:S(2)}) collective-permute-start(bf16[16,16,128]{2,1,0:T(8,128)(2,1)S(1)} %get-tuple-element.60), channel_id=1, source_target_pairs={{0,16},{4,20},{8,24},{12,28},{16,0},{20,4},{24,8},{28,12},{1,17},{... | collective-permute-start | bytes 196616 | tf_op jit(solution)/shard_map/ppermute | solution.py:667
  21.2 2.4 %shard_map.82 = (f32[128,16,128]{2,1,0:T(8,128)S(1)}, f32[2,8,16,128]{3,2,1,0:T(8,128)}) custom-call(f32[2,128,16,128]{3,2,1,0:T(8,128)S(1)} %copy-done, f32[2,8,16,128]{3,2,1,0:T(8,128)S(1)} %get-tuple-element.62.first_rows, f32[3,16,16,128]{3,2,1,0:T(8,128)S(1)} %get-tuple-element.48.table), custom_call_target="tpu_custom_call" | custom-call | flops 2000000000 | bytes 4194304 | tf_op jit(solution)/shard_map/pallas_call | solution.py:648
  23.6 1.6 %collective-permute-done.4.got = bf16[16,16,128]{2,1,0:T(8,128)(2,1)S(1)} collective-permute-done((bf16[16,16,128]{2,1,0:T(8,128)(2,1)S(1)}, bf16[16,16,128]{2,1,0:T(8,128)(2,1)S(1)}, u32[]{:S(2)}, u32[]{:S(2)}) %collective-permute-start.4) | collective-permute-done | bytes 65568 | tf_op jit(solution)/shard_map/ppermute | solution.py:667
  25.2 1.6 %shard_map.83 = (f32[128,16,128]{2,1,0:T(8,128)S(1)}, f32[2,128]{1,0:T(2,128)S(1)}) custom-call(s32[1]{0:T(128)} %bitcast.place, f32[16,16,128]{2,1,0:T(8,128)S(1)} %get-tuple-element.59.entering, bf16[16,16,128]{2,1,0:T(8,128)(2,1)S(1)} %collective-permute-done.4.got, f32[3,16,16,128]{3,2,1,0:T(8,128)S(1)} %get-tuple-element.48.table, ...), custom_call_target="tpu_custom_call" | custom-call | bytes 4194304 | tf_op jit(solution)/shard_map/pallas_call | solution.py:648
  26.8 5.7 %psum.7.sums = f32[2,128]{1,0:T(2,128)S(1)} all-reduce(f32[2,128]{1,0:T(2,128)S(1)} %get-tuple-element.68), channel_id=1, replica_groups=mesh['ctx'=8,'tp'=4] {'tp'}, use_global_device_ids=true, to_apply=%region_0.0 | all-reduce | flops 256 | bytes 2048 | tf_op jit(solution)/shard_map/psum | solution.py:774
  32.5 2.0 %shard_map.84 = (f32[128,16,128]{2,1,0:T(8,128)S(1)}, f32[128,16,128]{2,1,0:T(8,128)S(1)}, f32[16,16,128]{2,1,0:T(8,128)S(1)}, bf16[16,16,128]{2,1,0:T(8,128)(2,...) custom-call(f32[2,128]{1,0:T(2,128)S(1)} %psum.7.sums, f32[3,16,16,128]{3,2,1,0:T(8,128)S(1)} %get-tuple-element.48.table, ...), custom_call_target="tpu_custom_call" | custom-call | bytes 4194304 | tf_op jit(solution)/shard_map/pallas_call | solution.py:648
  34.5 0.8 %collective-permute-start.5 = (bf16[16,16,128]{2,1,0:T(8,128)(2,1)S(1)}, bf16[16,16,128]{2,1,0:T(8,128)(2,1)S(1)}, u32[]{:S(2)}, u32[]{:S(2)}) collective-permute-start(bf16[16,16,128]{2,1,0:T(8,128)(2,1)S(1)} %get-tuple-element.73), channel_id=1, source_target_pairs={{0,4},{4,0},{8,12},{12,8},{16,20},{20,16},{24,28},{28,24},{1,5},{5... | collective-permute-start | bytes 196616 | tf_op jit(solution)/shard_map/ppermute | solution.py:667
  35.3 0.0 collective-permute-start.6
  35.4 2.7 %collective-permute-start.7 = (bf16[16,16,128]{2,1,0:T(8,128)(2,1)S(1)}, bf16[16,16,128]{2,1,0:T(8,128)(2,1)S(1)}, u32[]{:S(2)}, u32[]{:S(2)}) collective-permute-start(bf16[16,16,128]{2,1,0:T(8,128)(2,1)S(1)} %get-tuple-element.73), channel_id=1, source_target_pairs={{0,12},{4,8},{8,4},{12,0},{16,28},{20,24},{24,20},{28,16},{1,13},{... | collective-permute-start | bytes 196616 | tf_op jit(solution)/shard_map/ppermute | solution.py:667
  38.1 2.3 %shard_map.85 = (f32[128,16,128]{2,1,0:T(8,128)S(1)}, bf16[4,6,16,128]{3,2,1,0:T(8,128)(2,1)S(1)}) custom-call(f32[3,16,16,128]{3,2,1,0:T(8,128)S(1)} %get-tuple-element.48.table, f32[128,16,128]{2,1,0:T(8,128)S(1)} %get-tuple-element.74.long_grad, f32[4,6,16,128]{3,2,1,0:T(8,128)S(1)} %get-tuple-element.75.head_in), custom_call_target="tpu_custom_call" | custom-call | flops 2000000000 | bytes 4194304 | tf_op jit(solution)/shard_map/pallas_call | solution.py:648
  40.3 1.3 %collective-permute-start.9 = (bf16[4,6,16,128]{3,2,1,0:T(8,128)(2,1)S(1)}, bf16[4,6,16,128]{3,2,1,0:T(8,128)(2,1)S(1)}, u32[]{:S(2)}, u32[]{:S(2)}) collective-permute-start(bf16[4,6,16,128]{3,2,1,0:T(8,128)(2,1)S(1)} %get-tuple-element.93), channel_id=1, source_target_pairs={{4,0},{8,4},{12,8},{16,12},{20,16},{24,20},{28,24},{5,1},{9,5},{13... | collective-permute-start | bytes 294920 | tf_op jit(solution)/shard_map/ppermute | solution.py:663
  41.6 0.0 collective-permute-done.6.second
  41.7 0.0 collective-permute-done.7.third
  41.7 0.6 %shard_map.87 = (f32[16,16,128]{2,1,0:T(8,128)S(1)}, f32[16,16,128]{2,1,0:T(8,128)S(1)}, f32[6,16,128]{2,1,0:T(8,128)S(1)}, bf16[22,16,128]{2,1,0:T(8,128)(2,1)S(1)}) custom-call(s32[1]{0:T(128)} %bitcast.place, f32[3,16,16,128]{3,2,1,0:T(8,128)S(1)} %get-tuple-element.48.table, f32[16,16,128]{2,1,0:T(8,128)S(1)} %get-tuple-element.80.state, ...), custom_call_target="tpu_custom_call" | custom-call | bytes 4194304 | tf_op jit(solution)/shard_map/pallas_call | solution.py:648
  42.3 2.4 %collective-permute-start.8 = (bf16[22,16,128]{2,1,0:T(8,128)(2,1)S(1)}, bf16[22,16,128]{2,1,0:T(8,128)(2,1)S(1)}, u32[]{:S(2)}, u32[]{:S(2)}) collective-permute-start(bf16[22,16,128]{2,1,0:T(8,128)(2,1)S(1)} %get-tuple-element.87), channel_id=1, source_target_pairs={{0,16},{4,20},{8,24},{12,28},{16,0},{20,4},{24,8},{28,12},{1,17},{... | collective-permute-start | bytes 270344 | tf_op jit(solution)/shard_map/ppermute | solution.py:667
  44.6 1.7 %shard_map.86 = (bf16[128,2048]{1,0:T(8,128)(2,1)}, bf16[128,2048]{1,0:T(8,128)(2,1)S(1)}, f32[128,128]{1,0:T(8,128)S(1)}) custom-call(f32[128,128]{1,0:T(8,128)S(1)} %get-tuple-element.71.inv, f32[3,7,16,128]{3,2,1,0:T(8,128)S(1)} %copy-done.3, f32[16,128]{1,0:T(8,128)S(1)} %bitcast.4, f32[128,16,128]{2,1,0:T(8,128)S(1)} %get-tuple-element.65.query, ...), custom_call_target="tpu_custom_call" | custom-call | flops 2000000000 | bytes 4194304 | tf_op jit(solution)/shard_map/pallas_call | solution.py:648
  46.3 2.5 %collective-permute-done.8.got = bf16[22,16,128]{2,1,0:T(8,128)(2,1)S(1)} collective-permute-done((bf16[22,16,128]{2,1,0:T(8,128)(2,1)S(1)}, bf16[22,16,128]{2,1,0:T(8,128)(2,1)S(1)}, u32[]{:S(2)}, u32[]{:S(2)}) %collective-permute-start.8) | collective-permute-done | bytes 90144 | tf_op jit(solution)/shard_map/ppermute | solution.py:667
  48.8 3.6 %shard_map.88 = bf16[3,128,2048]{2,1,0:T(8,128)(2,1)} custom-call(s32[1]{0:T(128)} %bitcast.place, f32[16,16,128]{2,1,0:T(8,128)S(1)} %get-tuple-element.84.entering, f32[16,16,128]{2,1,0:T(8,128)S(1)} %get-tuple-element.85.beyond_in, f32[6,16,128]{2,1,0:T(8,128)S(1)} %get-tuple-element.86.added, bf16[22,16,128]{2,1,0:T(8,128)(2,1)S(1)} %collective-permute-done.8.got, ...), custom_call_target="tpu_custom_call" | custom-call | bytes 4194304 | tf_op jit(solution)/shard_map/pallas_call | solution.py:648
  (11 shorter events, 0.0 us)
Async XLA Ops:
  1.6 8.7 %collective-permute-start = (bf16[3,8,2048]{2,1,0:T(8,128)(2,1)S(1)}, bf16[3,8,2048]{2,1,0:T(8,128)(2,1)S(1)}, u32[]{:S(2)}, u32[]{:S(2)}) collective-permute-start(bf16[3,8,2048]{2,1,0:T(8,128)(2,1)S(1)} %shard_map.78), channel_id=1, source_target_pairs={{0,4},{4,8},{8,12},{12,16},{16,20},{20,24},{24,28},{1,5},{5,9},{9,... | collective-permute-start | bytes 294920 | tf_op jit(solution)/shard_map/ppermute | solution.py:663
  6.4 7.7 %copy-start.4 = (f32[2048]{0:T(1024)S(1)}, f32[2048]{0:T(1024)}, u32[]{:S(2)}) copy-start(f32[2048]{0:T(1024)} %param.10) | copy-start | bytes 24580
  10.6 5.7 %collective-permute-start.1 = (bf16[16,16,128]{2,1,0:T(8,128)(2,1)S(1)}, bf16[16,16,128]{2,1,0:T(8,128)(2,1)S(1)}, u32[]{:S(2)}, u32[]{:S(2)}) collective-permute-start(bf16[16,16,128]{2,1,0:T(8,128)(2,1)S(1)} %get-tuple-element.53), channel_id=1, source_target_pairs={{0,4},{4,0},{8,12},{12,8},{16,20},{20,16},{24,28},{28,24},{1,5},{5... | collective-permute-start | bytes 196616 | tf_op jit(solution)/shard_map/ppermute | solution.py:667
  12.2 4.5 %collective-permute-start.2 = (bf16[16,16,128]{2,1,0:T(8,128)(2,1)S(1)}, bf16[16,16,128]{2,1,0:T(8,128)(2,1)S(1)}, u32[]{:S(2)}, u32[]{:S(2)}) collective-permute-start(bf16[16,16,128]{2,1,0:T(8,128)(2,1)S(1)} %get-tuple-element.53), channel_id=1, source_target_pairs={{0,8},{4,12},{8,0},{12,4},{16,24},{20,28},{24,16},{28,20},{1,9},{5... | collective-permute-start | bytes 196616 | tf_op jit(solution)/shard_map/ppermute | solution.py:667
  13.8 5.2 %collective-permute-start.3 = (bf16[16,16,128]{2,1,0:T(8,128)(2,1)S(1)}, bf16[16,16,128]{2,1,0:T(8,128)(2,1)S(1)}, u32[]{:S(2)}, u32[]{:S(2)}) collective-permute-start(bf16[16,16,128]{2,1,0:T(8,128)(2,1)S(1)} %get-tuple-element.53), channel_id=1, source_target_pairs={{0,12},{4,8},{8,4},{12,0},{16,28},{20,24},{24,20},{28,16},{1,13},{... | collective-permute-start | bytes 196616 | tf_op jit(solution)/shard_map/ppermute | solution.py:667
  14.2 7.0 %copy-start = (f32[2,128,16,128]{3,2,1,0:T(8,128)S(1)}, f32[2,128,16,128]{3,2,1,0:T(8,128)}, u32[]{:S(2)}) copy-start(f32[2,128,16,128]{3,2,1,0:T(8,128)} %get-tuple-element.61.pair) | copy-start | bytes 6291460
  19.4 5.8 %collective-permute-start.4 = (bf16[16,16,128]{2,1,0:T(8,128)(2,1)S(1)}, bf16[16,16,128]{2,1,0:T(8,128)(2,1)S(1)}, u32[]{:S(2)}, u32[]{:S(2)}) collective-permute-start(bf16[16,16,128]{2,1,0:T(8,128)(2,1)S(1)} %get-tuple-element.60), channel_id=1, source_target_pairs={{0,16},{4,20},{8,24},{12,28},{16,0},{20,4},{24,8},{28,12},{1,17},{... | collective-permute-start | bytes 196616 | tf_op jit(solution)/shard_map/ppermute | solution.py:667
  34.5 7.1 %collective-permute-start.5 = (bf16[16,16,128]{2,1,0:T(8,128)(2,1)S(1)}, bf16[16,16,128]{2,1,0:T(8,128)(2,1)S(1)}, u32[]{:S(2)}, u32[]{:S(2)}) collective-permute-start(bf16[16,16,128]{2,1,0:T(8,128)(2,1)S(1)} %get-tuple-element.73), channel_id=1, source_target_pairs={{0,4},{4,0},{8,12},{12,8},{16,20},{20,16},{24,28},{28,24},{1,5},{5... | collective-permute-start | bytes 196616 | tf_op jit(solution)/shard_map/ppermute | solution.py:667
  35.3 6.3 %collective-permute-start.6 = (bf16[16,16,128]{2,1,0:T(8,128)(2,1)S(1)}, bf16[16,16,128]{2,1,0:T(8,128)(2,1)S(1)}, u32[]{:S(2)}, u32[]{:S(2)}) collective-permute-start(bf16[16,16,128]{2,1,0:T(8,128)(2,1)S(1)} %get-tuple-element.73), channel_id=1, source_target_pairs={{0,8},{4,12},{8,0},{12,4},{16,24},{20,28},{24,16},{28,20},{1,9},{5... | collective-permute-start | bytes 196616 | tf_op jit(solution)/shard_map/ppermute | solution.py:667
  35.4 6.3 %collective-permute-start.7 = (bf16[16,16,128]{2,1,0:T(8,128)(2,1)S(1)}, bf16[16,16,128]{2,1,0:T(8,128)(2,1)S(1)}, u32[]{:S(2)}, u32[]{:S(2)}) collective-permute-start(bf16[16,16,128]{2,1,0:T(8,128)(2,1)S(1)} %get-tuple-element.73), channel_id=1, source_target_pairs={{0,12},{4,8},{8,4},{12,0},{16,28},{20,24},{24,20},{28,16},{1,13},{... | collective-permute-start | bytes 196616 | tf_op jit(solution)/shard_map/ppermute | solution.py:667
  38.1 6.6 %copy-start.3 = (f32[3,7,16,128]{3,2,1,0:T(8,128)S(1)}, f32[3,7,16,128]{3,2,1,0:T(8,128)}, u32[]{:S(2)}) copy-start(f32[3,7,16,128]{3,2,1,0:T(8,128)} %get-tuple-element.72.taps) | copy-start | bytes 516100
  40.3 8.5 %collective-permute-start.9 = (bf16[4,6,16,128]{3,2,1,0:T(8,128)(2,1)S(1)}, bf16[4,6,16,128]{3,2,1,0:T(8,128)(2,1)S(1)}, u32[]{:S(2)}, u32[]{:S(2)}) collective-permute-start(bf16[4,6,16,128]{3,2,1,0:T(8,128)(2,1)S(1)} %get-tuple-element.93), channel_id=1, source_target_pairs={{4,0},{8,4},{12,8},{16,12},{20,16},{24,20},{28,24},{5,1},{9,5},{13... | collective-permute-start | bytes 294920 | tf_op jit(solution)/shard_map/ppermute | solution.py:663
  42.3 6.5 %collective-permute-start.8 = (bf16[22,16,128]{2,1,0:T(8,128)(2,1)S(1)}, bf16[22,16,128]{2,1,0:T(8,128)(2,1)S(1)}, u32[]{:S(2)}, u32[]{:S(2)}) collective-permute-start(bf16[22,16,128]{2,1,0:T(8,128)(2,1)S(1)} %get-tuple-element.87), channel_id=1, source_target_pairs={{0,16},{4,20},{8,24},{12,28},{16,0},{20,4},{24,8},{28,12},{1,17},{... | collective-permute-start | bytes 270344 | tf_op jit(solution)/shard_map/ppermute | solution.py:667
  44.6 4.2 %copy-start.1 = (f32[2,128,16,128]{3,2,1,0:T(8,128)S(1)}, f32[2,128,16,128]{3,2,1,0:T(8,128)}, u32[]{:S(2)}) copy-start(f32[2,128,16,128]{3,2,1,0:T(8,128)} %get-tuple-element.61.pair) | copy-start | bytes 6291460
  44.6 4.2 %copy-start.2 = (f32[2,8,16,128]{3,2,1,0:T(8,128)S(1)}, f32[2,8,16,128]{3,2,1,0:T(8,128)}, u32[]{:S(2)}) copy-start(f32[2,8,16,128]{3,2,1,0:T(8,128)} %get-tuple-element.70.rows_far.first_rows) | copy-start | bytes 393220

commit v7 on v6

--- a/solution.py
+++ b/solution.py
@@ -342,14 +342,13 @@
                     first_rows[0, t, half, :],
                 )
                 for i, value in enumerate(found):
-                    head[i, t, half, :] = value
+                    head[i, t, half, :] = value.astype(head.dtype)
         for m, value in enumerate(to_send(table, half, state, rows // 2, message.dtype)):
             state_out[m, half, :] = state[m]
             message[m, half, :] = value
 
 
-def back_kernel(table, long_grad, head_in, local, head):
-    head[...] = head_in[...].astype(head.dtype)
+def back_kernel(table, long_grad, local):
     rows = long_grad.shape[0]
     modes, lane_blocks = table.shape[1:3]
     blocks = rows // SUB
@@ -781,7 +780,7 @@
             kept(*state_shape),
             jax.ShapeDtypeStruct(state_shape, wire),
             kept(rows, LANES),
-            kept(4, reach, lane_blocks, LANES),
+            jax.ShapeDtypeStruct((4, reach, lane_blocks, LANES), bf16),
         ],
         (
             (rows, LANES),
@@ -791,11 +790,8 @@
         ),
     )
 
-    local_back, head = run(
-        back_kernel,
-        v(table, long_grad, head),
-        [kept(*row_shape), jax.ShapeDtypeStruct(head.shape, bf16)],
-        work=2 * 10**9,
+    (local_back,) = run(
+        back_kernel, v(table, long_grad), [kept(*row_shape)], work=2 * 10**9
     )
     message_shape = (modes + reach, lane_blocks, LANES)
     adjoint = [kept(*state_shape), kept(*state_shape), kept(reach, lane_blocks, LANES)]

time: 52.6 us -> 51.3 us (0.975)
  waiting for transfers between devices: 6.77 us -> 3.17 us
  starting transfers between devices: 17.4 us -> 19.7 us
    ppermute x8, waiting for transfers between devices: 6.77 us -> 3.17 us  [swapped(): lax.ppermute(block, 'ctx', [(i, i ^ distance) for i in range(lax.axis_siz...]
    ppermute x8, starting transfers between devices: 11.3 us -> 13.5 us  [swapped(): lax.ppermute(block, 'ctx', [(i, i ^ distance) for i in range(lax.axis_siz...]
  transfers between devices with their start and end apart: 10 -> 10, of which waited for: 4 -> 5; matrix products, arithmetic and copies ran while one was open for 0% -> 0% of each run, Pallas kernels for 24% -> 25%
where the time goes in v7:
time: 51.3 us; the launch traced here: 51 us
  Pallas kernels  21.7 us (42%)
  starting transfers between devices  19.7 us (38%)
  blocking collectives  5.66 us (11%)
  waiting for transfers between devices  3.17 us (6%)
  between operations  0.76 us (1%)
    pallas_call x12, Pallas kernels, run(): pl.pallas_call(kernel, out_shape=outs, in_specs=[pl.BlockSpec(memory_spac...  21.7 us
    ppermute x8, starting transfers between devices, swapped(): lax.ppermute(block, 'ctx', [(i, i ^ distance) for i in range(lax.axis_siz...  13.5 us
    ppermute x2, starting transfers between devices, shifted(): return lax.ppermute(block, 'ctx', route)  6.13 us
    psum x1, blocking collectives, on_device(): sums = lax.psum(sums, 'tp')  5.66 us
    ppermute x8, waiting for transfers between devices, swapped(): lax.ppermute(block, 'ctx', [(i, i ^ distance) for i in range(lax.axis_siz...  3.17 us
  transfers between devices with their start and end apart: 10, of which 5 were waited for; matrix products, arithmetic and copies ran while one was open for 0% of the time, Pallas kernels for 25%

profile of v7, /device:TPU:0, one launch (start us, length us, event | category | flops | bytes accessed | tf_op | source)
XLA Modules:
  0.0 51.0 jit_solution(9752222222767381781)
XLA Ops:
  0.6 0.9 %shard_map.78 = bf16[3,8,2048]{2,1,0:T(8,128)(2,1)S(1)} custom-call(bf16[3,128,2048]{2,1,0:T(8,128)(2,1)} %x_far.3), custom_call_target="tpu_custom_call" | custom-call | bytes 4194304 | tf_op jit(solution)/shard_map/pallas_call | solution.py:647
  1.6 4.8 %collective-permute-start = (bf16[3,8,2048]{2,1,0:T(8,128)(2,1)S(1)}, bf16[3,8,2048]{2,1,0:T(8,128)(2,1)S(1)}, u32[]{:S(2)}, u32[]{:S(2)}) collective-permute-start(bf16[3,8,2048]{2,1,0:T(8,128)(2,1)S(1)} %shard_map.78), channel_id=1, source_target_pairs={{0,4},{4,8},{8,12},{12,16},{16,20},{20,24},{24,28},{1,5},{5,9},{9,... | collective-permute-start | bytes 294920 | tf_op jit(solution)/shard_map/ppermute | solution.py:662
  6.4 0.0 copy-start.4
  6.5 3.8 %shard_map.77 = (f32[2,128,16,128]{3,2,1,0:T(8,128)}, f32[3,7,16,128]{3,2,1,0:T(8,128)}, f32[2,8,16,128]{3,2,1,0:T(8,128)S(1)}, f32[3,16,16,128]{3,2,1,0:T(8,128...) custom-call(bf16[3,128,2048]{2,1,0:T(8,128)(2,1)} %x_far.3, bf16[3,7,128]{2,1,0:T(8,128)(2,1)} %bitcast.5, ...), custom_call_target="tpu_custom_call" | custom-call | flops 1000000000 | bytes 4194304 | tf_op jit(solution)/shard_map/pallas_call | solution.py:647
  10.3 0.0 collective-permute-done.halo
  10.3 0.3 shard_map.79
  10.6 2.6 %collective-permute-start.3 = (bf16[16,16,128]{2,1,0:T(8,128)(2,1)S(1)}, bf16[16,16,128]{2,1,0:T(8,128)(2,1)S(1)}, u32[]{:S(2)}, u32[]{:S(2)}) collective-permute-start(bf16[16,16,128]{2,1,0:T(8,128)(2,1)S(1)} %get-tuple-element.51), channel_id=1, source_target_pairs={{0,12},{4,8},{8,4},{12,0},{16,28},{20,24},{24,20},{28,16},{1,13},{... | collective-permute-start | bytes 196616 | tf_op jit(solution)/shard_map/ppermute | solution.py:666
  13.2 0.4 collective-permute-start.2
  13.7 0.5 collective-permute-start.1
  14.2 2.1 %shard_map.80 = (f32[128,16,128]{2,1,0:T(8,128)S(1)}, f32[128,16,128]{2,1,0:T(8,128)S(1)}) custom-call(bf16[3,128,2048]{2,1,0:T(8,128)(2,1)} %x_far.3, bf16[3,8,2048]{2,1,0:T(8,128)(2,1)S(1)} %collective-permute-done.halo, f32[3,7,16,128]{3,2,1,0:T(8,128)S(1)} %get-tuple-element.48.taps, f32[16,128]{1,0:T(8,128)S(1)} %bitcast.3, bf16[128,2048]{1,0:T(8,128)(2,1)} %grad_far.1), custom_call_target="tpu_custom_call" | custom-call | flops 2000000000 | bytes 4194304 | tf_op jit(solution)/shard_map/pallas_call | solution.py:647
  16.3 0.3 collective-permute-done.3.third
  16.5 1.0 %collective-permute-done.2.second = bf16[16,16,128]{2,1,0:T(8,128)(2,1)S(1)} collective-permute-done((bf16[16,16,128]{2,1,0:T(8,128)(2,1)S(1)}, bf16[16,16,128]{2,1,0:T(8,128)(2,1)S(1)}, u32[]{:S(2)}, u32[]{:S(2)}) %collective-permute-start.2) | collective-permute-done | bytes 65568 | tf_op jit(solution)/shard_map/ppermute | solution.py:666
  17.5 0.4 collective-permute-done.1.first
  18.0 0.4 shard_map.81
  18.4 2.7 %collective-permute-start.4 = (bf16[16,16,128]{2,1,0:T(8,128)(2,1)S(1)}, bf16[16,16,128]{2,1,0:T(8,128)(2,1)S(1)}, u32[]{:S(2)}, u32[]{:S(2)}) collective-permute-start(bf16[16,16,128]{2,1,0:T(8,128)(2,1)S(1)} %get-tuple-element.58), channel_id=1, source_target_pairs={{0,16},{4,20},{8,24},{12,28},{16,0},{20,4},{24,8},{28,12},{1,17},{... | collective-permute-start | bytes 196616 | tf_op jit(solution)/shard_map/ppermute | solution.py:666
  21.0 2.4 %shard_map.82 = (f32[128,16,128]{2,1,0:T(8,128)S(1)}, f32[2,8,16,128]{3,2,1,0:T(8,128)}) custom-call(f32[2,128,16,128]{3,2,1,0:T(8,128)S(1)} %copy-done, f32[2,8,16,128]{3,2,1,0:T(8,128)S(1)} %get-tuple-element.60.first_rows, f32[3,16,16,128]{3,2,1,0:T(8,128)S(1)} %get-tuple-element.46.table), custom_call_target="tpu_custom_call" | custom-call | flops 2000000000 | bytes 4194304 | tf_op jit(solution)/shard_map/pallas_call | solution.py:647
  23.4 0.2 collective-permute-done.4.got
  23.6 1.6 %shard_map.83 = (f32[128,16,128]{2,1,0:T(8,128)S(1)}, f32[2,128]{1,0:T(2,128)S(1)}) custom-call(s32[1]{0:T(128)} %bitcast.place, f32[16,16,128]{2,1,0:T(8,128)S(1)} %get-tuple-element.57.entering, bf16[16,16,128]{2,1,0:T(8,128)(2,1)S(1)} %collective-permute-done.4.got, f32[3,16,16,128]{3,2,1,0:T(8,128)S(1)} %get-tuple-element.46.table, ...), custom_call_target="tpu_custom_call" | custom-call | bytes 4194304 | tf_op jit(solution)/shard_map/pallas_call | solution.py:647
  25.2 5.7 %psum.7.sums = f32[2,128]{1,0:T(2,128)S(1)} all-reduce(f32[2,128]{1,0:T(2,128)S(1)} %get-tuple-element.66), channel_id=1, replica_groups=mesh['ctx'=8,'tp'=4] {'tp'}, use_global_device_ids=true, to_apply=%region_0.0 | all-reduce | flops 256 | bytes 2048 | tf_op jit(solution)/shard_map/psum | solution.py:773
  30.9 2.0 %shard_map.84 = (f32[128,16,128]{2,1,0:T(8,128)S(1)}, f32[128,16,128]{2,1,0:T(8,128)S(1)}, f32[16,16,128]{2,1,0:T(8,128)S(1)}, bf16[16,16,128]{2,1,0:T(8,128)(2,...) custom-call(f32[2,128]{1,0:T(2,128)S(1)} %psum.7.sums, ...), custom_call_target="tpu_custom_call" | custom-call | bytes 4194304 | tf_op jit(solution)/shard_map/pallas_call | solution.py:647
  32.9 1.7 %collective-permute-start.7 = (bf16[16,16,128]{2,1,0:T(8,128)(2,1)S(1)}, bf16[16,16,128]{2,1,0:T(8,128)(2,1)S(1)}, u32[]{:S(2)}, u32[]{:S(2)}) collective-permute-start(bf16[16,16,128]{2,1,0:T(8,128)(2,1)S(1)} %get-tuple-element.71), channel_id=1, source_target_pairs={{0,12},{4,8},{8,4},{12,0},{16,28},{20,24},{24,20},{28,16},{1,13},{... | collective-permute-start | bytes 196616 | tf_op jit(solution)/shard_map/ppermute | solution.py:666
  34.6 0.5 collective-permute-start.6
  35.1 1.4 %collective-permute-start.5 = (bf16[16,16,128]{2,1,0:T(8,128)(2,1)S(1)}, bf16[16,16,128]{2,1,0:T(8,128)(2,1)S(1)}, u32[]{:S(2)}, u32[]{:S(2)}) collective-permute-start(bf16[16,16,128]{2,1,0:T(8,128)(2,1)S(1)} %get-tuple-element.71), channel_id=1, source_target_pairs={{0,4},{4,0},{8,12},{12,8},{16,20},{20,16},{24,28},{28,24},{1,5},{5... | collective-permute-start | bytes 196616 | tf_op jit(solution)/shard_map/ppermute | solution.py:666
  36.5 1.3 %collective-permute-start.9 = (bf16[4,6,16,128]{3,2,1,0:T(8,128)(2,1)S(1)}, bf16[4,6,16,128]{3,2,1,0:T(8,128)(2,1)S(1)}, u32[]{:S(2)}, u32[]{:S(2)}) collective-permute-start(bf16[4,6,16,128]{3,2,1,0:T(8,128)(2,1)S(1)} %get-tuple-element.89), channel_id=1, source_target_pairs={{4,0},{8,4},{12,8},{16,12},{20,16},{24,20},{28,24},{5,1},{9,5},{13... | collective-permute-start | bytes 294920 | tf_op jit(solution)/shard_map/ppermute | solution.py:662
  37.8 0.0 copy-start.3
  37.8 2.3 %shard_map.85.local = f32[128,16,128]{2,1,0:T(8,128)S(1)} custom-call(f32[3,16,16,128]{3,2,1,0:T(8,128)S(1)} %get-tuple-element.46.table, f32[128,16,128]{2,1,0:T(8,128)S(1)} %get-tuple-element.72.long_grad), custom_call_target="tpu_custom_call" | custom-call | flops 2000000000 | bytes 4194304 | tf_op jit(solution)/shard_map/pallas_call | solution.py:647
  40.1 0.0 collective-permute-done.7.third
  40.1 0.6 %shard_map.87 = (f32[16,16,128]{2,1,0:T(8,128)S(1)}, f32[16,16,128]{2,1,0:T(8,128)S(1)}, f32[6,16,128]{2,1,0:T(8,128)S(1)}, bf16[22,16,128]{2,1,0:T(8,128)(2,1)S(1)}) custom-call(s32[1]{0:T(128)} %bitcast.place, f32[3,16,16,128]{3,2,1,0:T(8,128)S(1)} %get-tuple-element.46.table, f32[16,16,128]{2,1,0:T(8,128)S(1)} %get-tuple-element.76.state, ...), custom_call_target="tpu_custom_call" | custom-call | bytes 4194304 | tf_op jit(solution)/shard_map/pallas_call | solution.py:647
  40.7 3.8 %collective-permute-start.8 = (bf16[22,16,128]{2,1,0:T(8,128)(2,1)S(1)}, bf16[22,16,128]{2,1,0:T(8,128)(2,1)S(1)}, u32[]{:S(2)}, u32[]{:S(2)}) collective-permute-start(bf16[22,16,128]{2,1,0:T(8,128)(2,1)S(1)} %get-tuple-element.83), channel_id=1, source_target_pairs={{0,16},{4,20},{8,24},{12,28},{16,0},{20,4},{24,8},{28,12},{1,17},{... | collective-permute-start | bytes 270344 | tf_op jit(solution)/shard_map/ppermute | solution.py:666
  44.5 1.7 %shard_map.86 = (bf16[128,2048]{1,0:T(8,128)(2,1)}, bf16[128,2048]{1,0:T(8,128)(2,1)S(1)}, f32[128,128]{1,0:T(8,128)S(1)}) custom-call(f32[128,128]{1,0:T(8,128)S(1)} %get-tuple-element.69.inv, f32[3,7,16,128]{3,2,1,0:T(8,128)S(1)} %copy-done.3, f32[16,128]{1,0:T(8,128)S(1)} %bitcast.4, f32[128,16,128]{2,1,0:T(8,128)S(1)} %get-tuple-element.63.query, ...), custom_call_target="tpu_custom_call" | custom-call | flops 2000000000 | bytes 4194304 | tf_op jit(solution)/shard_map/pallas_call | solution.py:647
  46.2 1.3 %collective-permute-done.8.got = bf16[22,16,128]{2,1,0:T(8,128)(2,1)S(1)} collective-permute-done((bf16[22,16,128]{2,1,0:T(8,128)(2,1)S(1)}, bf16[22,16,128]{2,1,0:T(8,128)(2,1)S(1)}, u32[]{:S(2)}, u32[]{:S(2)}) %collective-permute-start.8) | collective-permute-done | bytes 90144 | tf_op jit(solution)/shard_map/ppermute | solution.py:666
  47.5 3.6 %shard_map.88 = bf16[3,128,2048]{2,1,0:T(8,128)(2,1)} custom-call(s32[1]{0:T(128)} %bitcast.place, f32[16,16,128]{2,1,0:T(8,128)S(1)} %get-tuple-element.80.entering, f32[16,16,128]{2,1,0:T(8,128)S(1)} %get-tuple-element.81.beyond_in, f32[6,16,128]{2,1,0:T(8,128)S(1)} %get-tuple-element.82.added, bf16[22,16,128]{2,1,0:T(8,128)(2,1)S(1)} %collective-permute-done.8.got, ...), custom_call_target="tpu_custom_call" | custom-call | bytes 4194304 | tf_op jit(solution)/shard_map/pallas_call | solution.py:647
  (11 shorter events, 0.0 us)
Async XLA Ops:
  1.6 8.7 %collective-permute-start = (bf16[3,8,2048]{2,1,0:T(8,128)(2,1)S(1)}, bf16[3,8,2048]{2,1,0:T(8,128)(2,1)S(1)}, u32[]{:S(2)}, u32[]{:S(2)}) collective-permute-start(bf16[3,8,2048]{2,1,0:T(8,128)(2,1)S(1)} %shard_map.78), channel_id=1, source_target_pairs={{0,4},{4,8},{8,12},{12,16},{16,20},{20,24},{24,28},{1,5},{5,9},{9,... | collective-permute-start | bytes 294920 | tf_op jit(solution)/shard_map/ppermute | solution.py:662
  6.4 7.7 %copy-start.4 = (f32[2048]{0:T(1024)S(1)}, f32[2048]{0:T(1024)}, u32[]{:S(2)}) copy-start(f32[2048]{0:T(1024)} %param.10) | copy-start | bytes 24580
  10.6 5.9 %collective-permute-start.3 = (bf16[16,16,128]{2,1,0:T(8,128)(2,1)S(1)}, bf16[16,16,128]{2,1,0:T(8,128)(2,1)S(1)}, u32[]{:S(2)}, u32[]{:S(2)}) collective-permute-start(bf16[16,16,128]{2,1,0:T(8,128)(2,1)S(1)} %get-tuple-element.51), channel_id=1, source_target_pairs={{0,12},{4,8},{8,4},{12,0},{16,28},{20,24},{24,20},{28,16},{1,13},{... | collective-permute-start | bytes 196616 | tf_op jit(solution)/shard_map/ppermute | solution.py:666
  13.2 4.3 %collective-permute-start.2 = (bf16[16,16,128]{2,1,0:T(8,128)(2,1)S(1)}, bf16[16,16,128]{2,1,0:T(8,128)(2,1)S(1)}, u32[]{:S(2)}, u32[]{:S(2)}) collective-permute-start(bf16[16,16,128]{2,1,0:T(8,128)(2,1)S(1)} %get-tuple-element.51), channel_id=1, source_target_pairs={{0,8},{4,12},{8,0},{12,4},{16,24},{20,28},{24,16},{28,20},{1,9},{5... | collective-permute-start | bytes 196616 | tf_op jit(solution)/shard_map/ppermute | solution.py:666
  13.7 4.3 %collective-permute-start.1 = (bf16[16,16,128]{2,1,0:T(8,128)(2,1)S(1)}, bf16[16,16,128]{2,1,0:T(8,128)(2,1)S(1)}, u32[]{:S(2)}, u32[]{:S(2)}) collective-permute-start(bf16[16,16,128]{2,1,0:T(8,128)(2,1)S(1)} %get-tuple-element.51), channel_id=1, source_target_pairs={{0,4},{4,0},{8,12},{12,8},{16,20},{20,16},{24,28},{28,24},{1,5},{5... | collective-permute-start | bytes 196616 | tf_op jit(solution)/shard_map/ppermute | solution.py:666
  14.2 6.8 %copy-start = (f32[2,128,16,128]{3,2,1,0:T(8,128)S(1)}, f32[2,128,16,128]{3,2,1,0:T(8,128)}, u32[]{:S(2)}) copy-start(f32[2,128,16,128]{3,2,1,0:T(8,128)} %get-tuple-element.59.pair) | copy-start | bytes 6291460
  18.4 5.2 %collective-permute-start.4 = (bf16[16,16,128]{2,1,0:T(8,128)(2,1)S(1)}, bf16[16,16,128]{2,1,0:T(8,128)(2,1)S(1)}, u32[]{:S(2)}, u32[]{:S(2)}) collective-permute-start(bf16[16,16,128]{2,1,0:T(8,128)(2,1)S(1)} %get-tuple-element.58), channel_id=1, source_target_pairs={{0,16},{4,20},{8,24},{12,28},{16,0},{20,4},{24,8},{28,12},{1,17},{... | collective-permute-start | bytes 196616 | tf_op jit(solution)/shard_map/ppermute | solution.py:666
  32.9 7.1 %collective-permute-start.7 = (bf16[16,16,128]{2,1,0:T(8,128)(2,1)S(1)}, bf16[16,16,128]{2,1,0:T(8,128)(2,1)S(1)}, u32[]{:S(2)}, u32[]{:S(2)}) collective-permute-start(bf16[16,16,128]{2,1,0:T(8,128)(2,1)S(1)} %get-tuple-element.71), channel_id=1, source_target_pairs={{0,12},{4,8},{8,4},{12,0},{16,28},{20,24},{24,20},{28,16},{1,13},{... | collective-permute-start | bytes 196616 | tf_op jit(solution)/shard_map/ppermute | solution.py:666
  34.6 5.4 %collective-permute-start.6 = (bf16[16,16,128]{2,1,0:T(8,128)(2,1)S(1)}, bf16[16,16,128]{2,1,0:T(8,128)(2,1)S(1)}, u32[]{:S(2)}, u32[]{:S(2)}) collective-permute-start(bf16[16,16,128]{2,1,0:T(8,128)(2,1)S(1)} %get-tuple-element.71), channel_id=1, source_target_pairs={{0,8},{4,12},{8,0},{12,4},{16,24},{20,28},{24,16},{28,20},{1,9},{5... | collective-permute-start | bytes 196616 | tf_op jit(solution)/shard_map/ppermute | solution.py:666
  35.1 4.9 %collective-permute-start.5 = (bf16[16,16,128]{2,1,0:T(8,128)(2,1)S(1)}, bf16[16,16,128]{2,1,0:T(8,128)(2,1)S(1)}, u32[]{:S(2)}, u32[]{:S(2)}) collective-permute-start(bf16[16,16,128]{2,1,0:T(8,128)(2,1)S(1)} %get-tuple-element.71), channel_id=1, source_target_pairs={{0,4},{4,0},{8,12},{12,8},{16,20},{20,16},{24,28},{28,24},{1,5},{5... | collective-permute-start | bytes 196616 | tf_op jit(solution)/shard_map/ppermute | solution.py:666
  36.5 11.0 %collective-permute-start.9 = (bf16[4,6,16,128]{3,2,1,0:T(8,128)(2,1)S(1)}, bf16[4,6,16,128]{3,2,1,0:T(8,128)(2,1)S(1)}, u32[]{:S(2)}, u32[]{:S(2)}) collective-permute-start(bf16[4,6,16,128]{3,2,1,0:T(8,128)(2,1)S(1)} %get-tuple-element.89), channel_id=1, source_target_pairs={{4,0},{8,4},{12,8},{16,12},{20,16},{24,20},{28,24},{5,1},{9,5},{13... | collective-permute-start | bytes 294920 | tf_op jit(solution)/shard_map/ppermute | solution.py:662
  37.8 6.7 %copy-start.3 = (f32[3,7,16,128]{3,2,1,0:T(8,128)S(1)}, f32[3,7,16,128]{3,2,1,0:T(8,128)}, u32[]{:S(2)}) copy-start(f32[3,7,16,128]{3,2,1,0:T(8,128)} %get-tuple-element.70.taps) | copy-start | bytes 516100
  40.7 6.8 %collective-permute-start.8 = (bf16[22,16,128]{2,1,0:T(8,128)(2,1)S(1)}, bf16[22,16,128]{2,1,0:T(8,128)(2,1)S(1)}, u32[]{:S(2)}, u32[]{:S(2)}) collective-permute-start(bf16[22,16,128]{2,1,0:T(8,128)(2,1)S(1)} %get-tuple-element.83), channel_id=1, source_target_pairs={{0,16},{4,20},{8,24},{12,28},{16,0},{20,4},{24,8},{28,12},{1,17},{... | collective-permute-start | bytes 270344 | tf_op jit(solution)/shard_map/ppermute | solution.py:666
  44.5 3.0 %copy-start.1 = (f32[2,128,16,128]{3,2,1,0:T(8,128)S(1)}, f32[2,128,16,128]{3,2,1,0:T(8,128)}, u32[]{:S(2)}) copy-start(f32[2,128,16,128]{3,2,1,0:T(8,128)} %get-tuple-element.59.pair) | copy-start | bytes 6291460
  44.5 3.0 %copy-start.2 = (f32[2,8,16,128]{3,2,1,0:T(8,128)S(1)}, f32[2,8,16,128]{3,2,1,0:T(8,128)}, u32[]{:S(2)}) copy-start(f32[2,8,16,128]{3,2,1,0:T(8,128)} %get-tuple-element.68.rows_far.first_rows) | copy-start | bytes 393220

commit v8 on v7

--- a/solution.py
+++ b/solution.py
@@ -770,7 +770,12 @@
         [kept(*row_shape), kept(2, rows)],
         ((rows * SUB, LANES), (rows * SUB, LANES)),
     )
-    sums = lax.psum(sums, "tp")
+    parts = lax.axis_size("tp")
+    if parts & (parts - 1):
+        sums = lax.psum(sums, "tp")
+    else:
+        for k in range(parts.bit_length() - 1):
+            sums = sums + lax.ppermute(sums, "tp", [(i, i ^ (1 << k)) for i in range(parts)])
     mixed, long_grad, back, message, inv, head = run(
         functools.partial(mixed_kernel, float(channels * lax.axis_size("tp"))),
         v(sums, table, query, long_conv, scaled) + far(rows_far),

time: 51.3 us -> 50.1 us (0.977)
  blocking collectives: 5.66 us -> 0 us
  waiting for transfers between devices: 3.17 us -> 5.99 us
  starting transfers between devices: 19.7 us -> 21.3 us
    psum x1 -> x0, blocking collectives: 5.66 us -> none  [on_device(): sums = lax.psum(sums, 'tp')]
    ppermute x0 -> x2, waiting for transfers between devices: none -> 3.17 us  [on_device(): lax.ppermute(sums, 'tp', [(i, i ^ 1 << k) for i in range(parts)])]
    ppermute x0 -> x2, starting transfers between devices: none -> 1.59 us  [on_device(): lax.ppermute(sums, 'tp', [(i, i ^ 1 << k) for i in range(parts)])]
  transfers between devices with their start and end apart: 10 -> 12, of which waited for: 5 -> 7; matrix products, arithmetic and copies ran while one was open for 0% -> 0% of each run, Pallas kernels for 25% -> 26%
where the time goes in v8:
time: 50.1 us; the launch traced here: 49.9 us
  Pallas kernels  21.8 us (44%)
  starting transfers between devices  21.3 us (43%)
  waiting for transfers between devices  5.99 us (12%)
  between operations  0.77 us (2%)
    pallas_call x12, Pallas kernels, run(): pl.pallas_call(kernel, out_shape=outs, in_specs=[pl.BlockSpec(memory_spac...  21.8 us
    ppermute x8, starting transfers between devices, swapped(): lax.ppermute(block, 'ctx', [(i, i ^ distance) for i in range(lax.axis_siz...  13.5 us
    ppermute x2, starting transfers between devices, shifted(): return lax.ppermute(block, 'ctx', route)  6.13 us
    ppermute x2, waiting for transfers between devices, on_device(): lax.ppermute(sums, 'tp', [(i, i ^ 1 << k) for i in range(parts)])  3.17 us
    ppermute x8, waiting for transfers between devices, swapped(): lax.ppermute(block, 'ctx', [(i, i ^ distance) for i in range(lax.axis_siz...  2.81 us
    ppermute x2, starting transfers between devices, on_device(): lax.ppermute(sums, 'tp', [(i, i ^ 1 << k) for i in range(parts)])  1.59 us
  transfers between devices with their start and end apart: 12, of which 7 were waited for; matrix products, arithmetic and copies ran while one was open for 0% of the time, Pallas kernels for 26%

profile of v8, /device:TPU:0, one launch (start us, length us, event | category | flops | bytes accessed | tf_op | source)
XLA Modules:
  0.0 49.9 jit_solution(13397392568426741680)
XLA Ops:
  0.6 0.9 %shard_map.78 = bf16[3,8,2048]{2,1,0:T(8,128)(2,1)S(1)} custom-call(bf16[3,128,2048]{2,1,0:T(8,128)(2,1)} %x_far.3), custom_call_target="tpu_custom_call" | custom-call | bytes 4194304 | tf_op jit(solution)/shard_map/pallas_call | solution.py:647
  1.6 4.8 %collective-permute-start = (bf16[3,8,2048]{2,1,0:T(8,128)(2,1)S(1)}, bf16[3,8,2048]{2,1,0:T(8,128)(2,1)S(1)}, u32[]{:S(2)}, u32[]{:S(2)}) collective-permute-start(bf16[3,8,2048]{2,1,0:T(8,128)(2,1)S(1)} %shard_map.78), channel_id=1, source_target_pairs={{0,4},{4,8},{8,12},{12,16},{16,20},{20,24},{24,28},{1,5},{5,9},{9,... | collective-permute-start | bytes 294920 | tf_op jit(solution)/shard_map/ppermute | solution.py:662
  6.4 0.0 copy-start.3
  6.5 3.8 %shard_map.77 = (f32[2,128,16,128]{3,2,1,0:T(8,128)}, f32[3,7,16,128]{3,2,1,0:T(8,128)}, f32[2,8,16,128]{3,2,1,0:T(8,128)S(1)}, f32[3,16,16,128]{3,2,1,0:T(8,128...) custom-call(bf16[3,128,2048]{2,1,0:T(8,128)(2,1)} %x_far.3, bf16[3,7,128]{2,1,0:T(8,128)(2,1)} %bitcast.5, ...), custom_call_target="tpu_custom_call" | custom-call | flops 1000000000 | bytes 4194304 | tf_op jit(solution)/shard_map/pallas_call | solution.py:647
  10.3 0.3 shard_map.79
  10.6 2.6 %collective-permute-start.3 = (bf16[16,16,128]{2,1,0:T(8,128)(2,1)S(1)}, bf16[16,16,128]{2,1,0:T(8,128)(2,1)S(1)}, u32[]{:S(2)}, u32[]{:S(2)}) collective-permute-start(bf16[16,16,128]{2,1,0:T(8,128)(2,1)S(1)} %get-tuple-element.51), channel_id=1, source_target_pairs={{0,12},{4,8},{8,4},{12,0},{16,28},{20,24},{24,20},{28,16},{1,13},{... | collective-permute-start | bytes 196616 | tf_op jit(solution)/shard_map/ppermute | solution.py:666
  13.2 0.4 collective-permute-start.2
  13.7 0.5 collective-permute-start.1
  14.2 2.1 %shard_map.80 = (f32[128,16,128]{2,1,0:T(8,128)S(1)}, f32[128,16,128]{2,1,0:T(8,128)S(1)}) custom-call(bf16[3,128,2048]{2,1,0:T(8,128)(2,1)} %x_far.3, bf16[3,8,2048]{2,1,0:T(8,128)(2,1)S(1)} %collective-permute-done.halo, f32[3,7,16,128]{3,2,1,0:T(8,128)S(1)} %get-tuple-element.48.taps, f32[16,128]{1,0:T(8,128)S(1)} %bitcast.3, bf16[128,2048]{1,0:T(8,128)(2,1)} %grad_far.1), custom_call_target="tpu_custom_call" | custom-call | flops 2000000000 | bytes 4194304 | tf_op jit(solution)/shard_map/pallas_call | solution.py:647
  16.3 0.3 collective-permute-done.3.third
  16.5 1.0 %collective-permute-done.2.second = bf16[16,16,128]{2,1,0:T(8,128)(2,1)S(1)} collective-permute-done((bf16[16,16,128]{2,1,0:T(8,128)(2,1)S(1)}, bf16[16,16,128]{2,1,0:T(8,128)(2,1)S(1)}, u32[]{:S(2)}, u32[]{:S(2)}) %collective-permute-start.2) | collective-permute-done | bytes 65568 | tf_op jit(solution)/shard_map/ppermute | solution.py:666
  17.5 0.4 collective-permute-done.1.first
  18.0 0.4 shard_map.81
  18.4 2.7 %collective-permute-start.4 = (bf16[16,16,128]{2,1,0:T(8,128)(2,1)S(1)}, bf16[16,16,128]{2,1,0:T(8,128)(2,1)S(1)}, u32[]{:S(2)}, u32[]{:S(2)}) collective-permute-start(bf16[16,16,128]{2,1,0:T(8,128)(2,1)S(1)} %get-tuple-element.58), channel_id=1, source_target_pairs={{0,16},{4,20},{8,24},{12,28},{16,0},{20,4},{24,8},{28,12},{1,17},{... | collective-permute-start | bytes 196616 | tf_op jit(solution)/shard_map/ppermute | solution.py:666
  21.0 2.4 %shard_map.82 = (f32[128,16,128]{2,1,0:T(8,128)S(1)}, f32[2,8,16,128]{3,2,1,0:T(8,128)}) custom-call(f32[2,128,16,128]{3,2,1,0:T(8,128)S(1)} %copy-done, f32[2,8,16,128]{3,2,1,0:T(8,128)S(1)} %get-tuple-element.60.first_rows, f32[3,16,16,128]{3,2,1,0:T(8,128)S(1)} %get-tuple-element.46.table), custom_call_target="tpu_custom_call" | custom-call | flops 2000000000 | bytes 4194304 | tf_op jit(solution)/shard_map/pallas_call | solution.py:647
  23.4 0.1 collective-permute-done.4.got
  23.6 1.6 %shard_map.83 = (f32[128,16,128]{2,1,0:T(8,128)S(1)}, f32[2,128]{1,0:T(2,128)S(1)}) custom-call(s32[1]{0:T(128)} %bitcast.place, f32[16,16,128]{2,1,0:T(8,128)S(1)} %get-tuple-element.57.entering, bf16[16,16,128]{2,1,0:T(8,128)(2,1)S(1)} %collective-permute-done.4.got, f32[3,16,16,128]{3,2,1,0:T(8,128)S(1)} %get-tuple-element.46.table, ...), custom_call_target="tpu_custom_call" | custom-call | bytes 4194304 | tf_op jit(solution)/shard_map/pallas_call | solution.py:647
  25.2 0.1 collective-permute-start.5
  25.3 1.1 %collective-permute-done.5 = f32[2,128]{1,0:T(2,128)S(1)} collective-permute-done((f32[2,128]{1,0:T(2,128)S(1)}, f32[2,128]{1,0:T(2,128)S(1)}, u32[]{:S(2)}, u32[]{:S(2)}) %collective-permute-start.5) | collective-permute-done | bytes 1056 | tf_op jit(solution)/shard_map/ppermute | solution.py:778
  26.4 1.5 %collective-permute-start.6 = (f32[2,128]{1,0:T(2,128)S(1)}, f32[2,128]{1,0:T(2,128)S(1)}, u32[]{:S(2)}, u32[]{:S(2)}) collective-permute-start(f32[2,128]{1,0:T(2,128)S(1)} %add.6), channel_id=1, source_target_pairs={{0,2},{1,3},{2,0},{3,1},{4,6},{5,7},{6,4},{7,5},{8,10},{9,11},{10,... | collective-permute-start | bytes 3080 | tf_op jit(solution)/shard_map/ppermute | solution.py:778
  27.9 2.0 %collective-permute-done.6 = f32[2,128]{1,0:T(2,128)S(1)} collective-permute-done((f32[2,128]{1,0:T(2,128)S(1)}, f32[2,128]{1,0:T(2,128)S(1)}, u32[]{:S(2)}, u32[]{:S(2)}) %collective-permute-start.6) | collective-permute-done | bytes 1056 | tf_op jit(solution)/shard_map/ppermute | solution.py:778
  30.0 2.1 %shard_map.84 = (f32[128,16,128]{2,1,0:T(8,128)S(1)}, f32[128,16,128]{2,1,0:T(8,128)S(1)}, f32[16,16,128]{2,1,0:T(8,128)S(1)}, bf16[16,16,128]{2,1,0:T(8,128)(2,...) custom-call(f32[2,128]{1,0:T(2,128)S(1)} %add.7.sums, ...), custom_call_target="tpu_custom_call" | custom-call | bytes 4194304 | tf_op jit(solution)/shard_map/pallas_call | solution.py:647
  32.1 1.7 %collective-permute-start.9 = (bf16[16,16,128]{2,1,0:T(8,128)(2,1)S(1)}, bf16[16,16,128]{2,1,0:T(8,128)(2,1)S(1)}, u32[]{:S(2)}, u32[]{:S(2)}) collective-permute-start(bf16[16,16,128]{2,1,0:T(8,128)(2,1)S(1)} %get-tuple-element.71), channel_id=1, source_target_pairs={{0,12},{4,8},{8,4},{12,0},{16,28},{20,24},{24,20},{28,16},{1,13},{... | collective-permute-start | bytes 196616 | tf_op jit(solution)/shard_map/ppermute | solution.py:666
  33.8 0.5 collective-permute-start.8
  34.3 1.4 %collective-permute-start.7 = (bf16[16,16,128]{2,1,0:T(8,128)(2,1)S(1)}, bf16[16,16,128]{2,1,0:T(8,128)(2,1)S(1)}, u32[]{:S(2)}, u32[]{:S(2)}) collective-permute-start(bf16[16,16,128]{2,1,0:T(8,128)(2,1)S(1)} %get-tuple-element.71), channel_id=1, source_target_pairs={{0,4},{4,0},{8,12},{12,8},{16,20},{20,16},{24,28},{28,24},{1,5},{5... | collective-permute-start | bytes 196616 | tf_op jit(solution)/shard_map/ppermute | solution.py:666
  35.6 1.3 %collective-permute-start.11 = (bf16[4,6,16,128]{3,2,1,0:T(8,128)(2,1)S(1)}, bf16[4,6,16,128]{3,2,1,0:T(8,128)(2,1)S(1)}, u32[]{:S(2)}, u32[]{:S(2)}) collective-permute-start(bf16[4,6,16,128]{3,2,1,0:T(8,128)(2,1)S(1)} %get-tuple-element.89), channel_id=1, source_target_pairs={{4,0},{8,4},{12,8},{16,12},{20,16},{24,20},{28,24},{5,1},{9,5},{13... | collective-permute-start | bytes 294920 | tf_op jit(solution)/shard_map/ppermute | solution.py:662
  36.9 2.3 %shard_map.85.local = f32[128,16,128]{2,1,0:T(8,128)S(1)} custom-call(f32[3,16,16,128]{3,2,1,0:T(8,128)S(1)} %get-tuple-element.46.table, f32[128,16,128]{2,1,0:T(8,128)S(1)} %get-tuple-element.72.long_grad), custom_call_target="tpu_custom_call" | custom-call | flops 2000000000 | bytes 4194304 | tf_op jit(solution)/shard_map/pallas_call | solution.py:647
  39.2 0.6 %shard_map.87 = (f32[16,16,128]{2,1,0:T(8,128)S(1)}, f32[16,16,128]{2,1,0:T(8,128)S(1)}, f32[6,16,128]{2,1,0:T(8,128)S(1)}, bf16[22,16,128]{2,1,0:T(8,128)(2,1)S(1)}) custom-call(s32[1]{0:T(128)} %bitcast.place, f32[3,16,16,128]{3,2,1,0:T(8,128)S(1)} %get-tuple-element.46.table, f32[16,16,128]{2,1,0:T(8,128)S(1)} %get-tuple-element.76.state, ...), custom_call_target="tpu_custom_call" | custom-call | bytes 4194304 | tf_op jit(solution)/shard_map/pallas_call | solution.py:647
  39.8 3.8 %collective-permute-start.10 = (bf16[22,16,128]{2,1,0:T(8,128)(2,1)S(1)}, bf16[22,16,128]{2,1,0:T(8,128)(2,1)S(1)}, u32[]{:S(2)}, u32[]{:S(2)}) collective-permute-start(bf16[22,16,128]{2,1,0:T(8,128)(2,1)S(1)} %get-tuple-element.83), channel_id=1, source_target_pairs={{0,16},{4,20},{8,24},{12,28},{16,0},{20,4},{24,8},{28,12},{1,17},{... | collective-permute-start | bytes 270344 | tf_op jit(solution)/shard_map/ppermute | solution.py:666
  43.6 1.7 %shard_map.86 = (bf16[128,2048]{1,0:T(8,128)(2,1)}, bf16[128,2048]{1,0:T(8,128)(2,1)S(1)}, f32[128,128]{1,0:T(8,128)S(1)}) custom-call(f32[128,128]{1,0:T(8,128)S(1)} %get-tuple-element.69.inv, f32[3,7,16,128]{3,2,1,0:T(8,128)S(1)} %copy-done.2, f32[16,128]{1,0:T(8,128)S(1)} %bitcast.4, f32[128,16,128]{2,1,0:T(8,128)S(1)} %get-tuple-element.63.query, ...), custom_call_target="tpu_custom_call" | custom-call | flops 2000000000 | bytes 4194304 | tf_op jit(solution)/shard_map/pallas_call | solution.py:647
  45.3 1.0 %collective-permute-done.10.got = bf16[22,16,128]{2,1,0:T(8,128)(2,1)S(1)} collective-permute-done((bf16[22,16,128]{2,1,0:T(8,128)(2,1)S(1)}, bf16[22,16,128]{2,1,0:T(8,128)(2,1)S(1)}, u32[]{:S(2)}, u32[]{:S(2)}) %collective-permute-start.10) | collective-permute-done | bytes 90144 | tf_op jit(solution)/shard_map/ppermute | solution.py:666
  46.3 3.6 %shard_map.88 = bf16[3,128,2048]{2,1,0:T(8,128)(2,1)} custom-call(s32[1]{0:T(128)} %bitcast.place, f32[16,16,128]{2,1,0:T(8,128)S(1)} %get-tuple-element.80.entering, f32[16,16,128]{2,1,0:T(8,128)S(1)} %get-tuple-element.81.beyond_in, f32[6,16,128]{2,1,0:T(8,128)S(1)} %get-tuple-element.82.added, bf16[22,16,128]{2,1,0:T(8,128)(2,1)S(1)} %collective-permute-done.10.got, ...), custom_call_target="tpu_custom_call" | custom-call | bytes 4194304 | tf_op jit(solution)/shard_map/pallas_call | solution.py:647
  (14 shorter events, 0.0 us)
Async XLA Ops:
  1.6 8.7 %collective-permute-start = (bf16[3,8,2048]{2,1,0:T(8,128)(2,1)S(1)}, bf16[3,8,2048]{2,1,0:T(8,128)(2,1)S(1)}, u32[]{:S(2)}, u32[]{:S(2)}) collective-permute-start(bf16[3,8,2048]{2,1,0:T(8,128)(2,1)S(1)} %shard_map.78), channel_id=1, source_target_pairs={{0,4},{4,8},{8,12},{12,16},{16,20},{20,24},{24,28},{1,5},{5,9},{9,... | collective-permute-start | bytes 294920 | tf_op jit(solution)/shard_map/ppermute | solution.py:662
  6.4 7.7 %copy-start.3 = (f32[2048]{0:T(1024)S(1)}, f32[2048]{0:T(1024)}, u32[]{:S(2)}) copy-start(f32[2048]{0:T(1024)} %param.10) | copy-start | bytes 24580
  10.6 5.9 %collective-permute-start.3 = (bf16[16,16,128]{2,1,0:T(8,128)(2,1)S(1)}, bf16[16,16,128]{2,1,0:T(8,128)(2,1)S(1)}, u32[]{:S(2)}, u32[]{:S(2)}) collective-permute-start(bf16[16,16,128]{2,1,0:T(8,128)(2,1)S(1)} %get-tuple-element.51), channel_id=1, source_target_pairs={{0,12},{4,8},{8,4},{12,0},{16,28},{20,24},{24,20},{28,16},{1,13},{... | collective-permute-start | bytes 196616 | tf_op jit(solution)/shard_map/ppermute | solution.py:666
  13.2 4.3 %collective-permute-start.2 = (bf16[16,16,128]{2,1,0:T(8,128)(2,1)S(1)}, bf16[16,16,128]{2,1,0:T(8,128)(2,1)S(1)}, u32[]{:S(2)}, u32[]{:S(2)}) collective-permute-start(bf16[16,16,128]{2,1,0:T(8,128)(2,1)S(1)} %get-tuple-element.51), channel_id=1, source_target_pairs={{0,8},{4,12},{8,0},{12,4},{16,24},{20,28},{24,16},{28,20},{1,9},{5... | collective-permute-start | bytes 196616 | tf_op jit(solution)/shard_map/ppermute | solution.py:666
  13.7 4.3 %collective-permute-start.1 = (bf16[16,16,128]{2,1,0:T(8,128)(2,1)S(1)}, bf16[16,16,128]{2,1,0:T(8,128)(2,1)S(1)}, u32[]{:S(2)}, u32[]{:S(2)}) collective-permute-start(bf16[16,16,128]{2,1,0:T(8,128)(2,1)S(1)} %get-tuple-element.51), channel_id=1, source_target_pairs={{0,4},{4,0},{8,12},{12,8},{16,20},{20,16},{24,28},{28,24},{1,5},{5... | collective-permute-start | bytes 196616 | tf_op jit(solution)/shard_map/ppermute | solution.py:666
  14.2 6.8 %copy-start = (f32[2,128,16,128]{3,2,1,0:T(8,128)S(1)}, f32[2,128,16,128]{3,2,1,0:T(8,128)}, u32[]{:S(2)}) copy-start(f32[2,128,16,128]{3,2,1,0:T(8,128)} %get-tuple-element.59.pair) | copy-start | bytes 6291460
  18.4 5.2 %collective-permute-start.4 = (bf16[16,16,128]{2,1,0:T(8,128)(2,1)S(1)}, bf16[16,16,128]{2,1,0:T(8,128)(2,1)S(1)}, u32[]{:S(2)}, u32[]{:S(2)}) collective-permute-start(bf16[16,16,128]{2,1,0:T(8,128)(2,1)S(1)} %get-tuple-element.58), channel_id=1, source_target_pairs={{0,16},{4,20},{8,24},{12,28},{16,0},{20,4},{24,8},{28,12},{1,17},{... | collective-permute-start | bytes 196616 | tf_op jit(solution)/shard_map/ppermute | solution.py:666
  25.2 1.2 %collective-permute-start.5 = (f32[2,128]{1,0:T(2,128)S(1)}, f32[2,128]{1,0:T(2,128)S(1)}, u32[]{:S(2)}, u32[]{:S(2)}) collective-permute-start(f32[2,128]{1,0:T(2,128)S(1)} %get-tuple-element.66), channel_id=1, source_target_pairs={{0,1},{1,0},{2,3},{3,2},{4,5},{5,4},{6,7},{7,6},{8,9},{9,8},{10,11... | collective-permute-start | bytes 3080 | tf_op jit(solution)/shard_map/ppermute | solution.py:778
  26.4 3.6 %collective-permute-start.6 = (f32[2,128]{1,0:T(2,128)S(1)}, f32[2,128]{1,0:T(2,128)S(1)}, u32[]{:S(2)}, u32[]{:S(2)}) collective-permute-start(f32[2,128]{1,0:T(2,128)S(1)} %add.6), channel_id=1, source_target_pairs={{0,2},{1,3},{2,0},{3,1},{4,6},{5,7},{6,4},{7,5},{8,10},{9,11},{10,... | collective-permute-start | bytes 3080 | tf_op jit(solution)/shard_map/ppermute | solution.py:778
  32.1 7.1 %collective-permute-start.9 = (bf16[16,16,128]{2,1,0:T(8,128)(2,1)S(1)}, bf16[16,16,128]{2,1,0:T(8,128)(2,1)S(1)}, u32[]{:S(2)}, u32[]{:S(2)}) collective-permute-start(bf16[16,16,128]{2,1,0:T(8,128)(2,1)S(1)} %get-tuple-element.71), channel_id=1, source_target_pairs={{0,12},{4,8},{8,4},{12,0},{16,28},{20,24},{24,20},{28,16},{1,13},{... | collective-permute-start | bytes 196616 | tf_op jit(solution)/shard_map/ppermute | solution.py:666
  33.8 5.4 %collective-permute-start.8 = (bf16[16,16,128]{2,1,0:T(8,128)(2,1)S(1)}, bf16[16,16,128]{2,1,0:T(8,128)(2,1)S(1)}, u32[]{:S(2)}, u32[]{:S(2)}) collective-permute-start(bf16[16,16,128]{2,1,0:T(8,128)(2,1)S(1)} %get-tuple-element.71), channel_id=1, source_target_pairs={{0,8},{4,12},{8,0},{12,4},{16,24},{20,28},{24,16},{28,20},{1,9},{5... | collective-permute-start | bytes 196616 | tf_op jit(solution)/shard_map/ppermute | solution.py:666
  34.3 5.0 %collective-permute-start.7 = (bf16[16,16,128]{2,1,0:T(8,128)(2,1)S(1)}, bf16[16,16,128]{2,1,0:T(8,128)(2,1)S(1)}, u32[]{:S(2)}, u32[]{:S(2)}) collective-permute-start(bf16[16,16,128]{2,1,0:T(8,128)(2,1)S(1)} %get-tuple-element.71), channel_id=1, source_target_pairs={{0,4},{4,0},{8,12},{12,8},{16,20},{20,16},{24,28},{28,24},{1,5},{5... | collective-permute-start | bytes 196616 | tf_op jit(solution)/shard_map/ppermute | solution.py:666
  35.6 10.7 %collective-permute-start.11 = (bf16[4,6,16,128]{3,2,1,0:T(8,128)(2,1)S(1)}, bf16[4,6,16,128]{3,2,1,0:T(8,128)(2,1)S(1)}, u32[]{:S(2)}, u32[]{:S(2)}) collective-permute-start(bf16[4,6,16,128]{3,2,1,0:T(8,128)(2,1)S(1)} %get-tuple-element.89), channel_id=1, source_target_pairs={{4,0},{8,4},{12,8},{16,12},{20,16},{24,20},{28,24},{5,1},{9,5},{13... | collective-permute-start | bytes 294920 | tf_op jit(solution)/shard_map/ppermute | solution.py:662
  36.9 6.7 %copy-start.2 = (f32[3,7,16,128]{3,2,1,0:T(8,128)S(1)}, f32[3,7,16,128]{3,2,1,0:T(8,128)}, u32[]{:S(2)}) copy-start(f32[3,7,16,128]{3,2,1,0:T(8,128)} %get-tuple-element.70.taps) | copy-start | bytes 516100
  39.8 6.4 %collective-permute-start.10 = (bf16[22,16,128]{2,1,0:T(8,128)(2,1)S(1)}, bf16[22,16,128]{2,1,0:T(8,128)(2,1)S(1)}, u32[]{:S(2)}, u32[]{:S(2)}) collective-permute-start(bf16[22,16,128]{2,1,0:T(8,128)(2,1)S(1)} %get-tuple-element.83), channel_id=1, source_target_pairs={{0,16},{4,20},{8,24},{12,28},{16,0},{20,4},{24,8},{28,12},{1,17},{... | collective-permute-start | bytes 270344 | tf_op jit(solution)/shard_map/ppermute | solution.py:666
  43.6 2.7 %copy-start.1 = (f32[2,8,16,128]{3,2,1,0:T(8,128)S(1)}, f32[2,8,16,128]{3,2,1,0:T(8,128)}, u32[]{:S(2)}) copy-start(f32[2,8,16,128]{3,2,1,0:T(8,128)} %get-tuple-element.68.rows_far.first_rows) | copy-start | bytes 393220
